TPU v7x, 128 devices: a whole 4x4x4 slice. The times are simulated.
128 devices in a mesh: tile: 32 (over y, x, core), band: 4 (over z).
Axes of the slice: x: 4, y: 4, z: 4, core: 2. Of those that a mesh axis runs over, the one named last changes fastest.
Arguments:
- noisy: bfloat16 [12, 1024, 512], P(None, 'tile', 'band'), may hold values from -6 to 6
- grad_pred: bfloat16 [12, 1024, 512], P(None, 'tile', 'band'), may hold values from -6 to 6
- coarse: bfloat16 [4, 64, 38, 128], P('band'), may hold values from -6 to 6
- margin_band: int32 [1024, 1], P(('tile', 'band')), may hold values from 0 to 3; in each aligned block of 8 rows (0 to 7, 8 to 15, ...) at most 4 rows name the same one
- margin_slot: int32 [1024], P(('tile', 'band')), may hold values from 0 to 63
- interp: bfloat16 [32, 4, 8, 128, 4096], P('tile', 'band'), may hold values from -0.1875 to 0.1875
- w_in: bfloat16 [128, 50], replicated, may hold values from -0.875 to 0.875
- w_conv1: bfloat16 [3, 3, 128, 128], replicated, may hold values from -0.1875 to 0.1875
- w_conv2: bfloat16 [3, 3, 128, 128], replicated, may hold values from -0.1875 to 0.1875
- w_out: bfloat16 [12, 128], replicated, may hold values from -0.5 to 0.5
Outputs:
- pred: float32 [12, 1024, 512], P(None, 'tile', 'band')
- coarse_grad: float32 [4, 64, 38, 128], P('band', 'tile')
- grad_in: float32 [128, 50], replicated
- grad_conv1: float32 [3, 3, 128, 128], replicated
- grad_conv2: float32 [3, 3, 128, 128], replicated
- grad_out: float32 [12, 128], replicated
Inputs may be any that keep to these rules, and one draw needn't show every extreme that they name: `margin_band`: of the 8 entries of one device, at most 4 name the same band, and every draw has devices where one band is named exactly 4 times.
All inputs are finite; a program needn't handle non-finite values.
Results may differ from a plain program's by a relative error of at most 0.015.
Values may be sent and summed in bfloat16 or wider, within the bound.
No kernel may reach another device: no remote copies, remote signals or barrier semaphores. Data moves between devices by JAX's collectives and lax.ppermute only.
A program may use at most 128 MiB of HBM per device.

v0:
```python
import math

import jax
import jax.numpy as jnp
from jax import lax
from jax.sharding import PartitionSpec as P

MOST = 4


def padded_2(cells, sides, width):
    for axis, dim in sides:
        count = lax.axis_size(axis)
        ends = count - 1
        head = lax.slice_in_dim(cells, 0, width, axis=dim)
        tail = lax.slice_in_dim(cells, cells.shape[dim] - width, cells.shape[dim], axis=dim)
        cells = jnp.concatenate(
            [
                lax.ppermute(tail, axis, [(i, (i + 1) % count) for i in range(ends)]),
                cells,
                lax.ppermute(head, axis, [((i + 1) % count, i) for i in range(ends)]),
            ],
            axis=dim,
        )
    return cells


def shifted_stack(padded, rows, cols, flip):
    pieces = []
    for p_tap in range(3):
        for q_tap in range(3):
            r_start = 2 - p_tap if flip else p_tap
            c_start = 2 - q_tap if flip else q_tap
            pieces.append(padded[:, r_start : r_start + rows, c_start : c_start + cols])
    stacked = jnp.stack(pieces, 0)
    return stacked.reshape(9 * padded.shape[0], rows * cols)


def rims_forward(field):
    return padded_2(field, (("tile", 1), ("band", 2)), 1)


def rims_backward(field):
    return padded_2(field, (("tile", 1), ("band", 2)), 1)


def forward_matrix(weight):
    return weight.transpose(2, 0, 1, 3).reshape(weight.shape[2], 9 * weight.shape[3])


def backward_matrix(weight):
    return weight.transpose(3, 0, 1, 2).reshape(weight.shape[3], 9 * weight.shape[2])


def silu_slope(value):
    sig = jax.nn.sigmoid(value)
    return sig * (1.0 + value * (1.0 - sig))


def outer_sum(left, right):
    return lax.dot_general(
        left, right, (((1,), (1,)), ((), ())), preferred_element_type=jnp.float32
    )


def per_device(
    noisy, grad_pred, coarse, margin_band, margin_slot, interp, w_in, w_conv1, w_conv2, w_out
):
    width = w_in.shape[0]
    chans = noisy.shape[0]
    rows = noisy.shape[1]
    cols = noisy.shape[2]
    cells = rows * cols
    coarse_ch = coarse.shape[2]
    block_cells = coarse.shape[3]
    per_band = coarse.shape[1]
    n_band = lax.axis_size("band")
    n_tile = lax.axis_size("tile")
    band_ids = margin_band[:, 0]
    count = band_ids.shape[0]
    local_interp = interp[0, 0]
    order = jnp.arange(count, dtype=jnp.int32)
    same = band_ids[:, None] == band_ids[None, :]
    before = order[None, :] < order[:, None]
    rank = jnp.sum(jnp.logical_and(same, before).astype(jnp.int32), axis=1)
    place = band_ids * MOST + rank
    select = place[:, None] == jnp.arange(n_band * MOST, dtype=jnp.int32)[None, :]
    wanted = jnp.sum(jnp.where(select, margin_slot[:, None] + 1, 0), axis=0) - 1
    asked = lax.all_to_all(
        wanted.reshape(n_band, MOST), "band", split_axis=0, concat_axis=0, tiled=True
    )
    owned = asked.reshape(n_band * MOST)[:, None] == jnp.arange(per_band, dtype=jnp.int32)[None, :]
    served = jnp.einsum(
        "sj,jcm->scm", owned.astype(jnp.bfloat16), coarse[0], preferred_element_type=jnp.float32
    ).astype(jnp.bfloat16)
    arrived = lax.all_to_all(
        served.reshape(n_band, MOST, coarse_ch, block_cells),
        "band",
        split_axis=0,
        concat_axis=0,
        tiled=True,
    )
    picked = jnp.einsum(
        "ks,scm->kcm",
        select.astype(jnp.bfloat16),
        arrived.reshape(n_band * MOST, coarse_ch, block_cells),
        preferred_element_type=jnp.float32,
    ).astype(jnp.bfloat16)
    cond = jnp.einsum(
        "kcm,kmn->cn", picked, local_interp, preferred_element_type=jnp.float32
    ).astype(jnp.bfloat16)
    inputs = jnp.concatenate([cond, noisy.reshape(chans, cells)], 0)
    h_zero = jnp.dot(w_in, inputs, preferred_element_type=jnp.float32)
    a_zero = jax.nn.silu(h_zero).astype(jnp.bfloat16)
    cols_zero = shifted_stack(rims_forward(a_zero.reshape(width, rows, cols)), rows, cols, False)
    z_one = jnp.dot(forward_matrix(w_conv1), cols_zero, preferred_element_type=jnp.float32)
    a_one = jax.nn.silu(z_one).astype(jnp.bfloat16)
    cols_one = shifted_stack(rims_forward(a_one.reshape(width, rows, cols)), rows, cols, False)
    z_two = jnp.dot(forward_matrix(w_conv2), cols_one, preferred_element_type=jnp.float32)
    a_two = (a_zero.astype(jnp.float32) + z_two).astype(jnp.bfloat16)
    pred = jnp.dot(w_out, a_two, preferred_element_type=jnp.float32)
    cotangent = grad_pred.reshape(chans, cells)
    grad_out_part = outer_sum(cotangent, a_two)
    d_two = jnp.dot(w_out.T, cotangent, preferred_element_type=jnp.float32).astype(jnp.bfloat16)
    grad_two_part = outer_sum(d_two, cols_one)
    back_two = shifted_stack(rims_backward(d_two.reshape(width, rows, cols)), rows, cols, True)
    d_one = (
        jnp.dot(backward_matrix(w_conv2), back_two, preferred_element_type=jnp.float32)
        * silu_slope(z_one)
    ).astype(jnp.bfloat16)
    grad_one_part = outer_sum(d_one, cols_zero)
    back_one = shifted_stack(rims_backward(d_one.reshape(width, rows, cols)), rows, cols, True)
    d_zero = (
        (
            jnp.dot(backward_matrix(w_conv1), back_one, preferred_element_type=jnp.float32)
            + d_two.astype(jnp.float32)
        )
        * silu_slope(h_zero)
    ).astype(jnp.bfloat16)
    grad_in_part = outer_sum(d_zero, inputs)
    d_cond = jnp.dot(w_in[:, :coarse_ch].T, d_zero, preferred_element_type=jnp.float32).astype(
        jnp.bfloat16
    )
    d_blocks = jnp.einsum("cn,kmn->kcm", d_cond, local_interp, preferred_element_type=jnp.float32)
    outgoing = jnp.einsum(
        "ks,kcm->scm", select.astype(jnp.float32), d_blocks, precision=lax.Precision.HIGHEST
    )
    returned = lax.all_to_all(
        outgoing.reshape(n_band, MOST, coarse_ch, block_cells).astype(jnp.bfloat16),
        "band",
        split_axis=0,
        concat_axis=0,
        tiled=True,
    ).astype(jnp.float32)
    band_total = jnp.einsum(
        "sj,scm->jcm",
        owned.astype(jnp.float32),
        returned.reshape(n_band * MOST, coarse_ch, block_cells),
        precision=lax.Precision.HIGHEST,
    )
    mine = lax.psum_scatter(
        band_total.astype(jnp.bfloat16), "tile", scatter_dimension=0, tiled=True
    ).astype(jnp.float32)
    coarse_grad = mine[None]
    sums = lax.psum((grad_in_part, grad_one_part, grad_two_part, grad_out_part), ("tile", "band"))
    factor = 1.0 / math.sqrt(cells * n_tile * n_band)
    grad_in = sums[0] * factor
    grad_conv1 = (sums[1] * factor).reshape(width, 3, 3, width).transpose(1, 2, 0, 3)
    grad_conv2 = (sums[2] * factor).reshape(width, 3, 3, width).transpose(1, 2, 0, 3)
    grad_out = sums[3] * factor
    return (pred.reshape(chans, rows, cols), coarse_grad, grad_in, grad_conv1, grad_conv2, grad_out)


def solution(mesh):
    placed = (
        P(None, "tile", "band"),
        P(None, "tile", "band"),
        P("band", None, None, None),
        P(("tile", "band"), None),
        P(("tile", "band")),
        P("tile", "band", None, None, None),
        P(),
        P(),
        P(),
        P(),
    )
    return jax.shard_map(
        per_device,
        mesh=mesh,
        in_specs=placed,
        out_specs=(P(None, "tile", "band"), P("band", "tile", None, None), P(), P(), P(), P()),
        check_vma=False,
    )
```

profile of v0, /device:TPU:1, one launch (start us, length us, event | category | flops | bytes accessed | tf_op | source)
XLA Modules:
  0.0 531.0 jit_solution(1252101570893281771)
XLA Ops:
  11.0 4.5 collective-permute-start.8
  15.5 1.9 collective-permute-start.9
  18.4 5.0 all-to-all-start
  30.4 4.2 all-to-all-start.1
  34.6 1.6 pad_maximum_fusion.2
  37.9 4.0 collective-permute-start.11
  45.2 1.4 fusion.76
  46.6 1.3 fusion.103
  49.0 1.3 fusion.73
  50.3 1.3 fusion.102
  53.1 5.0 fusion.58
  58.1 2.1 multiply_convert_fusion.1
  62.9 5.0 collective-permute-start
  67.9 1.9 collective-permute-start.1
  69.9 1.4 fusion.99
  71.2 12.9 %copy.140 = bf16[9,128,32,128]{3,2,1,0:T(8,128)(2,1)} copy(bf16[9,128,32,128]{1,3,2,0:T(8,128)(2,1)} %fusion.99) | data formatting | bytes 18874368 | tf_op jit(solution)/shard_map/stack | solution.py:35
  85.0 3.8 collective-permute-start.2
  89.1 1.6 collective-permute-start.3
  93.6 1.4 fusion.122
  94.9 1.4 fusion.85
  97.3 1.4 fusion.121
  101.1 1.3 fusion.116
  102.5 12.8 %copy.117 = bf16[9,128,32,128]{3,2,1,0:T(8,128)(2,1)} copy(bf16[9,128,32,128]{1,3,2,0:T(8,128)(2,1)} %fusion.116) | data formatting | bytes 18874368 | tf_op jit(solution)/shard_map/stack | solution.py:35
  115.2 8.0 %multiply_convert_fusion = (bf16[128,4096]{0,1:T(8,128)(2,1)S(1)}, f32[128,4096]{0,1:T(8,128)S(1)}) fusion(bf16[128,1152]{0,1:T(8,128)(2,1)S(1)} %bitcast.342, bf16[144,8,32,128]{3,2,1,0:T(8,128)(2,1)} %bitcast.322), kind=kOutput, calls=%fused_computation.39 | convolution fusion | flops 1210580992 | bytes 12877824 | tf_op jit(solution)/shard_map/dot_general | solution.py:116
  123.2 11.1 %fusion.49 = bf16[128,4096]{0,1:T(8,128)(2,1)S(1)} fusion(bf16[128,1152]{0,1:T(8,128)(2,1)S(1)} %bitcast.339, bf16[144,8,32,128]{3,2,1,0:T(8,128)(2,1)} %bitcast.319, f32[128,4096]{0,1:T(8,128)S(1)} %get-tuple-element.55), kind=kOutput, calls=%fused_computation.32 | convolution fusion | flops 1212678144 | bytes 12877824 | tf_op jit(solution)/shard_map/dot_general | solution.py:128
  134.3 4.4 fusion.10
  139.5 5.1 collective-permute-start.4
  144.6 2.1 collective-permute-start.5
  147.5 3.6 collective-permute-start.12
  151.1 1.9 collective-permute-start.13
  154.2 3.1 collective-permute-start.6
  161.0 4.6 collective-permute-start.15
  169.8 1.8 fusion.97
  173.9 12.9 %copy.128 = bf16[9,128,32,128]{3,2,1,0:T(8,128)(2,1)} copy(bf16[9,128,32,128]{1,3,2,0:T(8,128)(2,1)} %copy-done.9) | data formatting | bytes 18874368 | tf_op jit(solution)/shard_map/stack | solution.py:35
  186.8 1.4 fusion.70
  188.2 1.4 fusion.94
  190.7 1.4 fusion.67
  195.8 13.0 %copy.150 = bf16[9,128,32,128]{3,2,1,0:T(8,128)(2,1)} copy(bf16[9,128,32,128]{1,3,2,0:T(8,128)(2,1)} %fusion.90) | data formatting | bytes 18874368 | tf_op jit(solution)/shard_map/stack | solution.py:35
  208.8 12.6 %fusion.52 = bf16[128,4096]{0,1:T(8,128)(2,1)} fusion(bf16[128,1152]{0,1:T(8,128)(2,1)S(1)} %bitcast.340, bf16[144,8,32,128]{3,2,1,0:T(8,128)(2,1)} %bitcast.326, f32[128,4096]{0,1:T(8,128)} %get-tuple-element.53, bf16[128,4096]{0,1:T(8,128)(2,1)S(1)} %convolution_convert_fusion), kind=kOutput, calls=%fused_computation.34 | convolution fusion | flops 1213726720 | bytes 13926400 | tf_op jit(solution)/shard_map/dot_general | solution.py:135
  221.4 7.0 %fusion.62 = f32[8,38,128]{2,1,0:T(8,128)S(1)} fusion(bf16[1,1,8,128,4096]{4,3,2,1,0:T(8,128)(2,1)} %param.15, bf16[128,4096]{0,1:T(8,128)(2,1)} %fusion.52, bf16[128,50]{0,1:T(8,128)(2,1)S(1)} %copy-done.24), kind=kOutput, calls=%fused_computation.58 | convolution fusion | flops 358768640 | bytes 9603072 | tf_op jit(solution)/shard_map/cn,kmn->kcm/dot_general | solution.py:144
  229.5 3.9 all-to-all-start.2
  233.8 11.6 %fusion.46 = bf16[128,4096]{0,1:T(8,128)(2,1)} fusion(bf16[128,1152]{0,1:T(8,128)(2,1)S(1)} %bitcast.341, bf16[144,8,32,128]{3,2,1,0:T(8,128)(2,1)} %bitcast.320, bf16[128,4096]{0,1:T(8,128)(2,1)S(1)} %copy-done.4), kind=kOutput, calls=%fused_computation.31 | convolution fusion | flops 1209532416 | bytes 11829248 | tf_op jit(solution)/shard_map/dot_general | solution.py:119
  245.3 8.1 %fusion.6 = f32[128,1152]{1,0:T(8,128)} fusion(bf16[128,4096]{0,1:T(8,128)(2,1)S(1)} %convolution_convert_fusion, bf16[144,8,32,128]{3,2,1,0:T(8,128)(2,1)} %bitcast.321), kind=kOutput, calls=%fused_computation.6 | convolution fusion | flops 1207959552 | bytes 11075584 | tf_op jit(solution)/shard_map/dot_general | solution.py:61
  257.1 76.2 %all-reduce.1 = (f32[128,50]{0,1:T(8,128)S(1)}, f32[12,128]{1,0:T(8,128)S(1)}) all-reduce(f32[128,50]{0,1:T(8,128)S(1)} %fusion.126, f32[12,128]{1,0:T(8,128)S(1)} %convolution_bitcast_fusion.1), channel_id=1, replica_groups=mesh['tile'=32,'band'=4] {'tile','band'}, use_global_device_ids=true, to_apply=%region_3.4 | all-reduce | flops 7936 | bytes 63488 | tf_op jit(solution)/shard_map/psum | solution.py:165
  334.5 32.4 %all-reduce.6.cloned.1.call-done = bf16[64,38,128]{2,0,1:T(8,128)(2,1)} async-done(((bf16[64,38,128]{2,0,1:T(8,128)(2,1)}), bf16[64,38,128]{2,0,1:T(8,128)(2,1)}) %all-reduce.6.cloned.1.call-update) | async-done | bytes 622608
  366.9 1.5 bitcast_convert_fusion
  368.4 151.3 %all-reduce.8.cloned.1.call-done = (f32[128,1152]{1,0:T(8,128)}, f32[128,1152]{1,0:T(8,128)}) async-done(((f32[128,1152]{1,0:T(8,128)}, f32[128,1152]{1,0:T(8,128)}), (f32[128,1152]{1,0:T(8,128)}, f32[128,1152]{1,0:T(8,128)})) %all-reduce.8.cloned.1.call-update) | async-done | bytes 1179664 | tf_op jit(solution)/shard_map/psum | solution.py:165
  519.8 1.3 broadcast_multiply_fusion
  (191 shorter events, 54.7 us)
Async XLA Ops:
  7.2 22.2 %copy-start = (bf16[1,64,38,128]{3,1,2,0:T(8,128)(2,1)S(1)}, bf16[1,64,38,128]{3,1,2,0:T(8,128)(2,1)}, u32[]{:S(2)}) copy-start(bf16[1,64,38,128]{3,1,2,0:T(8,128)(2,1)} %param.12) | copy-start | bytes 1867780
  7.2 10.3 %copy-start.29 = (s32[8,1]{0,1:T(1,128)S(1)}, s32[8,1]{0,1:T(1,128)}, u32[]{:S(2)}) copy-start(s32[8,1]{0,1:T(1,128)} %param.13) | copy-start | bytes 100
  7.2 10.4 %copy-start.30 = (s32[8]{0:T(128)S(1)}, s32[8]{0:T(128)}, u32[]{:S(2)}) copy-start(s32[8]{0:T(128)} %param.14) | copy-start | bytes 100
  8.2 16.8 %copy-start.15 = (bf16[3,3,128,128]{3,2,1,0:T(8,128)(2,1)S(1)}, bf16[3,3,128,128]{3,2,1,0:T(8,128)(2,1)}, u32[]{:S(2)}) copy-start(bf16[3,3,128,128]{3,2,1,0:T(8,128)(2,1)} %param.17) | copy-start | bytes 884740
  8.2 17.7 %copy-start.14 = (bf16[3,3,128,128]{3,2,1,0:T(8,128)(2,1)S(1)}, bf16[3,3,128,128]{3,2,1,0:T(8,128)(2,1)}, u32[]{:S(2)}) copy-start(bf16[3,3,128,128]{3,2,1,0:T(8,128)(2,1)} %param.18) | copy-start | bytes 884740
  9.5 17.3 %copy-start.31 = (u32[128]{0:T(128)S(1)}, u32[128]{0:T(128)}, u32[]{:S(2)}) copy-start(u32[128]{0:T(128)} %constant.24) | copy-start | bytes 1540
  11.0 23.6 %collective-permute-start.8 = (bf16[128,1,128]{0,1,2:T(2,128)(2,1)}, bf16[128,1,128]{0,1,2:T(2,128)(2,1)S(1)}, u32[]{:S(2)}, u32[]{:S(2)}) collective-permute-start(bf16[128,1,128]{0,1,2:T(2,128)(2,1)} %get-tuple-element.46), channel_id=1, source_target_pairs={{0,4},{4,8},{8,12},{12,16},{16,20},{20,24},{24,28},{28,32},{32,36}... | collective-permute-start | bytes 98312 | tf_op jit(solution)/shard_map/ppermute | solution.py:19
  15.5 19.1 %collective-permute-start.9 = (bf16[128,1,128]{0,1,2:T(2,128)(2,1)}, bf16[128,1,128]{0,1,2:T(2,128)(2,1)}, u32[]{:S(2)}, u32[]{:S(2)}) collective-permute-start(bf16[128,1,128]{0,1,2:T(2,128)(2,1)} %get-tuple-element.47), channel_id=1, source_target_pairs={{4,0},{8,4},{12,8},{16,12},{20,16},{24,20},{28,24},{32,28},{36,32}... | collective-permute-start | bytes 98312 | tf_op jit(solution)/shard_map/ppermute | solution.py:21
  17.6 35.2 %copy-start.27 = (s32[8]{0:T(128)}, s32[8]{0:T(128)S(1)}, u32[]{:S(2)}) copy-start(s32[8]{0:T(128)S(1)} %fusion.142) | copy-start | bytes 100
  18.4 9.7 %all-to-all-start = ((s32[4,1,4]{2,1,0:T(1,128)}), s32[4,1,4]{2,1,0:T(1,128)S(1)}, u32[]{:S(2)}, u32[]{:S(2)}) async-start(s32[4,1,4]{2,1,0:T(1,128)} %bitcast.4), calls=%async_computation | async-start | bytes 4096 | tf_op jit(solution)/shard_map/all_to_all | solution.py:89
  29.4 6.8 %copy-start.25 = (s32[16]{0:T(128)}, s32[16]{0:T(128)S(1)}, u32[]{:S(2)}) copy-start(s32[16]{0:T(128)S(1)} %eq.53) | copy-start | bytes 196
  30.4 22.4 %all-to-all-start.1 = ((bf16[4,4,38,128]{3,1,2,0:T(4,128)(2,1)}), bf16[4,4,38,128]{3,1,2,0:T(4,128)(2,1)S(1)}, u32[]{:S(2)}, u32[]{:S(2)}) async-start(bf16[4,4,38,128]{3,1,2,0:T(4,128)(2,1)} %copy.105), calls=%async_computation.1 | async-start | bytes 311296 | tf_op jit(solution)/shard_map/all_to_all | solution.py:96
  36.2 6.5 %collective-permute-start.10 = (bf16[128,34,1]{0,1,2:T(8,128)(2,1)S(1)}, bf16[128,34,1]{0,1,2:T(8,128)(2,1)S(1)}, u32[]{:S(2)}, u32[]{:S(2)}) collective-permute-start(bf16[128,34,1]{0,1,2:T(8,128)(2,1)S(1)} %get-tuple-element.39), channel_id=1, source_target_pairs={{1,0},{2,1},{3,2},{5,4},{6,5},{7,6},{9,8},{10,9},{11,10},{13,12},{... | collective-permute-start | bytes 26120 | tf_op jit(solution)/shard_map/ppermute | solution.py:21
  37.5 5.2 copy-start.20
  37.9 7.3 %collective-permute-start.11 = (bf16[128,34,1]{0,1,2:T(8,128)(2,1)S(1)}, bf16[128,34,1]{0,1,2:T(8,128)(2,1)S(1)}, u32[]{:S(2)}, u32[]{:S(2)}) collective-permute-start(bf16[128,34,1]{0,1,2:T(8,128)(2,1)S(1)} %get-tuple-element.38), channel_id=1, source_target_pairs={{0,1},{1,2},{2,3},{4,5},{5,6},{6,7},{8,9},{9,10},{10,11},{12,13},{... | collective-permute-start | bytes 26120 | tf_op jit(solution)/shard_map/ppermute | solution.py:19
  53.0 5.0 copy-start.21
  53.0 5.0 copy-start.24
  62.9 21.3 %collective-permute-start = (bf16[128,1,128]{0,1,2:T(2,128)(2,1)S(1)}, bf16[128,1,128]{0,1,2:T(2,128)(2,1)S(1)}, u32[]{:S(2)}, u32[]{:S(2)}) collective-permute-start(bf16[128,1,128]{0,1,2:T(2,128)(2,1)S(1)} %get-tuple-element.50), channel_id=1, source_target_pairs={{0,4},{4,8},{8,12},{12,16},{16,20},{20,24},{24,28},{28,32},{32,36}... | collective-permute-start | bytes 98312 | tf_op jit(solution)/shard_map/ppermute | solution.py:19
  67.9 16.3 %collective-permute-start.1 = (bf16[128,1,128]{0,1,2:T(2,128)(2,1)S(1)}, bf16[128,1,128]{0,1,2:T(2,128)(2,1)S(1)}, u32[]{:S(2)}, u32[]{:S(2)}) collective-permute-start(bf16[128,1,128]{0,1,2:T(2,128)(2,1)S(1)} %get-tuple-element.51), channel_id=1, source_target_pairs={{4,0},{8,4},{12,8},{16,12},{20,16},{24,20},{28,24},{32,28},{36,32}... | collective-permute-start | bytes 98312 | tf_op jit(solution)/shard_map/ppermute | solution.py:21
  71.2 13.0 %copy-start.11 = (bf16[128,32,128]{0,1,2:T(8,128)(2,1)S(1)}, bf16[128,32,128]{0,1,2:T(8,128)(2,1)}, u32[]{:S(2)}) copy-start(bf16[128,32,128]{0,1,2:T(8,128)(2,1)} %copy-done.10) | copy-start | bytes 3145732
  85.0 7.2 %copy-start.3 = (bf16[128,4096]{0,1:T(8,128)(2,1)S(1)}, bf16[128,4096]{0,1:T(8,128)(2,1)}, u32[]{:S(2)}) copy-start(bf16[128,4096]{0,1:T(8,128)(2,1)} %copy-done.2) | copy-start | bytes 3145732
  85.0 5.8 %collective-permute-start.2 = (bf16[128,34,1]{0,1,2:T(8,128)(2,1)S(1)}, bf16[128,34,1]{0,1,2:T(8,128)(2,1)S(1)}, u32[]{:S(2)}, u32[]{:S(2)}) collective-permute-start(bf16[128,34,1]{0,1,2:T(8,128)(2,1)S(1)} %get-tuple-element.43), channel_id=1, source_target_pairs={{0,1},{1,2},{2,3},{4,5},{5,6},{6,7},{8,9},{9,10},{10,11},{12,13},{... | collective-permute-start | bytes 26120 | tf_op jit(solution)/shard_map/ppermute | solution.py:19
  89.1 4.4 collective-permute-start.3
  102.5 12.8 %copy-start.18 = (bf16[3,3,128,128]{2,3,1,0:T(8,128)(2,1)S(1)}, bf16[3,3,128,128]{2,3,1,0:T(8,128)(2,1)}, u32[]{:S(2)}) copy-start(bf16[3,3,128,128]{2,3,1,0:T(8,128)(2,1)} %copy.118) | copy-start | bytes 884740
  115.2 19.0 %slice-start = ((s8[9437184]{0:T(1024)(128)(4,1)}), s8[4194304]{0:T(1024)(128)(4,1)S(1)}, s32[]{:S(2)}) async-start(s8[9437184]{0:T(1024)(128)(4,1)} %bitcast.323), calls=%async_computation.5 | async-start | bytes 8388608
  115.2 19.1 %slice-start.1 = ((s8[9437184]{0:T(1024)(128)(4,1)}), s8[4194304]{0:T(1024)(128)(4,1)S(1)}, s32[]{:S(2)}) async-start(s8[9437184]{0:T(1024)(128)(4,1)} %bitcast.323), calls=%async_computation.6 | async-start | bytes 8388608
  123.2 11.1 %slice-start.2 = ((s8[9437184]{0:T(1024)(128)(4,1)}), s8[1048576]{0:T(1024)(128)(4,1)S(1)}, s32[]{:S(2)}) async-start(s8[9437184]{0:T(1024)(128)(4,1)} %bitcast.323), calls=%async_computation.7 | async-start | bytes 2097152
  134.3 37.3 %copy-start.5 = (bf16[128,4096]{0,1:T(8,128)(2,1)}, bf16[128,4096]{0,1:T(8,128)(2,1)S(1)}, u32[]{:S(2)}) copy-start(bf16[128,4096]{0,1:T(8,128)(2,1)S(1)} %fusion.49) | copy-start | bytes 3145732
  139.5 13.6 %collective-permute-start.4 = (bf16[128,1,128]{0,1,2:T(2,128)(2,1)S(1)}, bf16[128,1,128]{0,1,2:T(2,128)(2,1)S(1)}, u32[]{:S(2)}, u32[]{:S(2)}) collective-permute-start(bf16[128,1,128]{0,1,2:T(2,128)(2,1)S(1)} %get-tuple-element.48), channel_id=1, source_target_pairs={{0,4},{4,8},{8,12},{12,16},{16,20},{20,24},{24,28},{28,32},{32,36}... | collective-permute-start | bytes 98312 | tf_op jit(solution)/shard_map/ppermute | solution.py:19
  144.6 8.5 %collective-permute-start.5 = (bf16[128,1,128]{0,1,2:T(2,128)(2,1)S(1)}, bf16[128,1,128]{0,1,2:T(2,128)(2,1)S(1)}, u32[]{:S(2)}, u32[]{:S(2)}) collective-permute-start(bf16[128,1,128]{0,1,2:T(2,128)(2,1)S(1)} %get-tuple-element.49), channel_id=1, source_target_pairs={{4,0},{8,4},{12,8},{16,12},{20,16},{24,20},{28,24},{32,28},{36,32}... | collective-permute-start | bytes 98312 | tf_op jit(solution)/shard_map/ppermute | solution.py:21
  147.5 9.8 %collective-permute-start.12 = (bf16[128,1,128]{0,1,2:T(2,128)(2,1)S(1)}, bf16[128,1,128]{0,1,2:T(2,128)(2,1)S(1)}, u32[]{:S(2)}, u32[]{:S(2)}) collective-permute-start(bf16[128,1,128]{0,1,2:T(2,128)(2,1)S(1)} %get-tuple-element.44), channel_id=1, source_target_pairs={{0,4},{4,8},{8,12},{12,16},{16,20},{20,24},{24,28},{28,32},{32,36}... | collective-permute-start | bytes 98312 | tf_op jit(solution)/shard_map/ppermute | solution.py:19
  151.1 6.2 %collective-permute-start.13 = (bf16[128,1,128]{0,1,2:T(2,128)(2,1)S(1)}, bf16[128,1,128]{0,1,2:T(2,128)(2,1)S(1)}, u32[]{:S(2)}, u32[]{:S(2)}) collective-permute-start(bf16[128,1,128]{0,1,2:T(2,128)(2,1)S(1)} %get-tuple-element.45), channel_id=1, source_target_pairs={{4,0},{8,4},{12,8},{16,12},{20,16},{24,20},{28,24},{32,28},{36,32}... | collective-permute-start | bytes 98312 | tf_op jit(solution)/shard_map/ppermute | solution.py:21
  154.2 11.5 %collective-permute-start.6 = (bf16[128,34,1]{0,1,2:T(8,128)(2,1)S(1)}, bf16[128,34,1]{0,1,2:T(8,128)(2,1)S(1)}, u32[]{:S(2)}, u32[]{:S(2)}) collective-permute-start(bf16[128,34,1]{0,1,2:T(8,128)(2,1)S(1)} %get-tuple-element.41), channel_id=1, source_target_pairs={{0,1},{1,2},{2,3},{4,5},{5,6},{6,7},{8,9},{9,10},{10,11},{12,13},{... | collective-permute-start | bytes 26120 | tf_op jit(solution)/shard_map/ppermute | solution.py:19
  158.4 7.8 %collective-permute-start.7 = (bf16[128,34,1]{0,1,2:T(8,128)(2,1)S(1)}, bf16[128,34,1]{0,1,2:T(8,128)(2,1)S(1)}, u32[]{:S(2)}, u32[]{:S(2)}) collective-permute-start(bf16[128,34,1]{0,1,2:T(8,128)(2,1)S(1)} %get-tuple-element.40), channel_id=1, source_target_pairs={{1,0},{2,1},{3,2},{5,4},{6,5},{7,6},{9,8},{10,9},{11,10},{13,12},{... | collective-permute-start | bytes 26120 | tf_op jit(solution)/shard_map/ppermute | solution.py:21
  159.7 9.0 %collective-permute-start.14 = (bf16[128,34,1]{0,1,2:T(8,128)(2,1)S(1)}, bf16[128,34,1]{0,1,2:T(8,128)(2,1)S(1)}, u32[]{:S(2)}, u32[]{:S(2)}) collective-permute-start(bf16[128,34,1]{0,1,2:T(8,128)(2,1)S(1)} %get-tuple-element.37), channel_id=1, source_target_pairs={{1,0},{2,1},{3,2},{5,4},{6,5},{7,6},{9,8},{10,9},{11,10},{13,12},{... | collective-permute-start | bytes 26120 | tf_op jit(solution)/shard_map/ppermute | solution.py:21
  161.0 25.8 %collective-permute-start.15 = (bf16[128,34,1]{0,1,2:T(8,128)(2,1)S(1)}, bf16[128,34,1]{0,1,2:T(8,128)(2,1)S(1)}, u32[]{:S(2)}, u32[]{:S(2)}) collective-permute-start(bf16[128,34,1]{0,1,2:T(8,128)(2,1)S(1)} %get-tuple-element.36), channel_id=1, source_target_pairs={{0,1},{1,2},{2,3},{4,5},{5,6},{6,7},{8,9},{9,10},{10,11},{12,13},{... | collective-permute-start | bytes 26120 | tf_op jit(solution)/shard_map/ppermute | solution.py:19
  168.7 4.2 copy-start.9
  186.8 2.7 copy-start.6
  195.8 13.0 %copy-start.16 = (bf16[3,3,128,128]{3,2,1,0:T(8,128)(2,1)S(1)}, bf16[3,3,128,128]{3,2,1,0:T(8,128)(2,1)}, u32[]{:S(2)}) copy-start(bf16[3,3,128,128]{3,2,1,0:T(8,128)(2,1)} %param.17) | copy-start | bytes 884740
  221.4 7.0 %copy-start.28 = (s32[8]{0:T(128)S(1)}, s32[8]{0:T(128)}, u32[]{:S(2)}) copy-start(s32[8]{0:T(128)} %copy-done.27) | copy-start | bytes 100
  221.4 12.4 %copy-start.4 = (bf16[128,4096]{0,1:T(8,128)(2,1)S(1)}, bf16[128,4096]{0,1:T(8,128)(2,1)}, u32[]{:S(2)}) copy-start(bf16[128,4096]{0,1:T(8,128)(2,1)} %copy-done.2) | copy-start | bytes 3145732
  221.4 12.4 %copy-start.17 = (bf16[3,3,128,128]{2,3,1,0:T(8,128)(2,1)S(1)}, bf16[3,3,128,128]{2,3,1,0:T(8,128)(2,1)}, u32[]{:S(2)}) copy-start(bf16[3,3,128,128]{2,3,1,0:T(8,128)(2,1)} %copy.129) | copy-start | bytes 884740
  229.5 23.9 %all-to-all-start.2 = ((bf16[4,4,38,128]{3,1,2,0:T(4,128)(2,1)}), bf16[4,4,38,128]{3,1,2,0:T(4,128)(2,1)S(1)}, u32[]{:S(2)}, u32[]{:S(2)}) async-start(bf16[4,4,38,128]{3,1,2,0:T(4,128)(2,1)} %copy.152), calls=%async_computation.2 | async-start | bytes 311296 | tf_op jit(solution)/shard_map/all_to_all | solution.py:148
  233.5 133.5 %all-reduce.6.cloned.1.call-start = ((), (), s32[]{:S(2)}) async-start(), calls=%async_computation.3 | async-start | bytes 1245184
  245.3 8.2 %copy-start.26 = (s32[16]{0:T(128)S(1)}, s32[16]{0:T(128)}, u32[]{:S(2)}) copy-start(s32[16]{0:T(128)} %copy-done.25) | copy-start | bytes 196
  245.3 9.5 %copy-start.12 = (bf16[128,4096]{0,1:T(8,128)(2,1)S(1)}, bf16[128,4096]{0,1:T(8,128)(2,1)}, u32[]{:S(2)}) copy-start(bf16[128,4096]{0,1:T(8,128)(2,1)} %fusion.46) | copy-start | bytes 3145732
  254.8 265.0 %all-reduce.8.cloned.1.call-start = ((), (), s32[]{:S(2)}) async-start(), calls=%async_computation.4 | async-start | bytes 2359296 | tf_op jit(solution)/shard_map/psum | solution.py:165
  521.1 2.6 copy-start.1
  (8 other events, 10.2 us)
Sparse Core Ops, SparseCore 0:
  254.9 111.9 all-reduce.5
  372.3 147.3 all-reduce.7
where the time goes:
time: 541 us; the launch traced here: 531 us
  waiting for transfers between devices  184 us (34%)
  local copies, waits for them, and re-layouts  91 us (17%)
  blocking collectives  76.2 us (14%)
  matrix products  74 us (14%)
  starting transfers between devices  60.6 us (11%)
  other arithmetic  29 us (5%)
  between operations  16.1 us (3%)
    psum x1, waiting for transfers between devices, per_device(): lax.psum((grad_in_part, grad_one_part, grad_two_part, grad_out_part), ('t...  151 us
    psum x1, blocking collectives, per_device(): lax.psum((grad_in_part, grad_one_part, grad_two_part, grad_out_part), ('t...  76.2 us
    another operation x6, local copies, waits for them, and re-layouts, shifted_stack(): stacked = jnp.stack(pieces, 0)  53.3 us
    ppermute x8, starting transfers between devices, padded_2(): lax.ppermute(tail, axis, [(i, (i + 1) % count) for i in range(ends)])  33.7 us
    unnamed x3, waiting for transfers between devices  32.5 us
    unnamed x98, local copies, waits for them, and re-layouts  28.8 us
    unnamed x19, other arithmetic  17.3 us
    ppermute x8, starting transfers between devices, padded_2(): lax.ppermute(head, axis, [((i + 1) % count, i) for i in range(ends)])  13.4 us
  transfers between devices with their start and end apart: 21, of which 3 were waited for; matrix products, arithmetic and copies ran while one was open for 16% of the time, Pallas kernels for 0%

commit v1 on v0

v1 whole, which is shorter than its diff:
```python
import functools
import math

import jax
import jax.numpy as jnp
import numpy as np
from jax import lax
from jax.experimental import pallas as pl
from jax.experimental.pallas import tpu as pltpu
from jax.sharding import PartitionSpec as P

MOST = 4
ALL = ("tile", "band")

PITCH = 132
HIGH = 36
SPAN = 4864
GUARD = 256
STEP = 256
STEPS = SPAN // STEP
FEED = 80
NOISY_AT = 48
GRAD_AT = 60
CHUNK = 24
NT = (((1,), (1,)), ((), ()))


def f32dot(left, right):
    return jnp.dot(left, right, preferred_element_type=jnp.float32)


def vmem(limit=56 * 1024 * 1024):
    return pltpu.CompilerParams(vmem_limit_bytes=limit)


def whole():
    return pl.BlockSpec(memory_space=pltpu.VMEM)


def scalars():
    return pl.BlockSpec(memory_space=pltpu.SMEM)


def plan_kernel(band_ref, slot_ref, place_ref, wanted_ref):
    count = slot_ref.shape[0]
    for i in range(wanted_ref.shape[0]):
        wanted_ref[i] = jnp.int32(-1)
    for j in range(count):
        band = band_ref[j]
        rank = jnp.int32(0)
        for i in range(j):
            rank = rank + jnp.where(band_ref[i] == band, 1, 0)
        place = band * MOST + rank
        place_ref[j] = place
        wanted_ref[place] = slot_ref[j]


def plan(bands, slots, total):
    return pl.pallas_call(
        plan_kernel,
        out_shape=(
            jax.ShapeDtypeStruct(slots.shape, jnp.int32),
            jax.ShapeDtypeStruct((total,), jnp.int32),
        ),
        in_specs=[scalars(), scalars()],
        out_specs=(scalars(), scalars()),
    )(bands, slots)


def serve_kernel(asked_ref, coarse_ref, out_ref):
    for i in range(out_ref.shape[0]):
        out_ref[i] = coarse_ref[jnp.maximum(asked_ref[i], 0)]


def serve(asked, coarse):
    return pl.pallas_call(
        serve_kernel,
        out_shape=jax.ShapeDtypeStruct((asked.shape[0],) + coarse.shape[1:], coarse.dtype),
        in_specs=[scalars(), whole()],
        out_specs=whole(),
        compiler_params=vmem(),
    )(asked, coarse)


def feed_kernel(place_ref, arrived_ref, interp_ref, given_ref, feed_ref, edge_ref, picked):
    step = pl.program_id(0)
    ch = arrived_ref.shape[1]
    count = interp_ref.shape[0]
    cells = interp_ref.shape[1]
    lanes = interp_ref.shape[2]

    @pl.when(step == 0)
    def _():
        edge_ref[...] = jnp.zeros_like(edge_ref)
        for j in range(count):
            picked[:, j * cells : (j + 1) * cells] = arrived_ref[place_ref[j]]

    matrix = interp_ref[...].reshape(count * cells, lanes)
    cond = f32dot(picked[...], matrix).astype(jnp.bfloat16)
    feed_ref[...] = jnp.zeros_like(feed_ref)
    feed_ref[0:ch, :] = cond
    feed_ref[NOISY_AT:, :] = given_ref[...]
    rows = lanes // 128
    at = lax.broadcasted_iota(jnp.int32, (lanes, 128), 0)
    lane = lax.broadcasted_iota(jnp.int32, (lanes, 128), 1)
    row = jnp.bitwise_and(jnp.right_shift(lane, 1), 31) - step * rows
    col = jnp.bitwise_and(lane, 1) + jnp.where(lane >= 64, 126, 0)
    hit = jnp.where(row * 128 + col == at, 1.0, 0.0).astype(jnp.bfloat16)
    edge_ref[...] += f32dot(feed_ref[...], hit).astype(jnp.bfloat16)


def make_feed(place, arrived, interp, given, blocks=4):
    count, cells, n = interp.shape
    ch = arrived.shape[1]
    lanes = n // blocks
    return pl.pallas_call(
        feed_kernel,
        grid=(blocks,),
        out_shape=(
            jax.ShapeDtypeStruct((FEED, n), jnp.bfloat16),
            jax.ShapeDtypeStruct((FEED, 128), jnp.bfloat16),
        ),
        in_specs=[
            scalars(),
            whole(),
            pl.BlockSpec((count, cells, lanes), lambda i: (0, 0, i)),
            pl.BlockSpec((FEED - NOISY_AT, lanes), lambda i: (0, i)),
        ],
        out_specs=(
            pl.BlockSpec((FEED, lanes), lambda i: (0, i)),
            pl.BlockSpec((FEED, 128), lambda i: (0, 0)),
        ),
        scratch_shapes=[pltpu.VMEM((ch, count * cells), jnp.bfloat16)],
        compiler_params=vmem(),
    )(place, arrived, interp, given)


def strip_kernel(top_ref, bot_ref, edge_ref, left_ref, right_ref):
    wide = jnp.concatenate([top_ref[...], bot_ref[...]], axis=1)
    at = lax.broadcasted_iota(jnp.int32, (512, 128), 0)
    lane = lax.broadcasted_iota(jnp.int32, (512, 128), 1)
    spot = jnp.bitwise_and(lane, 63)
    source = jnp.right_shift(spot, 1) * 128 + jnp.bitwise_and(spot, 1)
    source = source + jnp.where(lane >= 64, 126, 0)
    hit = jnp.where(jnp.logical_and(source == at, spot < 8), 1.0, 0.0).astype(jnp.bfloat16)
    corner = f32dot(wide, hit).astype(jnp.bfloat16)
    edge = edge_ref[...]
    left_ref[...] = jnp.concatenate([edge[:, 0:64], corner[:, 0:64]], axis=1)
    right_ref[...] = jnp.concatenate([edge[:, 64:128], corner[:, 64:128]], axis=1)


def strips(top, bot, edge):
    shape = jax.ShapeDtypeStruct((FEED, 128), jnp.bfloat16)
    return pl.pallas_call(
        strip_kernel,
        out_shape=(shape, shape),
        in_specs=[whole()] * 3,
        out_specs=(whole(), whole()),
        compiler_params=vmem(),
    )(top, bot, edge)


def tap_offset(tap):
    return (tap // 3 - 1) * PITCH + tap % 3 - 1


def net_kernel(
    feed_ref,
    top_ref,
    bot_ref,
    left_ref,
    right_ref,
    mask_ref,
    w_first_ref,
    w_one_ref,
    w_one_back_ref,
    w_two_ref,
    w_two_back_ref,
    w_out_ref,
    w_cond_ref,
    pred_ref,
    dcond_ref,
    grads_ref,
    x_ref,
    a_zero_ref,
    d_two_ref,
    a_one_ref,
    d_one_ref,
    slope_zero_ref,
    sum_one_ref,
    sum_two_ref,
    sum_in_ref,
    sum_out_ref,
    pred_wide_ref,
    dcond_wide_ref,
):
    rows = pred_ref.shape[1]
    ch = 128
    x_ref[:, HIGH * PITCH :] = jnp.zeros((FEED, SPAN - HIGH * PITCH), jnp.bfloat16)
    left = left_ref[...]
    right = right_ref[...]
    for r in range(HIGH):
        if r < 2:
            body = top_ref[:, r * 128 : (r + 1) * 128]
            spot = 64 + 2 * r
        elif r < rows + 2:
            body = feed_ref[:, (r - 2) * 128 : (r - 1) * 128]
            spot = 2 * (r - 2)
        else:
            body = bot_ref[:, (r - rows - 2) * 128 : (r - rows - 1) * 128]
            spot = 68 + 2 * (r - rows - 2)
        line = jnp.concatenate([left[:, spot : spot + 2], body, right[:, spot : spot + 2]], axis=1)
        x_ref[:, r * PITCH : (r + 1) * PITCH] = line
    for ref in (a_zero_ref, d_two_ref, a_one_ref, d_one_ref):
        ref[:, 0:GUARD] = jnp.zeros((ch, GUARD), jnp.bfloat16)
        ref[:, GUARD + SPAN :] = jnp.zeros((ch, GUARD), jnp.bfloat16)
    for ref in (sum_one_ref, sum_two_ref, sum_in_ref, sum_out_ref):
        ref[...] = jnp.zeros_like(ref)

    def at(i, shift=0, extra=0):
        return pl.ds(pl.multiple_of(i * STEP + shift, 128), STEP + extra)

    def taps(ref, i, sign):
        window = ref[:, at(i, 0, 2 * GUARD)]
        pieces = []
        for tap in range(9):
            start = GUARD + sign * tap_offset(tap)
            pieces.append(window[:, start : start + STEP])
        return jnp.concatenate(pieces, axis=0)

    def first(i, carry):
        both = f32dot(w_first_ref[...], x_ref[:, at(i)])
        h_zero = both[0:ch]
        sig = jax.nn.sigmoid(h_zero)
        a_zero_ref[:, at(i, GUARD)] = (h_zero * sig).astype(jnp.bfloat16)
        slope_zero_ref[:, at(i)] = sig * (1.0 + h_zero * (1.0 - sig))
        d_two_ref[:, at(i, GUARD)] = both[ch:].astype(jnp.bfloat16)
        return carry

    lax.fori_loop(0, STEPS, first, 0)

    def second(i, carry):
        inside = mask_ref[0:1, at(i)]
        z_one = f32dot(w_one_ref[...], taps(a_zero_ref, i, 1))
        sig = jax.nn.sigmoid(z_one)
        a_one_ref[:, at(i, GUARD)] = (z_one * sig * inside).astype(jnp.bfloat16)
        slope = sig * (1.0 + z_one * (1.0 - sig))
        back = f32dot(w_two_back_ref[...], taps(d_two_ref, i, -1))
        d_one_ref[:, at(i, GUARD)] = (back * slope * inside).astype(jnp.bfloat16)
        return carry

    lax.fori_loop(0, STEPS, second, 0)

    def third(i, carry):
        own = mask_ref[1:2, at(i)]
        x = x_ref[:, at(i)]
        d_two = d_two_ref[:, at(i, GUARD)].astype(jnp.float32)
        cols_one = taps(a_one_ref, i, 1)
        z_two = f32dot(w_two_ref[...], cols_one)
        a_two = (a_zero_ref[:, at(i, GUARD)].astype(jnp.float32) + z_two).astype(jnp.bfloat16)
        pred_wide_ref[:, at(i)] = f32dot(w_out_ref[...], a_two)
        a_two_own = (a_two.astype(jnp.float32) * own).astype(jnp.bfloat16)
        sum_out_ref[...] += lax.dot_general(a_two_own, x, NT, preferred_element_type=jnp.float32)
        d_two_own = (d_two * own).astype(jnp.bfloat16)
        sum_two_ref[...] += lax.dot_general(
            d_two_own, cols_one, NT, preferred_element_type=jnp.float32
        )
        back = f32dot(w_one_back_ref[...], taps(d_one_ref, i, -1))
        d_zero = ((back + d_two) * slope_zero_ref[:, at(i)] * own).astype(jnp.bfloat16)
        sum_in_ref[...] += lax.dot_general(d_zero, x, NT, preferred_element_type=jnp.float32)
        dcond_wide_ref[:, at(i)] = f32dot(w_cond_ref[...], d_zero)
        d_one_own = (d_one_ref[:, at(i, GUARD)].astype(jnp.float32) * own).astype(jnp.bfloat16)
        sum_one_ref[...] += lax.dot_general(
            d_one_own, taps(a_zero_ref, i, 1), NT, preferred_element_type=jnp.float32
        )
        return carry

    lax.fori_loop(0, STEPS, third, 0)

    for r in range(rows):
        start = (r + 2) * PITCH + 2
        pred_ref[:, r, :] = pred_wide_ref[0 : pred_ref.shape[0], start : start + 128]
        dcond_ref[:, r * 128 : (r + 1) * 128] = dcond_wide_ref[
            :, start : start + 128
        ].astype(jnp.bfloat16)
    for tap in range(9):
        lanes = slice(tap * 128, (tap + 1) * 128)
        grads_ref[tap * 128 : (tap + 1) * 128, :] = sum_two_ref[:, lanes].astype(jnp.bfloat16)
        grads_ref[(9 + tap) * 128 : (10 + tap) * 128, :] = sum_one_ref[:, lanes].astype(
            jnp.bfloat16
        )
    grads_ref[2304:2560, :] = jnp.zeros((256, 128), jnp.bfloat16)
    grads_ref[2304:2432, 0:FEED] = sum_in_ref[...].astype(jnp.bfloat16)
    grads_ref[2432:2560, 0:FEED] = sum_out_ref[...].astype(jnp.bfloat16)
    grads_ref[2560:, :] = jnp.zeros((128 * CHUNK - 2560, 128), jnp.bfloat16)


def net(chans, rows, cols, args):
    ch = 128
    wide = SPAN + 2 * GUARD
    bf, f32 = jnp.bfloat16, jnp.float32
    return pl.pallas_call(
        net_kernel,
        out_shape=(
            jax.ShapeDtypeStruct((chans, rows, cols), f32),
            jax.ShapeDtypeStruct((48, rows * cols), bf),
            jax.ShapeDtypeStruct((128 * CHUNK, 128), bf),
        ),
        in_specs=[whole()] * len(args),
        out_specs=(whole(),) * 3,
        scratch_shapes=[
            pltpu.VMEM((FEED, SPAN), bf),
            pltpu.VMEM((ch, wide), bf),
            pltpu.VMEM((ch, wide), bf),
            pltpu.VMEM((ch, wide), bf),
            pltpu.VMEM((ch, wide), bf),
            pltpu.VMEM((ch, SPAN), f32),
            pltpu.VMEM((ch, 9 * ch), f32),
            pltpu.VMEM((ch, 9 * ch), f32),
            pltpu.VMEM((ch, FEED), f32),
            pltpu.VMEM((ch, FEED), f32),
            pltpu.VMEM((16, SPAN), f32),
            pltpu.VMEM((48, SPAN), f32),
        ],
        compiler_params=vmem(),
    )(*args)


def block_kernel(place_ref, dcond_ref, interp_ref, out_ref, total):
    step = pl.program_id(0)
    count, cells, lanes = interp_ref.shape
    ch = out_ref.shape[1]
    matrix = interp_ref[...].reshape(count * cells, lanes)
    part = lax.dot_general(dcond_ref[...], matrix, NT, preferred_element_type=jnp.float32)

    @pl.when(step == 0)
    def _():
        total[...] = part

    @pl.when(step > 0)
    def _():
        total[...] += part

    @pl.when(step == pl.num_programs(0) - 1)
    def _():
        out_ref[...] = jnp.zeros_like(out_ref)
        for j in range(count):
            out_ref[place_ref[j]] = total[0:ch, j * cells : (j + 1) * cells].astype(jnp.bfloat16)


def blocks_back(place, dcond, interp, slots, ch, blocks=4):
    count, cells, n = interp.shape
    lanes = n // blocks
    return pl.pallas_call(
        block_kernel,
        grid=(blocks,),
        out_shape=jax.ShapeDtypeStruct((slots, ch, cells), jnp.bfloat16),
        in_specs=[
            scalars(),
            pl.BlockSpec((dcond.shape[0], lanes), lambda i: (0, i)),
            pl.BlockSpec((count, cells, lanes), lambda i: (0, 0, i)),
        ],
        out_specs=pl.BlockSpec((slots, ch, cells), lambda i: (0, 0, 0)),
        scratch_shapes=[pltpu.VMEM((dcond.shape[0], count * cells), jnp.float32)],
        compiler_params=vmem(),
    )(place, dcond, interp)


def gather_kernel(asked_ref, returned_ref, out_ref, total):
    total[...] = jnp.zeros_like(total)
    for i in range(returned_ref.shape[0]):
        slot = asked_ref[i]

        @pl.when(slot >= 0)
        def _(slot=slot, i=i):
            total[slot] += returned_ref[i].astype(jnp.float32)

    out_ref[...] = total[...].astype(jnp.bfloat16)


def band_blocks(asked, returned, per_band):
    shape = (per_band,) + returned.shape[1:]
    return pl.pallas_call(
        gather_kernel,
        out_shape=jax.ShapeDtypeStruct(shape, jnp.bfloat16),
        in_specs=[scalars(), whole()],
        out_specs=whole(),
        scratch_shapes=[pltpu.VMEM(shape, jnp.float32)],
        compiler_params=vmem(),
    )(asked, returned)


def block_sum_kernel(parts_ref, out_ref):
    total = parts_ref[0].astype(jnp.float32)
    for i in range(1, parts_ref.shape[0]):
        total = total + parts_ref[i].astype(jnp.float32)
    out_ref[...] = total


def block_sum(parts):
    return pl.pallas_call(
        block_sum_kernel,
        out_shape=jax.ShapeDtypeStruct(parts.shape[1:], jnp.float32),
        in_specs=[whole()],
        out_specs=whole(),
        compiler_params=vmem(),
    )(parts)


def share_kernel(parts_ref, out_ref):
    total = parts_ref[0].astype(jnp.float32)
    for i in range(1, parts_ref.shape[0]):
        total = total + parts_ref[i].astype(jnp.float32)
    out_ref[...] = jnp.broadcast_to(total.astype(jnp.bfloat16)[None], out_ref.shape)


def share(parts):
    return pl.pallas_call(
        share_kernel,
        out_shape=jax.ShapeDtypeStruct(parts.shape, jnp.bfloat16),
        in_specs=[whole()],
        out_specs=whole(),
        compiler_params=vmem(),
    )(parts)


def final_kernel(factor, parts_ref, in_ref, one_ref, two_ref, out_ref):
    ch = in_ref.shape[0]
    side = two_ref.shape[0]
    for tap in range(9):
        two_ref[tap // side, tap % side] = (
            parts_ref[tap * ch : (tap + 1) * ch, :].astype(jnp.float32) * factor
        )
        one_ref[tap // side, tap % side] = (
            parts_ref[(9 + tap) * ch : (10 + tap) * ch, :].astype(jnp.float32) * factor
        )
    first = parts_ref[18 * ch : 19 * ch, :].astype(jnp.float32) * factor
    chans = out_ref.shape[0]
    coarse_ch = in_ref.shape[1] - chans
    in_ref[:, 0:coarse_ch] = first[:, 0:coarse_ch]
    in_ref[:, coarse_ch:] = first[:, NOISY_AT : NOISY_AT + chans]
    last = parts_ref[19 * ch : 20 * ch, :].astype(jnp.float32) * factor
    out_ref[...] = last.T[GRAD_AT : GRAD_AT + chans, :]


def final(parts, width, taps, inner, chans, factor):
    f32 = jnp.float32
    return pl.pallas_call(
        functools.partial(final_kernel, factor),
        out_shape=(
            jax.ShapeDtypeStruct((width, inner), f32),
            jax.ShapeDtypeStruct(taps, f32),
            jax.ShapeDtypeStruct(taps, f32),
            jax.ShapeDtypeStruct((chans, width), f32),
        ),
        in_specs=[whole()],
        out_specs=(whole(),) * 4,
        compiler_params=vmem(),
    )(parts)


def halo(first, last, axis):
    count = lax.axis_size(axis)
    up = [(i, i + 1) for i in range(count - 1)]
    down = [(i + 1, i) for i in range(count - 1)]
    return lax.ppermute(last, axis, up), lax.ppermute(first, axis, down)


def cell_masks(rows, cols, n_tile, n_band):
    flat = np.arange(SPAN)
    row = flat // PITCH
    col = flat % PITCH
    own = (row >= 2) & (row < rows + 2) & (col >= 2) & (col < cols + 2)
    grid_row = lax.axis_index("tile") * rows + (row - 2)
    grid_col = lax.axis_index("band") * cols + (col - 2)
    inside = (
        (grid_row >= 0)
        & (grid_row < rows * n_tile)
        & (grid_col >= 0)
        & (grid_col < cols * n_band)
    )
    masks = jnp.stack([inside.astype(jnp.float32), jnp.asarray(own, jnp.float32)])
    return jnp.pad(masks, ((0, 6), (0, 0)))


def per_device(
    noisy, grad_pred, coarse, margin_band, margin_slot, interp, w_in, w_conv1, w_conv2, w_out
):
    width = w_in.shape[0]
    chans, rows, cols = noisy.shape
    cells = rows * cols
    coarse_ch = coarse.shape[2]
    per_band = coarse.shape[1]
    n_band = lax.axis_size("band")
    n_tile = lax.axis_size("tile")
    slots = n_band * MOST
    local_interp = interp[0, 0]

    place, wanted = plan(margin_band.reshape(-1), margin_slot, slots)
    asked = lax.all_to_all(
        wanted.reshape(n_band, MOST), "band", split_axis=0, concat_axis=0, tiled=True
    ).reshape(slots)
    served = serve(asked, coarse[0])
    arrived = lax.all_to_all(served, "band", split_axis=0, concat_axis=0, tiled=True)

    given = jnp.concatenate(
        [
            noisy.reshape(chans, cells),
            grad_pred.reshape(chans, cells),
            jnp.zeros((FEED - NOISY_AT - 2 * chans, cells), jnp.bfloat16),
        ],
        0,
    )
    w_pad = lambda w, before: jnp.pad(w, ((0, 0), (before, FEED - before - w.shape[1])))
    w_first = jnp.concatenate(
        [
            w_pad(w_in[:, :coarse_ch], 0) + w_pad(w_in[:, coarse_ch:], NOISY_AT),
            w_pad(w_out.T, GRAD_AT),
        ],
        0,
    )
    forward = lambda w: w.transpose(2, 0, 1, 3).reshape(width, 9 * width)
    backward = lambda w: w.transpose(3, 0, 1, 2).reshape(width, 9 * width)
    masks = cell_masks(rows, cols, n_tile, n_band)

    feed, edge = make_feed(place, arrived, local_interp, given)
    top, bot = halo(feed[:, : 2 * cols], feed[:, cells - 2 * cols :], "tile")
    left_out, right_out = strips(top, bot, edge)
    left, right = halo(left_out, right_out, "band")
    pred, dcond, grads = net(
        chans,
        rows,
        cols,
        (
            feed,
            top,
            bot,
            left,
            right,
            masks,
            w_first,
            forward(w_conv1),
            backward(w_conv1),
            forward(w_conv2),
            backward(w_conv2),
            jnp.pad(w_out, ((0, 16 - chans), (0, 0))),
            jnp.pad(w_in[:, :coarse_ch].T, ((0, 48 - coarse_ch), (0, 0))),
        ),
    )
    grads = lax.all_to_all(
        grads.reshape(n_tile * n_band, CHUNK, 128), ALL, split_axis=0, concat_axis=0, tiled=True
    )
    outgoing = blocks_back(place, dcond, local_interp, slots, coarse_ch)
    returned = lax.all_to_all(outgoing, "band", split_axis=0, concat_axis=0, tiled=True)
    summed = lax.all_to_all(share(grads), ALL, split_axis=0, concat_axis=0, tiled=True)
    owned = band_blocks(asked, returned, per_band)
    mine = lax.all_to_all(owned, "tile", split_axis=0, concat_axis=0, tiled=True)
    coarse_grad = block_sum(
        mine.reshape((n_tile, 1, per_band // n_tile) + coarse.shape[2:])
    )
    factor = 1.0 / math.sqrt(cells * n_tile * n_band)
    grad_in, grad_one, grad_two, grad_out = final(
        summed.reshape(-1, 128), width, w_conv1.shape, w_in.shape[1], chans, factor
    )
    return (pred, coarse_grad, grad_in, grad_one, grad_two, grad_out)


def solution(mesh):
    placed = (
        P(None, "tile", "band"),
        P(None, "tile", "band"),
        P("band", None, None, None),
        P(("tile", "band"), None),
        P(("tile", "band")),
        P("tile", "band", None, None, None),
        P(),
        P(),
        P(),
        P(),
    )
    return jax.shard_map(
        per_device,
        mesh=mesh,
        in_specs=placed,
        out_specs=(P(None, "tile", "band"), P("band", "tile", None, None), P(), P(), P(), P()),
        check_vma=False,
    )
```

time: 541 us -> 203 us (0.38); the launches traced: 531 us -> 202 us
  waiting for transfers between devices: 184 us -> 44.3 us
  Pallas kernels: 0 us -> 83 us
  matrix products: 74 us -> 0 us
  local copies, waits for them, and re-layouts: 91 us -> 21.3 us
  blocking collectives: 76.2 us -> 9.82 us
  other arithmetic: 29 us -> 3.66 us
  starting transfers between devices: 60.6 us -> 38.7 us
  between operations: 16.1 us -> 0.84 us
    psum x1 -> x0, waiting for transfers between devices: 151 us -> none  [per_device(): lax.psum((grad_in_part, grad_one_part, grad_two_part, grad_out_part), ('t...]
    pallas_call x0 -> x10, Pallas kernels: none -> 83 us  [the longest x1 57.4 us: net(): pl.pallas_call(net_kernel, out_shape=(jax.ShapeDtypeStruct((chans, rows,...]
    psum x1 -> x0, blocking collectives: 76.2 us -> none  [per_device(): lax.psum((grad_in_part, grad_one_part, grad_two_part, grad_out_part), ('t...]
    dot_general x17 -> x0, matrix products: 74 us -> none  [the longest x4 13 us: outer_sum(): lax.dot_general(left, right, (((1,), (1,)), ((), ())), preferred_element_...]
    another operation x6 -> x1, local copies, waits for them, and re-layouts: 53.3 us -> 0.02 us  [cell_masks(): jnp.stack([inside.astype(jnp.float32), jnp.asarray(own, jnp.float32)])]
    all_to_all x2 -> x4, waiting for transfers between devices: 0.01 us -> 43.2 us  [the longest x1 14.6 us: per_device(): lax.all_to_all(grads.reshape(n_tile * n_band, CHUNK, 128), ALL, split_axi...]
    ppermute x16 -> x4, starting transfers between devices: 47.1 us -> 11.1 us  [halo(): return (lax.ppermute(last, axis, up), lax.ppermute(first, axis, down))]
    unnamed x3 -> x0, waiting for transfers between devices: 32.5 us -> none
  transfers between devices with their start and end apart: 21 -> 9, of which waited for: 3 -> 5; matrix products, arithmetic and copies ran while one was open for 16% -> 8% of each run, Pallas kernels for 0% -> 3%
where the time goes in v1:
time: 203 us; the launch traced here: 202 us
  Pallas kernels  83 us (41%)
  waiting for transfers between devices  44.3 us (22%)
  starting transfers between devices  38.7 us (19%)
  local copies, waits for them, and re-layouts  21.3 us (10%)
  blocking collectives  9.82 us (5%)
  other arithmetic  3.66 us (2%)
    pallas_call x1, Pallas kernels, net(): pl.pallas_call(net_kernel, out_shape=(jax.ShapeDtypeStruct((chans, rows,...  57.4 us
    all_to_all x1, waiting for transfers between devices, per_device(): lax.all_to_all(grads.reshape(n_tile * n_band, CHUNK, 128), ALL, split_axi...  14.6 us
    all_to_all x1, waiting for transfers between devices, per_device(): lax.all_to_all(share(grads), ALL, split_axis=0, concat_axis=0, tiled=True)  13.5 us
    ppermute x4, starting transfers between devices, halo(): return (lax.ppermute(last, axis, up), lax.ppermute(first, axis, down))  11.1 us
    unnamed x31, local copies, waits for them, and re-layouts  11 us
    all_to_all x1, waiting for transfers between devices, per_device(): lax.all_to_all(owned, 'tile', split_axis=0, concat_axis=0, tiled=True)  10.8 us
    all_to_all x1, blocking collectives, per_device(): lax.all_to_all(outgoing, 'band', split_axis=0, concat_axis=0, tiled=True)  9.82 us
    all_to_all x1, starting transfers between devices, per_device(): lax.all_to_all(grads.reshape(n_tile * n_band, CHUNK, 128), ALL, split_axi...  9.63 us
  transfers between devices with their start and end apart: 9, of which 5 were waited for; matrix products, arithmetic and copies ran while one was open for 8% of the time, Pallas kernels for 3%

profile of v1, /device:TPU:1, one launch (start us, length us, event | category | flops | bytes accessed | tf_op | source)
XLA Modules:
  0.0 201.7 jit_solution(12794286612678213626)
XLA Ops:
  0.7 1.4 shard_map.172
  2.0 1.3 all_to_all.21
  3.4 5.9 %all-to-all-start = ((s32[4,1,4]{2,1,0:T(1,128)}), s32[4,1,4]{2,1,0:T(1,128)S(1)}, u32[]{:S(2)}, u32[]{:S(2)}) async-start(s32[4,1,4]{2,1,0:T(1,128)} %bitcast.1), calls=%async_computation | async-start | bytes 4096 | tf_op jit(solution)/shard_map/all_to_all | solution.py:500
  9.2 0.7 slice.16
  9.9 0.8 fusion.5
  10.7 0.9 pad.40
  11.7 0.9 pad.41
  12.6 2.3 %copy.51 = bf16[1,64,38,128]{3,2,1,0:T(8,128)(2,1)} copy(bf16[1,64,38,128]{3,1,2,0:T(8,128)(2,1)} %param.15) | data formatting | bytes 1245184 | tf_op args[2]
  15.0 1.4 select_maximum_fusion.mask_ref
  16.5 0.8 maximum_maximum_fusion.given_ref
  17.8 0.7 reduce.3
  18.5 0.7 reshape.51.asked_ref
  19.1 1.8 shard_map.173
  20.9 4.2 %all-to-all-start.1 = ((bf16[16,38,128]{2,1,0:T(8,128)(2,1)}), bf16[16,38,128]{2,1,0:T(8,128)(2,1)S(1)}, u32[]{:S(2)}, u32[]{:S(2)}) async-start(bf16[16,38,128]{2,1,0:T(8,128)(2,1)} %shard_map.173), calls=%async_computation.1 | async-start | bytes 327680 | tf_op jit(solution)/shard_map/all_to_all | solution.py:504
  25.2 0.7 slice_bitcast_fusion
  25.9 4.3 %all-to-all-done.1.arrived_ref = bf16[16,38,128]{2,1,0:T(8,128)(2,1)S(1)} async-done(((bf16[16,38,128]{2,1,0:T(8,128)(2,1)}), bf16[16,38,128]{2,1,0:T(8,128)(2,1)S(1)}, u32[]{:S(2)}, u32[]{:S(2)}) %all-to-all-start.1) | async-done | bytes 155680 | tf_op jit(solution)/shard_map/all_to_all | solution.py:504
  30.2 0.7 copy-done.5
  30.8 6.0 %shard_map.174 = (bf16[80,4096]{1,0:T(8,128)(2,1)}, bf16[80,128]{1,0:T(8,128)(2,1)}) custom-call(s32[8]{0:T(128)} %get-tuple-element.19.place_ref, bf16[16,38,128]{2,1,0:T(8,128)(2,1)} %copy-done.5, bf16[8,128,4096]{2,1,0:T(8,128)(2,1)} %bitcast.30, bf16[32,4096]{1,0:T(8,128)(2,1)} %maximum_maximum_fusion.given_ref), custom_call_target="tpu_custom_call" | custom-call | tf_op jit(solution)/shard_map/pallas_call | solution.py:116
  36.8 0.8 fusion.6
  37.6 4.6 %collective-permute-start.1 = (bf16[80,256]{1,0:T(8,128)(2,1)S(1)}, bf16[80,256]{1,0:T(8,128)(2,1)S(1)}, u32[]{:S(2)}, u32[]{:S(2)}) collective-permute-start(bf16[80,256]{1,0:T(8,128)(2,1)S(1)} %get-tuple-element.50), channel_id=1, source_target_pairs={{4,0},{8,4},{12,8},{16,12},{20,16},{24,20},{28,24},{32,28},{36,32}... | collective-permute-start | bytes 122888 | tf_op jit(solution)/shard_map/ppermute | solution.py:466
  42.2 3.0 %collective-permute-start = (bf16[80,256]{1,0:T(8,128)(2,1)S(1)}, bf16[80,256]{1,0:T(8,128)(2,1)S(1)}, u32[]{:S(2)}, u32[]{:S(2)}) collective-permute-start(bf16[80,256]{1,0:T(8,128)(2,1)S(1)} %get-tuple-element.51), channel_id=1, source_target_pairs={{0,4},{4,8},{8,12},{12,16},{16,20},{20,24},{24,28},{28,32},{32,36}... | collective-permute-start | bytes 122888 | tf_op jit(solution)/shard_map/ppermute | solution.py:466
  45.2 1.0 collective-permute-done.top_ref
  46.3 0.6 copy-done.7
  46.9 1.7 shard_map.175
  48.6 2.2 %collective-permute-start.2 = (bf16[80,128]{1,0:T(8,128)(2,1)}, bf16[80,128]{1,0:T(8,128)(2,1)S(1)}, u32[]{:S(2)}, u32[]{:S(2)}) collective-permute-start(bf16[80,128]{1,0:T(8,128)(2,1)} %get-tuple-element.23), channel_id=1, source_target_pairs={{0,1},{1,2},{2,3},{4,5},{5,6},{6,7},{8,9},{9,10},{10,11},{12,13},{... | collective-permute-start | bytes 61448 | tf_op jit(solution)/shard_map/ppermute | solution.py:466
  50.7 1.3 collective-permute-start.3
  53.3 0.7 copy.41.w_first_ref
  54.2 0.9 copy.45.w_two_back_ref
  55.3 0.9 copy.43.w_one_back_ref
  56.2 0.9 copy.42.w_one_ref
  57.1 0.9 copy.44.w_two_ref
  58.6 0.6 copy-done.9
  59.2 57.4 %shard_map.176 = (f32[12,32,128]{2,1,0:T(8,128)}, bf16[48,4096]{1,0:T(8,128)(2,1)}, bf16[3072,128]{1,0:T(8,128)(2,1)}) custom-call(bf16[80,4096]{1,0:T(8,128)(2,1)} %get-tuple-element.21.feed_ref, bf16[80,256]{1,0:T(8,128)(2,1)} %copy-done.7, bf16[80,256]{1,0:T(8,128)(2,1)} %copy-done.6, bf16[80,128]{1,0:T(8,128)(2,1)} %copy-done.8, ...), custom_call_target="tpu_custom_call" | custom-call | tf_op jit(solution)/shard_map/pallas_call | solution.py:302
  116.7 6.5 %shard_map.177 = bf16[16,38,128]{2,1,0:T(8,128)(2,1)} custom-call(s32[8]{0:T(128)} %get-tuple-element.19.place_ref, bf16[48,4096]{1,0:T(8,128)(2,1)} %get-tuple-element.26.dcond_ref, bf16[8,128,4096]{2,1,0:T(8,128)(2,1)} %bitcast.31), custom_call_target="tpu_custom_call" | custom-call | tf_op jit(solution)/shard_map/pallas_call | solution.py:354
  123.1 9.8 %all_to_all.34.returned_ref = bf16[16,38,128]{2,1,0:T(8,128)(2,1)} all-to-all(bf16[16,38,128]{2,1,0:T(8,128)(2,1)} %shard_map.177), channel_id=1, replica_groups=mesh['tile'=32,'band'=4] {'band'}, dimensions={0} | all-to-all | bytes 311296 | tf_op jit(solution)/shard_map/all_to_all | solution.py:554
  133.0 9.6 %all-to-all-start.4 = ((bf16[128,24,128]{2,1,0:T(8,128)(2,1)}), bf16[128,24,128]{2,1,0:T(8,128)(2,1)S(1)}, u32[]{:S(2)}, u32[]{:S(2)}) async-start(bf16[128,24,128]{2,1,0:T(8,128)(2,1)} %bitcast.15), calls=%async_computation.4 | async-start | bytes 1572864 | tf_op jit(solution)/shard_map/all_to_all | solution.py:550
  142.6 2.1 %shard_map.178 = bf16[64,38,128]{2,1,0:T(8,128)(2,1)} custom-call(s32[16]{0:T(128)} %reshape.51.asked_ref, bf16[16,38,128]{2,1,0:T(8,128)(2,1)} %all_to_all.34.returned_ref), custom_call_target="tpu_custom_call" | custom-call | tf_op jit(solution)/shard_map/pallas_call | solution.py:383
  144.6 14.6 %all-to-all-done.4.parts_ref = bf16[128,24,128]{2,1,0:T(8,128)(2,1)S(1)} async-done(((bf16[128,24,128]{2,1,0:T(8,128)(2,1)}), bf16[128,24,128]{2,1,0:T(8,128)(2,1)S(1)}, u32[]{:S(2)}, u32[]{:S(2)}) %all-to-all-start.4) | async-done | bytes 786464 | tf_op jit(solution)/shard_map/all_to_all | solution.py:550
  159.2 3.9 %all-to-all-start.3 = ((bf16[64,38,128]{2,1,0:T(8,128)(2,1)}), bf16[64,38,128]{2,1,0:T(8,128)(2,1)S(1)}, u32[]{:S(2)}, u32[]{:S(2)}) async-start(bf16[64,38,128]{2,1,0:T(8,128)(2,1)} %shard_map.178), calls=%async_computation.3 | async-start | bytes 1310720 | tf_op jit(solution)/shard_map/all_to_all | solution.py:557
  163.2 2.2 %shard_map.180 = bf16[128,24,128]{2,1,0:T(8,128)(2,1)} custom-call(bf16[128,24,128]{2,1,0:T(8,128)(2,1)} %copy-done), custom_call_target="tpu_custom_call" | custom-call | tf_op jit(solution)/shard_map/pallas_call | solution.py:418
  165.4 10.8 %all-to-all-done.3 = bf16[64,38,128]{2,1,0:T(8,128)(2,1)S(1)} async-done(((bf16[64,38,128]{2,1,0:T(8,128)(2,1)}), bf16[64,38,128]{2,1,0:T(8,128)(2,1)S(1)}, u32[]{:S(2)}, u32[]{:S(2)}) %all-to-all-start.3) | async-done | bytes 622624 | tf_op jit(solution)/shard_map/all_to_all | solution.py:557
  176.2 4.0 %all-to-all-start.5 = ((bf16[128,24,128]{2,1,0:T(8,128)(2,1)}), bf16[128,24,128]{2,1,0:T(8,128)(2,1)S(1)}, u32[]{:S(2)}, u32[]{:S(2)}) async-start(bf16[128,24,128]{2,1,0:T(8,128)(2,1)} %shard_map.180), calls=%async_computation.5 | async-start | bytes 1572864 | tf_op jit(solution)/shard_map/all_to_all | solution.py:555
  180.2 1.8 shard_map.179
  182.0 1.4 copy.46
  183.4 13.5 %all-to-all-done.5 = bf16[128,24,128]{2,1,0:T(8,128)(2,1)S(1)} async-done(((bf16[128,24,128]{2,1,0:T(8,128)(2,1)}), bf16[128,24,128]{2,1,0:T(8,128)(2,1)S(1)}, u32[]{:S(2)}, u32[]{:S(2)}) %all-to-all-start.5) | async-done | bytes 786464 | tf_op jit(solution)/shard_map/all_to_all | solution.py:555
  197.0 0.9 copy-done.1
  197.9 2.3 %shard_map.181 = (f32[128,50]{1,0:T(8,128)}, f32[3,3,128,128]{3,2,1,0:T(8,128)}, f32[3,3,128,128]{3,2,1,0:T(8,128)}, f32[12,128]{1,0:T(8,128)}) custom-call(bf16[3072,128]{1,0:T(8,128)(2,1)} %bitcast.32), custom_call_target="tpu_custom_call" | custom-call | tf_op jit(solution)/shard_map/pallas_call | solution.py:448
  200.1 1.5 copy.47
  (34 shorter events, 3.0 us)
Async XLA Ops:
  0.6 51.4 %copy-start.10 = (bf16[12,128]{1,0:T(8,128)(2,1)S(1)}, bf16[12,128]{1,0:T(8,128)(2,1)}, u32[]{:S(2)}) copy-start(bf16[12,128]{1,0:T(8,128)(2,1)} %param.22) | copy-start | bytes 9220
  0.6 53.4 %copy-start.3 = (bf16[3,3,128,128]{3,2,1,0:T(8,128)(2,1)S(1)}, bf16[3,3,128,128]{3,2,1,0:T(8,128)(2,1)}, u32[]{:S(2)}) copy-start(bf16[3,3,128,128]{3,2,1,0:T(8,128)(2,1)} %param.21) | copy-start | bytes 884740
  0.7 54.5 %copy-start.4 = (bf16[3,3,128,128]{3,2,1,0:T(8,128)(2,1)S(1)}, bf16[3,3,128,128]{3,2,1,0:T(8,128)(2,1)}, u32[]{:S(2)}) copy-start(bf16[3,3,128,128]{3,2,1,0:T(8,128)(2,1)} %param.20) | copy-start | bytes 884740
  3.4 13.9 %all-to-all-start = ((s32[4,1,4]{2,1,0:T(1,128)}), s32[4,1,4]{2,1,0:T(1,128)S(1)}, u32[]{:S(2)}, u32[]{:S(2)}) async-start(s32[4,1,4]{2,1,0:T(1,128)} %bitcast.1), calls=%async_computation | async-start | bytes 4096 | tf_op jit(solution)/shard_map/all_to_all | solution.py:500
  20.9 9.2 %all-to-all-start.1 = ((bf16[16,38,128]{2,1,0:T(8,128)(2,1)}), bf16[16,38,128]{2,1,0:T(8,128)(2,1)S(1)}, u32[]{:S(2)}, u32[]{:S(2)}) async-start(bf16[16,38,128]{2,1,0:T(8,128)(2,1)} %shard_map.173), calls=%async_computation.1 | async-start | bytes 327680 | tf_op jit(solution)/shard_map/all_to_all | solution.py:504
  30.2 0.7 copy-start.5
  37.6 7.6 %collective-permute-start.1 = (bf16[80,256]{1,0:T(8,128)(2,1)S(1)}, bf16[80,256]{1,0:T(8,128)(2,1)S(1)}, u32[]{:S(2)}, u32[]{:S(2)}) collective-permute-start(bf16[80,256]{1,0:T(8,128)(2,1)S(1)} %get-tuple-element.50), channel_id=1, source_target_pairs={{4,0},{8,4},{12,8},{16,12},{20,16},{24,20},{28,24},{32,28},{36,32}... | collective-permute-start | bytes 122888 | tf_op jit(solution)/shard_map/ppermute | solution.py:466
  42.2 4.1 %collective-permute-start = (bf16[80,256]{1,0:T(8,128)(2,1)S(1)}, bf16[80,256]{1,0:T(8,128)(2,1)S(1)}, u32[]{:S(2)}, u32[]{:S(2)}) collective-permute-start(bf16[80,256]{1,0:T(8,128)(2,1)S(1)} %get-tuple-element.51), channel_id=1, source_target_pairs={{0,4},{4,8},{8,12},{12,16},{16,20},{20,24},{24,28},{28,32},{32,36}... | collective-permute-start | bytes 122888 | tf_op jit(solution)/shard_map/ppermute | solution.py:466
  45.2 1.1 copy-start.6
  46.3 0.6 copy-start.7
  48.6 9.5 %collective-permute-start.2 = (bf16[80,128]{1,0:T(8,128)(2,1)}, bf16[80,128]{1,0:T(8,128)(2,1)S(1)}, u32[]{:S(2)}, u32[]{:S(2)}) collective-permute-start(bf16[80,128]{1,0:T(8,128)(2,1)} %get-tuple-element.23), channel_id=1, source_target_pairs={{0,1},{1,2},{2,3},{4,5},{5,6},{6,7},{8,9},{9,10},{10,11},{12,13},{... | collective-permute-start | bytes 61448 | tf_op jit(solution)/shard_map/ppermute | solution.py:466
  50.7 7.3 %collective-permute-start.3 = (bf16[80,128]{1,0:T(8,128)(2,1)}, bf16[80,128]{1,0:T(8,128)(2,1)S(1)}, u32[]{:S(2)}, u32[]{:S(2)}) collective-permute-start(bf16[80,128]{1,0:T(8,128)(2,1)} %get-tuple-element.24), channel_id=1, source_target_pairs={{1,0},{2,1},{3,2},{5,4},{6,5},{7,6},{9,8},{10,9},{11,10},{13,12},{... | collective-permute-start | bytes 61448 | tf_op jit(solution)/shard_map/ppermute | solution.py:466
  58.0 0.6 copy-start.8
  58.6 0.6 copy-start.9
  133.0 26.3 %all-to-all-start.4 = ((bf16[128,24,128]{2,1,0:T(8,128)(2,1)}), bf16[128,24,128]{2,1,0:T(8,128)(2,1)S(1)}, u32[]{:S(2)}, u32[]{:S(2)}) async-start(bf16[128,24,128]{2,1,0:T(8,128)(2,1)} %bitcast.15), calls=%async_computation.4 | async-start | bytes 1572864 | tf_op jit(solution)/shard_map/all_to_all | solution.py:550
  159.2 4.0 %copy-start = (bf16[128,24,128]{2,1,0:T(8,128)(2,1)}, bf16[128,24,128]{2,1,0:T(8,128)(2,1)S(1)}, u32[]{:S(2)}) copy-start(bf16[128,24,128]{2,1,0:T(8,128)(2,1)S(1)} %all-to-all-done.4.parts_ref) | copy-start | bytes 2359300
  159.2 17.0 %all-to-all-start.3 = ((bf16[64,38,128]{2,1,0:T(8,128)(2,1)}), bf16[64,38,128]{2,1,0:T(8,128)(2,1)S(1)}, u32[]{:S(2)}, u32[]{:S(2)}) async-start(bf16[64,38,128]{2,1,0:T(8,128)(2,1)} %shard_map.178), calls=%async_computation.3 | async-start | bytes 1310720 | tf_op jit(solution)/shard_map/all_to_all | solution.py:557
  176.2 4.0 %copy-start.2 = (bf16[64,38,128]{2,1,0:T(8,128)(2,1)}, bf16[64,38,128]{2,1,0:T(8,128)(2,1)S(1)}, u32[]{:S(2)}) copy-start(bf16[64,38,128]{2,1,0:T(8,128)(2,1)S(1)} %all-to-all-done.3) | copy-start | bytes 1867780
  176.2 20.8 %all-to-all-start.5 = ((bf16[128,24,128]{2,1,0:T(8,128)(2,1)}), bf16[128,24,128]{2,1,0:T(8,128)(2,1)S(1)}, u32[]{:S(2)}, u32[]{:S(2)}) async-start(bf16[128,24,128]{2,1,0:T(8,128)(2,1)} %shard_map.180), calls=%async_computation.5 | async-start | bytes 1572864 | tf_op jit(solution)/shard_map/all_to_all | solution.py:555
  197.0 0.9 copy-start.1

commit v2 on v1

v2 whole, which is shorter than its diff:
```python
import functools
import math

import jax
import jax.numpy as jnp
from jax import lax
from jax.experimental import pallas as pl
from jax.experimental.pallas import tpu as pltpu
from jax.sharding import PartitionSpec as P

MOST = 4
ALL = ("tile", "band")

FEED = 80
NOISY_AT = 48
GRAD_AT = 60
WIDE = 48
SUMS = 2560
OUT_AT = 80
LOW, HIGH = 40, 112
CHUNK = 24
NT = (((1,), (1,)), ((), ()))


def f32dot(left, right):
    return jnp.dot(left, right, preferred_element_type=jnp.float32)


def vmem(limit=56 * 1024 * 1024):
    return pltpu.CompilerParams(vmem_limit_bytes=limit)


def whole():
    return pl.BlockSpec(memory_space=pltpu.VMEM)


def scalars():
    return pl.BlockSpec(memory_space=pltpu.SMEM)


def plan_kernel(band_ref, slot_ref, place_ref, wanted_ref):
    count = slot_ref.shape[0]
    for i in range(wanted_ref.shape[0]):
        wanted_ref[i] = jnp.int32(-1)
    for j in range(count):
        band = band_ref[j]
        rank = jnp.int32(0)
        for i in range(j):
            rank = rank + jnp.where(band_ref[i] == band, 1, 0)
        place = band * MOST + rank
        place_ref[j] = place
        wanted_ref[place] = slot_ref[j]


def plan(bands, slots, total):
    return pl.pallas_call(
        plan_kernel,
        out_shape=(
            jax.ShapeDtypeStruct(slots.shape, jnp.int32),
            jax.ShapeDtypeStruct((total,), jnp.int32),
        ),
        in_specs=[scalars(), scalars()],
        out_specs=(scalars(), scalars()),
    )(bands, slots)


def serve_kernel(asked_ref, coarse_ref, out_ref):
    for i in range(out_ref.shape[0]):
        out_ref[i] = coarse_ref[jnp.maximum(asked_ref[i], 0)]


def serve(asked, coarse):
    return pl.pallas_call(
        serve_kernel,
        out_shape=jax.ShapeDtypeStruct((asked.shape[0],) + coarse.shape[1:], coarse.dtype),
        in_specs=[scalars(), whole()],
        out_specs=whole(),
        compiler_params=vmem(),
    )(asked, coarse)


def feed_kernel(place_ref, arrived_ref, interp_ref, given_ref, feed_ref, edge_ref, picked):
    step = pl.program_id(0)
    ch = arrived_ref.shape[1]
    count = interp_ref.shape[0]
    cells = interp_ref.shape[1]
    lanes = interp_ref.shape[2]

    @pl.when(step == 0)
    def _():
        edge_ref[...] = jnp.zeros_like(edge_ref)
        for j in range(count):
            picked[:, j * cells : (j + 1) * cells] = arrived_ref[place_ref[j]]

    matrix = interp_ref[...].reshape(count * cells, lanes)
    cond = f32dot(picked[...], matrix).astype(jnp.bfloat16)
    feed_ref[...] = jnp.zeros_like(feed_ref)
    feed_ref[0:ch, :] = cond
    feed_ref[NOISY_AT:, :] = given_ref[...]
    rows = lanes // 128
    at = lax.broadcasted_iota(jnp.int32, (lanes, 256), 0)
    lane = lax.broadcasted_iota(jnp.int32, (lanes, 256), 1)
    row = jnp.bitwise_and(lane, 63) - 2 - step * rows
    kind = jnp.right_shift(lane, 6)
    col = kind + jnp.where(kind >= 2, 124, 0)
    hit = jnp.where(row * 128 + col == at, 1.0, 0.0).astype(jnp.bfloat16)
    edge_ref[...] += f32dot(feed_ref[...], hit).astype(jnp.bfloat16)


def make_feed(place, arrived, interp, given, blocks=4):
    count, cells, n = interp.shape
    ch = arrived.shape[1]
    lanes = n // blocks
    return pl.pallas_call(
        feed_kernel,
        grid=(blocks,),
        out_shape=(
            jax.ShapeDtypeStruct((FEED, n), jnp.bfloat16),
            jax.ShapeDtypeStruct((FEED, 256), jnp.bfloat16),
        ),
        in_specs=[
            scalars(),
            whole(),
            pl.BlockSpec((count, cells, lanes), lambda i: (0, 0, i)),
            pl.BlockSpec((FEED - NOISY_AT, lanes), lambda i: (0, i)),
        ],
        out_specs=(
            pl.BlockSpec((FEED, lanes), lambda i: (0, i)),
            pl.BlockSpec((FEED, 256), lambda i: (0, 0)),
        ),
        scratch_shapes=[pltpu.VMEM((ch, count * cells), jnp.bfloat16)],
        compiler_params=vmem(),
    )(place, arrived, interp, given)


def strip_kernel(top_ref, bot_ref, edge_ref, left_ref, right_ref, own_ref):
    wide = jnp.concatenate([top_ref[...], bot_ref[...]], axis=1)
    at = lax.broadcasted_iota(jnp.int32, (512, 256), 0)
    lane = lax.broadcasted_iota(jnp.int32, (512, 256), 1)
    spot = jnp.bitwise_and(lane, 63)
    row = jnp.where(spot < 2, spot, jnp.where(jnp.logical_or(spot == 34, spot == 35), spot - 32, 8))
    kind = jnp.right_shift(lane, 6)
    col = kind + jnp.where(kind >= 2, 124, 0)
    hit = jnp.where(row * 128 + col == at, 1.0, 0.0).astype(jnp.bfloat16)
    edge = (edge_ref[...].astype(jnp.float32) + f32dot(wide, hit)).astype(jnp.bfloat16)
    left_ref[...] = edge[:, 0:128]
    right_ref[...] = edge[:, 128:256]
    own_ref[...] = jnp.concatenate([edge[:, 0:64], edge[:, 192:256]], axis=1)


def strips(top, bot, edge):
    shape = jax.ShapeDtypeStruct((FEED, 128), jnp.bfloat16)
    return pl.pallas_call(
        strip_kernel,
        out_shape=(shape,) * 3,
        in_specs=[whole()] * 3,
        out_specs=(whole(),) * 3,
        compiler_params=vmem(),
    )(top, bot, edge)


def silu_parts(value):
    sig = jax.nn.sigmoid(value)
    return value * sig, sig * (1.0 + value * (1.0 - sig))


def net_kernel(
    place_ref,
    flag_ref,
    feed_ref,
    top_ref,
    bot_ref,
    left_ref,
    right_ref,
    own_ref,
    w_first_ref,
    w_one_ref,
    w_one_back_ref,
    w_two_ref,
    w_two_back_ref,
    w_out_ref,
    w_cond_ref,
    interp_ref,
    pred_ref,
    pack_ref,
    x_ref,
    a_zero_ref,
    d_two_ref,
    a_one_ref,
    d_one_ref,
    slope_ref,
    sum_one_ref,
    sum_two_ref,
    dcond_ref,
    matrix_ref,
    sem,
):
    rows = pred_ref.shape[1]
    tall = rows + 4
    ch = 128
    bf, f32 = jnp.bfloat16, jnp.float32
    fetch = pltpu.make_async_copy(interp_ref, matrix_ref, sem)
    fetch.start()
    lane = lax.broadcasted_iota(jnp.int32, (ch, 128), 1)
    at_left = lane == 0
    at_right = lane == 127

    def put(ref, row, value, edge, edge_row):
        lanes = slice(row * 128, (row + 1) * 128)
        value = value.astype(f32)
        left = pltpu.roll(edge, (128 - edge_row) % 128, 1)
        right = pltpu.roll(edge, 63 - edge_row, 1)
        ref[0:ch, lanes] = jnp.where(at_left, left, pltpu.roll(value, 1, 1)).astype(bf)
        ref[ch : 2 * ch, lanes] = value.astype(bf)
        ref[2 * ch :, lanes] = jnp.where(at_right, right, pltpu.roll(value, 127, 1)).astype(bf)

    def around(ref, row, count):
        return jnp.concatenate(
            [ref[:, (row + p) * 128 : (row + p + count) * 128] for p in range(3)], axis=0
        )

    left, right, own = left_ref[...], right_ref[...], own_ref[...]
    groups = (
        jnp.concatenate([left[:, 0:64], own[:, 64:128]], axis=1),
        jnp.concatenate([left[:, 64:128], right[:, 0:64]], axis=1),
        jnp.concatenate([own[:, 0:64], right[:, 64:128]], axis=1),
    )
    edge_x = jnp.concatenate(groups, axis=1)
    both = f32dot(w_first_ref[...], edge_x)
    edge_a = silu_parts(both[0:ch])[0].astype(bf).astype(f32)
    edge_d = both[ch:].astype(bf).astype(f32)

    def edge_taps(field):
        pieces = []
        for p in range(3):
            for q in range(3):
                part = field[:, q * 128 : (q + 1) * 128]
                pieces.append(part if p == 1 else pltpu.roll(part, (1 - p) % 128, 1))
        return jnp.concatenate(pieces, axis=0).astype(bf)

    spot = jnp.bitwise_and(lane, 63)
    edge_in = jnp.where(lane >= 64, flag_ref[3], flag_ref[2])
    edge_in = edge_in * jnp.where(spot == 1, flag_ref[0], 1.0)
    edge_in = edge_in * jnp.where(spot == rows + 2, flag_ref[1], 1.0)
    edge_act, edge_slope = silu_parts(f32dot(w_one_ref[...], edge_taps(edge_a)))
    edge_a_one = (edge_act * edge_in).astype(bf).astype(f32)
    edge_back = f32dot(w_two_back_ref[...], edge_taps(edge_d))
    edge_d_one = (edge_back * edge_slope * edge_in).astype(bf).astype(f32)
    edge_a = edge_a[:, 128:256]
    edge_d = edge_d[:, 128:256]

    x_ref[:, 0:256] = top_ref[...]
    x_ref[:, 256 : (rows + 2) * 128] = feed_ref[...]
    x_ref[:, (rows + 2) * 128 :] = bot_ref[...]
    for row in range(0, tall, 4):
        both = f32dot(w_first_ref[...], x_ref[:, row * 128 : (row + 4) * 128])
        act, slope = silu_parts(both[0:ch])
        slope_ref[:, row * 128 : (row + 4) * 128] = slope
        for k in range(4):
            lanes = slice(k * 128, (k + 1) * 128)
            put(a_zero_ref, row + k, act[:, lanes], edge_a, row + k)
            put(d_two_ref, row + k, both[ch:, lanes], edge_d, row + k)

    half = (rows + 2) // 2
    for row in (0, half):
        act, slope = silu_parts(f32dot(w_one_ref[...], around(a_zero_ref, row, half)))
        back = f32dot(w_two_back_ref[...], around(d_two_ref, row, half)) * slope
        for k in range(half):
            lanes = slice(k * 128, (k + 1) * 128)
            act_row, back_row = act[:, lanes], back[:, lanes]
            if row + k == 0:
                act_row, back_row = act_row * flag_ref[0], back_row * flag_ref[0]
            if row + k == rows + 1:
                act_row, back_row = act_row * flag_ref[1], back_row * flag_ref[1]
            put(a_one_ref, row + k, act_row, edge_a_one, row + k + 1)
            put(d_one_ref, row + k, back_row, edge_d_one, row + k + 1)

    half = rows // 2
    sum_in = jnp.zeros((ch, FEED), f32)
    sum_out = jnp.zeros((ch, FEED - NOISY_AT), f32)
    for row in (0, half):
        mine = slice((row + 2) * 128, (row + 2 + half) * 128)
        inner = slice((row + 1) * 128, (row + 1 + half) * 128)
        x = x_ref[:, mine]
        d_two = d_two_ref[ch : 2 * ch, mine]
        cols_one = around(a_one_ref, row, half)
        z_two = f32dot(w_two_ref[...], cols_one)
        a_two = (a_zero_ref[ch : 2 * ch, mine].astype(f32) + z_two).astype(bf)
        pred = f32dot(w_out_ref[...], a_two)
        for k in range(half):
            pred_ref[:, row + k, :] = pred[0 : pred_ref.shape[0], k * 128 : (k + 1) * 128]
        sum_out = sum_out + nt_dot(a_two, x[NOISY_AT:, :])
        part_two = nt_dot(d_two, cols_one)
        back = f32dot(w_one_back_ref[...], around(d_one_ref, row, half))
        d_zero = ((back + d_two.astype(f32)) * slope_ref[:, mine]).astype(bf)
        sum_in = sum_in + nt_dot(d_zero, x)
        dcond_ref[:, row * 128 : (row + half) * 128] = f32dot(w_cond_ref[...], d_zero).astype(bf)
        part_one = nt_dot(d_one_ref[ch : 2 * ch, inner], around(a_zero_ref, row + 1, half))
        if row == 0:
            sum_two_ref[...] = part_two
            sum_one_ref[...] = part_one
        else:
            sum_two_ref[...] += part_two
            sum_one_ref[...] += part_one

    bands = pack_ref.shape[0]
    share_rows = SUMS // bands

    def store(first, value):
        done = 0
        while done < value.shape[0]:
            band, spot = divmod(first + done, share_rows)
            count = min(value.shape[0] - done, share_rows - spot)
            pack_ref[band, spot : spot + count, :] = value[done : done + count, :]
            done += count

    for tap in range(9):
        lanes = slice(tap * 128, (tap + 1) * 128)
        store(tap * ch, sum_two_ref[:, lanes].astype(bf))
        store((9 + tap) * ch, sum_one_ref[:, lanes].astype(bf))
    pad = jnp.zeros((ch, 128 - OUT_AT - (FEED - NOISY_AT)), f32)
    store(18 * ch, jnp.concatenate([sum_in, sum_out, pad], axis=1).astype(bf))
    store(19 * ch, jnp.zeros((ch, 128), bf))
    for band in range(bands):
        pack_ref[band, share_rows:, :] = jnp.zeros((MOST * WIDE, 128), bf)
    fetch.wait()
    count, cells, n = matrix_ref.shape
    blocks = nt_dot(dcond_ref[...], matrix_ref[...].reshape(count * cells, n)).astype(bf)
    for j in range(count):
        place = place_ref[j]
        spot = share_rows + jnp.bitwise_and(place, MOST - 1) * WIDE
        pack_ref[jnp.right_shift(place, 2), pl.ds(pl.multiple_of(spot, 16), WIDE), :] = blocks[
            :, j * cells : (j + 1) * cells
        ]


def nt_dot(left, right):
    return lax.dot_general(left, right, NT, preferred_element_type=jnp.float32)


def net(chans, rows, cols, n_band, args):
    ch = 128
    bf, f32 = jnp.bfloat16, jnp.float32
    tall = (rows + 4) * cols
    inner = (rows + 2) * cols
    interp = args[-1]
    return pl.pallas_call(
        net_kernel,
        out_shape=(
            jax.ShapeDtypeStruct((chans, rows, cols), f32),
            jax.ShapeDtypeStruct((n_band, SUMS // n_band + MOST * WIDE, 128), bf),
        ),
        in_specs=[scalars(), scalars()]
        + [whole()] * (len(args) - 3)
        + [pl.BlockSpec(memory_space=pl.ANY)],
        out_specs=(whole(),) * 2,
        scratch_shapes=[
            pltpu.VMEM((FEED, tall), bf),
            pltpu.VMEM((3 * ch, tall), bf),
            pltpu.VMEM((3 * ch, tall), bf),
            pltpu.VMEM((3 * ch, inner), bf),
            pltpu.VMEM((3 * ch, inner), bf),
            pltpu.VMEM((ch, tall), f32),
            pltpu.VMEM((ch, 9 * ch), f32),
            pltpu.VMEM((ch, 9 * ch), f32),
            pltpu.VMEM((WIDE, rows * cols), bf),
            pltpu.VMEM(interp.shape, bf),
            pltpu.SemaphoreType.DMA(()),
        ],
        compiler_params=vmem(),
    )(*args)


def merge_kernel(asked_ref, parts_ref, out_ref, total, weights):
    bands = parts_ref.shape[0]
    dests = out_ref.shape[0]
    share_rows = weights.shape[0]
    f32 = jnp.float32
    total[...] = jnp.zeros_like(total)
    whole_sum = parts_ref[0, 0:share_rows, :].astype(f32)
    for band in range(1, bands):
        whole_sum = whole_sum + parts_ref[band, 0:share_rows, :].astype(f32)
    weights[...] = whole_sum
    each = share_rows // dests
    for dest in range(dests):
        total[dest, 2 * LOW : 2 * LOW + each, :] = weights[dest * each : (dest + 1) * each, :]
    for i in range(bands * MOST):
        slot = asked_ref[i]
        start = share_rows + (i % MOST) * WIDE
        block = parts_ref[i // MOST, start : start + WIDE, :].astype(f32)[0:LOW]

        @pl.when(slot >= 0)
        def _(slot=slot, block=block):
            spot = pl.ds(pl.multiple_of(jnp.bitwise_and(slot, 1) * LOW, 8), LOW)
            total[jnp.right_shift(slot, 1), spot, :] += block

    out_ref[...] = total[...].astype(jnp.bfloat16)


def merge(asked, parts, dests):
    return pl.pallas_call(
        merge_kernel,
        out_shape=jax.ShapeDtypeStruct((dests, HIGH, 128), jnp.bfloat16),
        in_specs=[scalars(), whole()],
        out_specs=whole(),
        scratch_shapes=[
            pltpu.VMEM((dests, HIGH, 128), jnp.float32),
            pltpu.VMEM((SUMS // parts.shape[0], 128), jnp.float32),
        ],
        compiler_params=vmem(),
    )(asked, parts)


def share_kernel(parts_ref, block_ref, out_ref, total):
    value = parts_ref[0].astype(jnp.float32)
    for i in range(1, parts_ref.shape[0]):
        value = value + parts_ref[i].astype(jnp.float32)
    total[...] = value
    ch = block_ref.shape[2]
    for k in range(block_ref.shape[1]):
        block_ref[0, k] = total[k * LOW : k * LOW + ch, :]
    chunk = total[2 * LOW : 2 * LOW + CHUNK, :].astype(jnp.bfloat16)
    out_ref[...] = jnp.broadcast_to(chunk[None], out_ref.shape)


def share(parts, block_shape, devices):
    return pl.pallas_call(
        share_kernel,
        out_shape=(
            jax.ShapeDtypeStruct(block_shape, jnp.float32),
            jax.ShapeDtypeStruct((devices, CHUNK, 128), jnp.bfloat16),
        ),
        in_specs=[whole()],
        out_specs=(whole(), whole()),
        scratch_shapes=[pltpu.VMEM((HIGH, 128), jnp.float32)],
        compiler_params=vmem(),
    )(parts)


def final_kernel(factor, n_band, parts_ref, in_ref, one_ref, two_ref, out_ref, total):
    ch = in_ref.shape[0]
    side = two_ref.shape[0]
    devices = parts_ref.shape[0]
    each = SUMS // devices
    for device in range(devices):
        tile, band = divmod(device, n_band)
        first = (band * (devices // n_band) + tile) * each
        total[first : first + each, :] = parts_ref[device].astype(jnp.float32)[0:each] * factor
    for tap in range(9):
        two_ref[tap // side, tap % side] = total[tap * ch : (tap + 1) * ch, :]
        one_ref[tap // side, tap % side] = total[(9 + tap) * ch : (10 + tap) * ch, :]
    last = total[18 * ch : 19 * ch, :]
    chans = out_ref.shape[0]
    coarse_ch = in_ref.shape[1] - chans
    in_ref[:, 0:coarse_ch] = last[:, 0:coarse_ch]
    in_ref[:, coarse_ch:] = last[:, NOISY_AT : NOISY_AT + chans]
    start = OUT_AT + GRAD_AT - NOISY_AT
    out_ref[...] = last.T[start : start + chans, :]


def final(parts, n_band, width, taps, inner, chans, factor):
    f32 = jnp.float32
    return pl.pallas_call(
        functools.partial(final_kernel, factor, n_band),
        out_shape=(
            jax.ShapeDtypeStruct((width, inner), f32),
            jax.ShapeDtypeStruct(taps, f32),
            jax.ShapeDtypeStruct(taps, f32),
            jax.ShapeDtypeStruct((chans, width), f32),
        ),
        in_specs=[whole()],
        out_specs=(whole(),) * 4,
        scratch_shapes=[pltpu.VMEM((SUMS, 128), f32)],
        compiler_params=vmem(),
    )(parts)


def halo(first, last, axis):
    count = lax.axis_size(axis)
    up = [(i, i + 1) for i in range(count - 1)]
    down = [(i + 1, i) for i in range(count - 1)]
    return lax.ppermute(last, axis, up), lax.ppermute(first, axis, down)


def per_device(
    noisy, grad_pred, coarse, margin_band, margin_slot, interp, w_in, w_conv1, w_conv2, w_out
):
    width = w_in.shape[0]
    chans, rows, cols = noisy.shape
    cells = rows * cols
    coarse_ch = coarse.shape[2]
    per_band = coarse.shape[1]
    n_band = lax.axis_size("band")
    n_tile = lax.axis_size("tile")
    slots = n_band * MOST
    local_interp = interp[0, 0]

    place, wanted = plan(margin_band.reshape(-1), margin_slot, slots)
    asked = lax.all_to_all(
        wanted.reshape(n_band, MOST), "band", split_axis=0, concat_axis=0, tiled=True
    ).reshape(slots)
    served = serve(asked, coarse[0])
    arrived = lax.all_to_all(served, "band", split_axis=0, concat_axis=0, tiled=True)

    given = jnp.concatenate(
        [
            noisy.reshape(chans, cells),
            grad_pred.reshape(chans, cells),
            jnp.zeros((FEED - NOISY_AT - 2 * chans, cells), jnp.bfloat16),
        ],
        0,
    )
    w_pad = lambda w, before: jnp.pad(w, ((0, 0), (before, FEED - before - w.shape[1])))
    w_first = jnp.concatenate(
        [
            w_pad(w_in[:, :coarse_ch], 0) + w_pad(w_in[:, coarse_ch:], NOISY_AT),
            w_pad(w_out.T, GRAD_AT),
        ],
        0,
    )
    forward = lambda w: w.transpose(2, 0, 1, 3).reshape(width, 9 * width)
    backward = lambda w: w[::-1, ::-1].transpose(3, 0, 1, 2).reshape(width, 9 * width)
    weights = (
        w_first,
        forward(w_conv1),
        backward(w_conv1),
        forward(w_conv2),
        backward(w_conv2),
        jnp.pad(w_out, ((0, 16 - chans), (0, 0))),
        jnp.pad(w_in[:, :coarse_ch].T, ((0, WIDE - coarse_ch), (0, 0))),
    )
    tile, band = lax.axis_index("tile"), lax.axis_index("band")
    flags = jnp.stack([tile > 0, tile < n_tile - 1, band > 0, band < n_band - 1])
    flags = flags.astype(jnp.float32)
    arrived, weights = lax.optimization_barrier((arrived, weights))

    feed, edge = make_feed(place, arrived, local_interp, given)
    top, bot = halo(feed[:, : 2 * cols], feed[:, cells - 2 * cols :], "tile")
    left_out, right_out, own = strips(top, bot, edge)
    left, right = halo(left_out, right_out, "band")
    pred, pack = net(
        chans,
        rows,
        cols,
        n_band,
        (place, flags, feed, top, bot, left, right, own) + weights + (local_interp,),
    )
    pack = lax.all_to_all(pack, "band", split_axis=0, concat_axis=0, tiled=True)
    parts = lax.all_to_all(
        merge(asked, pack, n_tile), "tile", split_axis=0, concat_axis=0, tiled=True
    )
    coarse_grad, sums = share(
        parts, (1, per_band // n_tile) + coarse.shape[2:], n_tile * n_band
    )
    sums = lax.all_to_all(sums, ALL, split_axis=0, concat_axis=0, tiled=True)
    factor = 1.0 / math.sqrt(cells * n_tile * n_band)
    grad_in, grad_one, grad_two, grad_out = final(
        sums, n_band, width, w_conv1.shape, w_in.shape[1], chans, factor
    )
    return (pred, coarse_grad, grad_in, grad_one, grad_two, grad_out)


def solution(mesh):
    placed = (
        P(None, "tile", "band"),
        P(None, "tile", "band"),
        P("band", None, None, None),
        P(("tile", "band"), None),
        P(("tile", "band")),
        P("tile", "band", None, None, None),
        P(),
        P(),
        P(),
        P(),
    )
    return jax.shard_map(
        per_device,
        mesh=mesh,
        in_specs=placed,
        out_specs=(P(None, "tile", "band"), P("band", "tile", None, None), P(), P(), P(), P()),
        check_vma=False,
    )
```

time: 203 us -> 152 us (0.75)
  Pallas kernels: 83 us -> 37.8 us
  blocking collectives: 9.82 us -> 42.6 us
  waiting for transfers between devices: 44.3 us -> 16.4 us
  starting transfers between devices: 38.7 us -> 25.4 us
  local copies, waits for them, and re-layouts: 21.3 us -> 25.3 us
    pallas_call x1, Pallas kernels: 57.4 us -> 19.9 us  [net(): pl.pallas_call(net_kernel, out_shape=(jax.ShapeDtypeStruct((chans, rows,...]
    all_to_all x1 -> x2, blocking collectives: 9.82 us -> 42.6 us  [the longest x1 24.4 us: per_device(): lax.all_to_all(merge(asked, pack, n_tile), 'tile', split_axis=0, concat_a...]
    all_to_all x3 -> x1, waiting for transfers between devices: 38.9 us -> 15.4 us  [per_device(): sums = lax.all_to_all(sums, ALL, split_axis=0, concat_axis=0, tiled=True)]
    all_to_all x3 -> x1, starting transfers between devices: 17.6 us -> 3.81 us  [per_device(): sums = lax.all_to_all(sums, ALL, split_axis=0, concat_axis=0, tiled=True)]
    pallas_call x6 -> x4, Pallas kernels: 16.5 us -> 8.67 us  [the longest x1 2.54 us: merge(): pl.pallas_call(merge_kernel, out_shape=jax.ShapeDtypeStruct((dests, HIGH,...]
    optimization_barrier x0 -> x5, local copies, waits for them, and re-layouts: none -> 4.3 us  [per_device(): arrived, weights = lax.optimization_barrier((arrived, weights))]
    all_to_all x1, waiting for transfers between devices: 4.3 us -> 0.01 us  [per_device(): lax.all_to_all(served, 'band', split_axis=0, concat_axis=0, tiled=True)]
    reshape x4 -> x0, local copies, waits for them, and re-layouts: 3.58 us -> none  [the longest x2 1.8 us: per_device(): backward = lambda w: w.transpose(3, 0, 1, 2).reshape(width, 9 * width)]
  transfers between devices with their start and end apart: 9 -> 7, of which waited for: 5 -> 2; matrix products, arithmetic and copies ran while one was open for 8% -> 13% of each run, Pallas kernels for 3% -> 0%
where the time goes in v2:
time: 152 us; the launch traced here: 151 us
  blocking collectives  42.6 us (28%)
  Pallas kernels  37.8 us (25%)
  starting transfers between devices  25.4 us (17%)
  local copies, waits for them, and re-layouts  25.3 us (17%)
  waiting for transfers between devices  16.4 us (11%)
  other arithmetic  2.85 us (2%)
    all_to_all x1, blocking collectives, per_device(): lax.all_to_all(merge(asked, pack, n_tile), 'tile', split_axis=0, concat_a...  24.4 us
    pallas_call x1, Pallas kernels, net(): pl.pallas_call(net_kernel, out_shape=(jax.ShapeDtypeStruct((chans, rows,...  19.9 us
    all_to_all x1, blocking collectives, per_device(): pack = lax.all_to_all(pack, 'band', split_axis=0, concat_axis=0, tiled=True)  18.1 us
    all_to_all x1, waiting for transfers between devices, per_device(): sums = lax.all_to_all(sums, ALL, split_axis=0, concat_axis=0, tiled=True)  15.4 us
    unnamed x21, local copies, waits for them, and re-layouts  12.3 us
    ppermute x4, starting transfers between devices, halo(): return (lax.ppermute(last, axis, up), lax.ppermute(first, axis, down))  11.5 us
    pallas_call x1, Pallas kernels, make_feed(): pl.pallas_call(feed_kernel, grid=(blocks,), out_shape=(jax.ShapeDtypeStru...  6.13 us
    all_to_all x1, starting transfers between devices, per_device(): lax.all_to_all(wanted.reshape(n_band, MOST), 'band', split_axis=0, concat...  5.86 us
  transfers between devices with their start and end apart: 7, of which 2 were waited for; matrix products, arithmetic and copies ran while one was open for 13% of the time, Pallas kernels for 0%

profile of v2, /device:TPU:1, one launch (start us, length us, event | category | flops | bytes accessed | tf_op | source)
XLA Modules:
  0.0 151.1 jit_solution(10776249364122139867)
XLA Ops:
  0.6 1.2 shard_map.145
  1.9 1.3 all_to_all.18
  3.2 5.9 %all-to-all-start = ((s32[4,1,4]{2,1,0:T(1,128)}), s32[4,1,4]{2,1,0:T(1,128)S(1)}, u32[]{:S(2)}, u32[]{:S(2)}) async-start(s32[4,1,4]{2,1,0:T(1,128)} %bitcast.5), calls=%async_computation | async-start | bytes 4096 | tf_op jit(solution)/shard_map/all_to_all | solution.py:499
  9.1 0.7 slice.14
  9.8 0.7 slice_bitcast_fusion
  10.5 0.9 pad.35
  11.4 0.9 pad.36
  12.4 2.3 %copy.48 = bf16[1,64,38,128]{3,2,1,0:T(8,128)(2,1)} copy(bf16[1,64,38,128]{3,1,2,0:T(8,128)(2,1)} %param.12) | data formatting | bytes 1245184 | tf_op args[2]
  14.8 0.8 maximum_maximum_fusion.given_ref
  16.2 0.7 reduce.3
  16.8 0.7 reshape.42.asked_ref
  17.5 1.8 %shard_map.146 = bf16[16,38,128]{2,1,0:T(8,128)(2,1)} custom-call(s32[16]{0:T(128)} %reshape.42.asked_ref, bf16[64,38,128]{2,1,0:T(8,128)(2,1)} %bitcast.33), custom_call_target="tpu_custom_call" | custom-call | tf_op jit(solution)/shard_map/pallas_call | solution.py:73
  19.3 4.2 %all-to-all-start.1 = ((bf16[16,38,128]{2,1,0:T(8,128)(2,1)}), bf16[16,38,128]{2,1,0:T(8,128)(2,1)S(1)}, u32[]{:S(2)}, u32[]{:S(2)}) async-start(bf16[16,38,128]{2,1,0:T(8,128)(2,1)} %shard_map.146), calls=%async_computation.1 | async-start | bytes 327680 | tf_op jit(solution)/shard_map/all_to_all | solution.py:503
  23.5 1.0 rev.6
  24.5 1.2 copy.36
  25.7 1.0 rev.7
  26.7 1.2 copy.37
  27.8 1.3 pad.23.w_out_ref
  29.1 0.6 pad.24.w_cond_ref
  29.7 0.7 fusion.1
  30.4 0.7 copy-done.1
  31.1 6.1 %shard_map.147 = (bf16[80,4096]{1,0:T(8,128)(2,1)}, bf16[80,256]{1,0:T(8,128)(2,1)}) custom-call(s32[8]{0:T(128)} %get-tuple-element.29.place_ref, bf16[16,38,128]{2,1,0:T(8,128)(2,1)} %copy-done.1, bf16[8,128,4096]{2,1,0:T(8,128)(2,1)} %bitcast.31, bf16[32,4096]{1,0:T(8,128)(2,1)} %maximum_maximum_fusion.given_ref), custom_call_target="tpu_custom_call" | custom-call | tf_op jit(solution)/shard_map/pallas_call | solution.py:114
  37.2 0.8 fusion.2
  38.0 3.4 %collective-permute-start.1 = (bf16[80,256]{1,0:T(8,128)(2,1)S(1)}, bf16[80,256]{1,0:T(8,128)(2,1)S(1)}, u32[]{:S(2)}, u32[]{:S(2)}) collective-permute-start(bf16[80,256]{1,0:T(8,128)(2,1)S(1)} %get-tuple-element.70), channel_id=1, source_target_pairs={{4,0},{8,4},{12,8},{16,12},{20,16},{24,20},{28,24},{32,28},{36,32}... | collective-permute-start | bytes 122888 | tf_op jit(solution)/shard_map/ppermute | solution.py:482
  41.5 3.0 %collective-permute-start = (bf16[80,256]{1,0:T(8,128)(2,1)S(1)}, bf16[80,256]{1,0:T(8,128)(2,1)S(1)}, u32[]{:S(2)}, u32[]{:S(2)}) collective-permute-start(bf16[80,256]{1,0:T(8,128)(2,1)S(1)} %get-tuple-element.71), channel_id=1, source_target_pairs={{0,4},{4,8},{8,12},{12,16},{16,20},{20,24},{24,28},{28,32},{32,36}... | collective-permute-start | bytes 122888 | tf_op jit(solution)/shard_map/ppermute | solution.py:482
  44.5 1.0 collective-permute-done.top_ref
  45.6 0.6 copy-done.3
  46.2 1.6 %shard_map.148 = (bf16[80,128]{1,0:T(8,128)(2,1)}, bf16[80,128]{1,0:T(8,128)(2,1)}, bf16[80,128]{1,0:T(8,128)(2,1)}) custom-call(bf16[80,256]{1,0:T(8,128)(2,1)} %copy-done.3, bf16[80,256]{1,0:T(8,128)(2,1)} %copy-done.2, bf16[80,256]{1,0:T(8,128)(2,1)} %get-tuple-element.33.edge_ref), custom_call_target="tpu_custom_call" | custom-call | tf_op jit(solution)/shard_map/pallas_call | solution.py:153
  47.8 3.6 %collective-permute-start.2 = (bf16[80,128]{1,0:T(8,128)(2,1)}, bf16[80,128]{1,0:T(8,128)(2,1)S(1)}, u32[]{:S(2)}, u32[]{:S(2)}) collective-permute-start(bf16[80,128]{1,0:T(8,128)(2,1)} %get-tuple-element.34), channel_id=1, source_target_pairs={{0,1},{1,2},{2,3},{4,5},{5,6},{6,7},{8,9},{9,10},{10,11},{12,13},{... | collective-permute-start | bytes 61448 | tf_op jit(solution)/shard_map/ppermute | solution.py:482
  51.4 1.5 collective-permute-start.3
  52.9 0.7 add_convert_fusion.flag_ref
  53.6 0.7 copy.38.w_first_ref
  54.3 0.9 copy.39.w_one_ref
  55.2 0.9 copy.40.w_one_back_ref
  56.1 0.9 copy.41.w_two_ref
  57.0 0.9 copy.42.w_two_back_ref
  57.9 0.6 copy-done.4
  58.5 19.9 %shard_map.149 = (f32[12,32,128]{2,1,0:T(8,128)}, bf16[4,832,128]{2,1,0:T(8,128)(2,1)}) custom-call(s32[8]{0:T(128)} %get-tuple-element.29.place_ref, f32[4]{0:T(128)} %add_convert_fusion.flag_ref, bf16[80,4096]{1,0:T(8,128)(2,1)} %get-tuple-element.32.feed_ref, bf16[80,256]{1,0:T(8,128)(2,1)} %copy-done.3, bf16[80,256]{1,0:T(8,128)(2,1)} %copy-done.2, ...), custom_call_target="tpu_custom_call" | custom-call | tf_op jit(solution)/shard_map/pallas_call | solution.py:347
  78.5 18.1 %all_to_all.29.parts_ref = bf16[4,832,128]{2,1,0:T(8,128)(2,1)} all-to-all(bf16[4,832,128]{2,1,0:T(8,128)(2,1)} %get-tuple-element.45), channel_id=1, replica_groups=mesh['tile'=32,'band'=4] {'band'}, dimensions={0} | all-to-all | bytes 1703936 | tf_op jit(solution)/shard_map/all_to_all | solution.py:548
  96.6 2.5 %shard_map.150 = bf16[32,112,128]{2,1,0:T(8,128)(2,1)} custom-call(s32[16]{0:T(128)} %reshape.42.asked_ref, bf16[4,832,128]{2,1,0:T(8,128)(2,1)} %all_to_all.29.parts_ref), custom_call_target="tpu_custom_call" | custom-call | tf_op jit(solution)/shard_map/pallas_call | solution.py:401
  99.1 24.4 %all_to_all.30.parts_ref = bf16[32,112,128]{2,1,0:T(8,128)(2,1)} all-to-all(bf16[32,112,128]{2,1,0:T(8,128)(2,1)} %shard_map.150), channel_id=1, replica_groups=mesh['tile'=32,'band'=4] {'tile'}, dimensions={0} | all-to-all | bytes 1835008 | tf_op jit(solution)/shard_map/all_to_all | solution.py:549
  123.5 2.2 %shard_map.151 = (f32[1,2,38,128]{3,2,1,0:T(8,128)}, bf16[128,24,128]{2,1,0:T(8,128)(2,1)}) custom-call(bf16[32,112,128]{2,1,0:T(8,128)(2,1)} %all_to_all.30.parts_ref), custom_call_target="tpu_custom_call" | custom-call | tf_op jit(solution)/shard_map/pallas_call | solution.py:427
  125.8 3.8 %all-to-all-start.4 = ((bf16[128,24,128]{2,1,0:T(8,128)(2,1)}), bf16[128,24,128]{2,1,0:T(8,128)(2,1)S(1)}, u32[]{:S(2)}, u32[]{:S(2)}) async-start(bf16[128,24,128]{2,1,0:T(8,128)(2,1)} %get-tuple-element.47), calls=%async_computation.4 | async-start | bytes 1572864 | tf_op jit(solution)/shard_map/all_to_all | solution.py:555
  129.6 1.4 copy.43
  131.0 15.4 %all-to-all-done.4.parts_ref = bf16[128,24,128]{2,1,0:T(8,128)(2,1)S(1)} async-done(((bf16[128,24,128]{2,1,0:T(8,128)(2,1)}), bf16[128,24,128]{2,1,0:T(8,128)(2,1)S(1)}, u32[]{:S(2)}, u32[]{:S(2)}) %all-to-all-start.4) | async-done | bytes 786464 | tf_op jit(solution)/shard_map/all_to_all | solution.py:555
  146.4 0.9 copy-done
  147.3 2.3 %shard_map.152 = (f32[128,50]{1,0:T(8,128)}, f32[3,3,128,128]{3,2,1,0:T(8,128)}, f32[3,3,128,128]{3,2,1,0:T(8,128)}, f32[12,128]{1,0:T(8,128)}) custom-call(bf16[128,24,128]{2,1,0:T(8,128)(2,1)} %copy-done), custom_call_target="tpu_custom_call" | custom-call | tf_op jit(solution)/shard_map/pallas_call | solution.py:463
  149.6 1.5 %copy.44 = f32[128,50]{0,1:T(8,128)} copy(f32[128,50]{1,0:T(8,128)} %get-tuple-element.66) | data formatting | bytes 51200
  (19 shorter events, 0.7 us)
Async XLA Ops:
  3.2 12.4 %all-to-all-start = ((s32[4,1,4]{2,1,0:T(1,128)}), s32[4,1,4]{2,1,0:T(1,128)S(1)}, u32[]{:S(2)}, u32[]{:S(2)}) async-start(s32[4,1,4]{2,1,0:T(1,128)} %bitcast.5), calls=%async_computation | async-start | bytes 4096 | tf_op jit(solution)/shard_map/all_to_all | solution.py:499
  19.3 11.2 %all-to-all-start.1 = ((bf16[16,38,128]{2,1,0:T(8,128)(2,1)}), bf16[16,38,128]{2,1,0:T(8,128)(2,1)S(1)}, u32[]{:S(2)}, u32[]{:S(2)}) async-start(bf16[16,38,128]{2,1,0:T(8,128)(2,1)} %shard_map.146), calls=%async_computation.1 | async-start | bytes 327680 | tf_op jit(solution)/shard_map/all_to_all | solution.py:503
  30.4 0.7 copy-start.1
  38.0 6.5 %collective-permute-start.1 = (bf16[80,256]{1,0:T(8,128)(2,1)S(1)}, bf16[80,256]{1,0:T(8,128)(2,1)S(1)}, u32[]{:S(2)}, u32[]{:S(2)}) collective-permute-start(bf16[80,256]{1,0:T(8,128)(2,1)S(1)} %get-tuple-element.70), channel_id=1, source_target_pairs={{4,0},{8,4},{12,8},{16,12},{20,16},{24,20},{28,24},{32,28},{36,32}... | collective-permute-start | bytes 122888 | tf_op jit(solution)/shard_map/ppermute | solution.py:482
  41.5 4.1 %collective-permute-start = (bf16[80,256]{1,0:T(8,128)(2,1)S(1)}, bf16[80,256]{1,0:T(8,128)(2,1)S(1)}, u32[]{:S(2)}, u32[]{:S(2)}) collective-permute-start(bf16[80,256]{1,0:T(8,128)(2,1)S(1)} %get-tuple-element.71), channel_id=1, source_target_pairs={{0,4},{4,8},{8,12},{12,16},{16,20},{20,24},{24,28},{28,32},{32,36}... | collective-permute-start | bytes 122888 | tf_op jit(solution)/shard_map/ppermute | solution.py:482
  44.5 1.1 copy-start.2
  45.6 0.6 copy-start.3
  47.8 10.1 %collective-permute-start.2 = (bf16[80,128]{1,0:T(8,128)(2,1)}, bf16[80,128]{1,0:T(8,128)(2,1)S(1)}, u32[]{:S(2)}, u32[]{:S(2)}) collective-permute-start(bf16[80,128]{1,0:T(8,128)(2,1)} %get-tuple-element.34), channel_id=1, source_target_pairs={{0,1},{1,2},{2,3},{4,5},{5,6},{6,7},{8,9},{9,10},{10,11},{12,13},{... | collective-permute-start | bytes 61448 | tf_op jit(solution)/shard_map/ppermute | solution.py:482
  51.4 6.5 %collective-permute-start.3 = (bf16[80,128]{1,0:T(8,128)(2,1)}, bf16[80,128]{1,0:T(8,128)(2,1)S(1)}, u32[]{:S(2)}, u32[]{:S(2)}) collective-permute-start(bf16[80,128]{1,0:T(8,128)(2,1)} %get-tuple-element.35), channel_id=1, source_target_pairs={{1,0},{2,1},{3,2},{5,4},{6,5},{7,6},{9,8},{10,9},{11,10},{13,12},{... | collective-permute-start | bytes 61448 | tf_op jit(solution)/shard_map/ppermute | solution.py:482
  57.9 0.6 copy-start.4
  57.9 0.6 copy-start.5
  125.8 20.6 %all-to-all-start.4 = ((bf16[128,24,128]{2,1,0:T(8,128)(2,1)}), bf16[128,24,128]{2,1,0:T(8,128)(2,1)S(1)}, u32[]{:S(2)}, u32[]{:S(2)}) async-start(bf16[128,24,128]{2,1,0:T(8,128)(2,1)} %get-tuple-element.47), calls=%async_computation.4 | async-start | bytes 1572864 | tf_op jit(solution)/shard_map/all_to_all | solution.py:555
  146.4 0.9 copy-start

commit v3 on v2

--- a/solution.py
+++ b/solution.py
@@ -3,6 +3,7 @@
 
 import jax
 import jax.numpy as jnp
+import numpy as np
 from jax import lax
 from jax.experimental import pallas as pl
 from jax.experimental.pallas import tpu as pltpu
@@ -26,8 +27,8 @@
     return jnp.dot(left, right, preferred_element_type=jnp.float32)
 
 
-def vmem(limit=56 * 1024 * 1024):
-    return pltpu.CompilerParams(vmem_limit_bytes=limit)
+def vmem(mib):
+    return pltpu.CompilerParams(vmem_limit_bytes=mib * 1024 * 1024)
 
 
 def whole():
@@ -40,46 +41,127 @@
 
 def plan_kernel(band_ref, slot_ref, place_ref, wanted_ref):
     count = slot_ref.shape[0]
-    for i in range(wanted_ref.shape[0]):
-        wanted_ref[i] = jnp.int32(-1)
+    at_band = lax.broadcasted_iota(jnp.int32, wanted_ref.shape, 0)
+    at_rank = lax.broadcasted_iota(jnp.int32, wanted_ref.shape, 2)
+    wanted = jnp.full(wanted_ref.shape, -1, jnp.int32)
     for j in range(count):
         band = band_ref[j]
         rank = jnp.int32(0)
         for i in range(j):
             rank = rank + jnp.where(band_ref[i] == band, 1, 0)
-        place = band * MOST + rank
-        place_ref[j] = place
-        wanted_ref[place] = slot_ref[j]
-
-
-def plan(bands, slots, total):
+        place_ref[j] = band * MOST + rank
+        hit = jnp.logical_and(at_band == band, at_rank == rank)
+        wanted = jnp.where(hit, slot_ref[j], wanted)
+    wanted_ref[...] = wanted
+
+
+def plan(bands, slots, n_band):
     return pl.pallas_call(
         plan_kernel,
         out_shape=(
             jax.ShapeDtypeStruct(slots.shape, jnp.int32),
-            jax.ShapeDtypeStruct((total,), jnp.int32),
+            jax.ShapeDtypeStruct((n_band, 8, 128), jnp.int32),
         ),
         in_specs=[scalars(), scalars()],
-        out_specs=(scalars(), scalars()),
+        out_specs=(scalars(), whole()),
     )(bands, slots)
+
+
+def prep_kernel(
+    noisy_ref,
+    grad_ref,
+    w_in_ref,
+    w_out_ref,
+    w_one_ref,
+    w_two_ref,
+    given_ref,
+    first_ref,
+    one_ref,
+    one_back_ref,
+    two_ref,
+    two_back_ref,
+    out_ref,
+    cond_ref,
+    small,
+    noisy_wide,
+    grad_wide,
+):
+    bf, f32 = jnp.bfloat16, jnp.float32
+    chans, rows, _ = noisy_ref.shape
+    coarse_ch = w_in_ref.shape[0] - chans
+    ch = w_in_ref.shape[1]
+    small[...] = jnp.zeros_like(small)
+    w_in = w_in_ref[...].astype(f32)
+    w_out = w_out_ref[...].astype(f32)
+    small[0:coarse_ch, 0:ch] = w_in[0:coarse_ch]
+    cond_ref[...] = small[0:WIDE, 0:ch].astype(bf)
+    small[NOISY_AT : NOISY_AT + chans, 0:ch] = w_in[coarse_ch:]
+    small[GRAD_AT : GRAD_AT + chans, ch:] = w_out
+    first_ref[...] = small[...].T[:, 0:FEED].astype(bf)
+    out_ref[...] = jnp.concatenate([w_out, jnp.zeros((16 - chans, ch), f32)], axis=0).astype(bf)
+    for source, straight, back in (
+        (w_one_ref, one_ref, one_back_ref),
+        (w_two_ref, two_ref, two_back_ref),
+    ):
+        for tap in range(9):
+            lanes = slice(tap * ch, (tap + 1) * ch)
+            straight[:, lanes] = source[tap // 3, tap % 3]
+            back[:, lanes] = source[2 - tap // 3, 2 - tap % 3].T
+    noisy_wide[...] = noisy_ref[...].astype(f32)
+    grad_wide[...] = grad_ref[...].astype(f32)
+    pad = jnp.zeros((FEED - NOISY_AT - 2 * chans, 128), f32)
+    for r in range(rows):
+        pieces = [noisy_wide[:, r, :], grad_wide[:, r, :], pad]
+        given_ref[:, r * 128 : (r + 1) * 128] = jnp.concatenate(pieces, axis=0).astype(bf)
+
+
+def prep(noisy, grad_pred, w_in, w_out, w_one, w_two):
+    bf = jnp.bfloat16
+    chans, rows, cols = noisy.shape
+    ch = w_in.shape[0]
+    square = jax.ShapeDtypeStruct((ch, 9 * ch), bf)
+    return pl.pallas_call(
+        prep_kernel,
+        out_shape=(
+            jax.ShapeDtypeStruct((FEED - NOISY_AT, rows * cols), bf),
+            jax.ShapeDtypeStruct((2 * ch, FEED), bf),
+            square,
+            square,
+            square,
+            square,
+            jax.ShapeDtypeStruct((16, ch), bf),
+            jax.ShapeDtypeStruct((WIDE, ch), bf),
+        ),
+        in_specs=[whole()] * 6,
+        out_specs=(whole(),) * 8,
+        scratch_shapes=[
+            pltpu.VMEM((128, 2 * ch), jnp.float32),
+            pltpu.VMEM(noisy.shape, jnp.float32),
+            pltpu.VMEM(noisy.shape, jnp.float32),
+        ],
+        compiler_params=vmem(56),
+    )(noisy, grad_pred, w_in.T, w_out, w_one, w_two)
 
 
 def serve_kernel(asked_ref, coarse_ref, out_ref):
     for i in range(out_ref.shape[0]):
-        out_ref[i] = coarse_ref[jnp.maximum(asked_ref[i], 0)]
+        out_ref[i] = coarse_ref[jnp.maximum(asked_ref[i // MOST, 0, i % MOST], 0)]
 
 
 def serve(asked, coarse):
+    slots = asked.shape[0] * MOST
     return pl.pallas_call(
         serve_kernel,
-        out_shape=jax.ShapeDtypeStruct((asked.shape[0],) + coarse.shape[1:], coarse.dtype),
+        out_shape=jax.ShapeDtypeStruct((slots,) + coarse.shape[1:], coarse.dtype),
         in_specs=[scalars(), whole()],
         out_specs=whole(),
-        compiler_params=vmem(),
+        compiler_params=vmem(4),
     )(asked, coarse)
 
 
-def feed_kernel(place_ref, arrived_ref, interp_ref, given_ref, feed_ref, edge_ref, picked):
+def feed_kernel(
+    place_ref, arrived_ref, interp_ref, given_ref, hit_ref, feed_ref, first_ref, last_ref, edge_ref, picked
+):
     step = pl.program_id(0)
     ch = arrived_ref.shape[1]
     count = interp_ref.shape[0]
@@ -97,40 +179,57 @@
     feed_ref[...] = jnp.zeros_like(feed_ref)
     feed_ref[0:ch, :] = cond
     feed_ref[NOISY_AT:, :] = given_ref[...]
-    rows = lanes // 128
-    at = lax.broadcasted_iota(jnp.int32, (lanes, 256), 0)
-    lane = lax.broadcasted_iota(jnp.int32, (lanes, 256), 1)
-    row = jnp.bitwise_and(lane, 63) - 2 - step * rows
-    kind = jnp.right_shift(lane, 6)
-    col = kind + jnp.where(kind >= 2, 124, 0)
-    hit = jnp.where(row * 128 + col == at, 1.0, 0.0).astype(jnp.bfloat16)
-    edge_ref[...] += f32dot(feed_ref[...], hit).astype(jnp.bfloat16)
+
+    @pl.when(step == 0)
+    def _():
+        first_ref[...] = feed_ref[:, 0:256]
+
+    @pl.when(step == pl.num_programs(0) - 1)
+    def _():
+        last_ref[...] = feed_ref[:, lanes - 256 :]
+
+    piece = pltpu.roll(f32dot(feed_ref[...], hit_ref[...]), 2 + step * (lanes // 128), 1)
+    edge_ref[...] += piece.astype(jnp.bfloat16)
+
+
+def column_picks(lanes):
+    hit = np.zeros((lanes, 256), np.float32)
+    for k, col in enumerate((0, 1, 126, 127)):
+        for r in range(lanes // 128):
+            hit[r * 128 + col, k * 64 + r] = 1.0
+    return jnp.asarray(hit, jnp.bfloat16)
 
 
 def make_feed(place, arrived, interp, given, blocks=4):
     count, cells, n = interp.shape
     ch = arrived.shape[1]
     lanes = n // blocks
+    bf = jnp.bfloat16
     return pl.pallas_call(
         feed_kernel,
         grid=(blocks,),
         out_shape=(
-            jax.ShapeDtypeStruct((FEED, n), jnp.bfloat16),
-            jax.ShapeDtypeStruct((FEED, 256), jnp.bfloat16),
+            jax.ShapeDtypeStruct((FEED, n), bf),
+            jax.ShapeDtypeStruct((FEED, 256), bf),
+            jax.ShapeDtypeStruct((FEED, 256), bf),
+            jax.ShapeDtypeStruct((FEED, 256), bf),
         ),
         in_specs=[
             scalars(),
             whole(),
             pl.BlockSpec((count, cells, lanes), lambda i: (0, 0, i)),
             pl.BlockSpec((FEED - NOISY_AT, lanes), lambda i: (0, i)),
+            whole(),
         ],
         out_specs=(
             pl.BlockSpec((FEED, lanes), lambda i: (0, i)),
             pl.BlockSpec((FEED, 256), lambda i: (0, 0)),
+            pl.BlockSpec((FEED, 256), lambda i: (0, 0)),
+            pl.BlockSpec((FEED, 256), lambda i: (0, 0)),
         ),
-        scratch_shapes=[pltpu.VMEM((ch, count * cells), jnp.bfloat16)],
-        compiler_params=vmem(),
-    )(place, arrived, interp, given)
+        scratch_shapes=[pltpu.VMEM((ch, count * cells), bf)],
+        compiler_params=vmem(56),
+    )(place, arrived, interp, given, column_picks(lanes))
 
 
 def strip_kernel(top_ref, bot_ref, edge_ref, left_ref, right_ref, own_ref):
@@ -155,7 +254,7 @@
         out_shape=(shape,) * 3,
         in_specs=[whole()] * 3,
         out_specs=(whole(),) * 3,
-        compiler_params=vmem(),
+        compiler_params=vmem(4),
     )(top, bot, edge)
 
 
@@ -367,7 +466,7 @@
             pltpu.VMEM(interp.shape, bf),
             pltpu.SemaphoreType.DMA(()),
         ],
-        compiler_params=vmem(),
+        compiler_params=vmem(56),
     )(*args)
 
 
@@ -385,7 +484,7 @@
     for dest in range(dests):
         total[dest, 2 * LOW : 2 * LOW + each, :] = weights[dest * each : (dest + 1) * each, :]
     for i in range(bands * MOST):
-        slot = asked_ref[i]
+        slot = asked_ref[i // MOST, 0, i % MOST]
         start = share_rows + (i % MOST) * WIDE
         block = parts_ref[i // MOST, start : start + WIDE, :].astype(f32)[0:LOW]
 
@@ -407,7 +506,7 @@
             pltpu.VMEM((dests, HIGH, 128), jnp.float32),
             pltpu.VMEM((SUMS // parts.shape[0], 128), jnp.float32),
         ],
-        compiler_params=vmem(),
+        compiler_params=vmem(12),
     )(asked, parts)
 
 
@@ -433,12 +532,12 @@
         in_specs=[whole()],
         out_specs=(whole(), whole()),
         scratch_shapes=[pltpu.VMEM((HIGH, 128), jnp.float32)],
-        compiler_params=vmem(),
+        compiler_params=vmem(8),
     )(parts)
 
 
 def final_kernel(factor, n_band, parts_ref, in_ref, one_ref, two_ref, out_ref, total):
-    ch = in_ref.shape[0]
+    ch = in_ref.shape[1]
     side = two_ref.shape[0]
     devices = parts_ref.shape[0]
     each = SUMS // devices
@@ -451,11 +550,12 @@
         one_ref[tap // side, tap % side] = total[(9 + tap) * ch : (10 + tap) * ch, :]
     last = total[18 * ch : 19 * ch, :]
     chans = out_ref.shape[0]
-    coarse_ch = in_ref.shape[1] - chans
-    in_ref[:, 0:coarse_ch] = last[:, 0:coarse_ch]
-    in_ref[:, coarse_ch:] = last[:, NOISY_AT : NOISY_AT + chans]
+    coarse_ch = in_ref.shape[0] - chans
+    flipped = last.T
+    in_ref[0:coarse_ch, :] = flipped[0:coarse_ch, :]
+    in_ref[coarse_ch:, :] = flipped[NOISY_AT : NOISY_AT + chans, :]
     start = OUT_AT + GRAD_AT - NOISY_AT
-    out_ref[...] = last.T[start : start + chans, :]
+    out_ref[...] = flipped[start : start + chans, :]
 
 
 def final(parts, n_band, width, taps, inner, chans, factor):
@@ -463,7 +563,7 @@
     return pl.pallas_call(
         functools.partial(final_kernel, factor, n_band),
         out_shape=(
-            jax.ShapeDtypeStruct((width, inner), f32),
+            jax.ShapeDtypeStruct((inner, width), f32),
             jax.ShapeDtypeStruct(taps, f32),
             jax.ShapeDtypeStruct(taps, f32),
             jax.ShapeDtypeStruct((chans, width), f32),
@@ -471,7 +571,7 @@
         in_specs=[whole()],
         out_specs=(whole(),) * 4,
         scratch_shapes=[pltpu.VMEM((SUMS, 128), f32)],
-        compiler_params=vmem(),
+        compiler_params=vmem(12),
     )(parts)
 
 
@@ -492,50 +592,22 @@
     per_band = coarse.shape[1]
     n_band = lax.axis_size("band")
     n_tile = lax.axis_size("tile")
-    slots = n_band * MOST
     local_interp = interp[0, 0]
 
-    place, wanted = plan(margin_band.reshape(-1), margin_slot, slots)
-    asked = lax.all_to_all(
-        wanted.reshape(n_band, MOST), "band", split_axis=0, concat_axis=0, tiled=True
-    ).reshape(slots)
+    place, wanted = plan(margin_band.reshape(-1), margin_slot, n_band)
+    asked = lax.all_to_all(wanted, "band", split_axis=0, concat_axis=0, tiled=True)
+    prepared = prep(noisy, grad_pred, w_in, w_out, w_conv1, w_conv2)
+    asked, prepared = lax.optimization_barrier((asked, prepared))
+    given, weights = prepared[0], tuple(prepared[1:])
     served = serve(asked, coarse[0])
     arrived = lax.all_to_all(served, "band", split_axis=0, concat_axis=0, tiled=True)
-
-    given = jnp.concatenate(
-        [
-            noisy.reshape(chans, cells),
-            grad_pred.reshape(chans, cells),
-            jnp.zeros((FEED - NOISY_AT - 2 * chans, cells), jnp.bfloat16),
-        ],
-        0,
-    )
-    w_pad = lambda w, before: jnp.pad(w, ((0, 0), (before, FEED - before - w.shape[1])))
-    w_first = jnp.concatenate(
-        [
-            w_pad(w_in[:, :coarse_ch], 0) + w_pad(w_in[:, coarse_ch:], NOISY_AT),
-            w_pad(w_out.T, GRAD_AT),
-        ],
-        0,
-    )
-    forward = lambda w: w.transpose(2, 0, 1, 3).reshape(width, 9 * width)
-    backward = lambda w: w[::-1, ::-1].transpose(3, 0, 1, 2).reshape(width, 9 * width)
-    weights = (
-        w_first,
-        forward(w_conv1),
-        backward(w_conv1),
-        forward(w_conv2),
-        backward(w_conv2),
-        jnp.pad(w_out, ((0, 16 - chans), (0, 0))),
-        jnp.pad(w_in[:, :coarse_ch].T, ((0, WIDE - coarse_ch), (0, 0))),
-    )
     tile, band = lax.axis_index("tile"), lax.axis_index("band")
     flags = jnp.stack([tile > 0, tile < n_tile - 1, band > 0, band < n_band - 1])
     flags = flags.astype(jnp.float32)
-    arrived, weights = lax.optimization_barrier((arrived, weights))
-
-    feed, edge = make_feed(place, arrived, local_interp, given)
-    top, bot = halo(feed[:, : 2 * cols], feed[:, cells - 2 * cols :], "tile")
+    arrived, flags = lax.optimization_barrier((arrived, flags))
+
+    feed, first, last, edge = make_feed(place, arrived, local_interp, given)
+    top, bot = halo(first, last, "tile")
     left_out, right_out, own = strips(top, bot, edge)
     left, right = halo(left_out, right_out, "band")
     pred, pack = net(
@@ -557,7 +629,7 @@
     grad_in, grad_one, grad_two, grad_out = final(
         sums, n_band, width, w_conv1.shape, w_in.shape[1], chans, factor
     )
-    return (pred, coarse_grad, grad_in, grad_one, grad_two, grad_out)
+    return (pred, coarse_grad, grad_in.T, grad_one, grad_two, grad_out)
 
 
 def solution(mesh):

time: 152 us -> 135 us (0.89)
  local copies, waits for them, and re-layouts: 25.3 us -> 4.78 us
  waiting for transfers between devices: 16.4 us -> 27.3 us
  blocking collectives: 42.6 us -> 40.2 us
  other arithmetic: 2.85 us -> 0.65 us
  Pallas kernels: 37.8 us -> 35.8 us
    unnamed x21 -> x16, local copies, waits for them, and re-layouts: 12.3 us -> 4.78 us
    ppermute x4, waiting for transfers between devices: 1.05 us -> 6.61 us  [halo(): return (lax.ppermute(last, axis, up), lax.ppermute(first, axis, down))]
    all_to_all x1, waiting for transfers between devices: 0.01 us -> 4.35 us  [per_device(): lax.all_to_all(served, 'band', split_axis=0, concat_axis=0, tiled=True)]
    optimization_barrier x5 -> x0, local copies, waits for them, and re-layouts: 4.3 us -> none  [per_device(): arrived, weights = lax.optimization_barrier((arrived, weights))]
    pallas_call x1 -> x2, Pallas kernels: 1.79 us -> 4.04 us  [the longest x1 2.55 us: prep(): pl.pallas_call(prep_kernel, out_shape=(jax.ShapeDtypeStruct((FEED - NOISY...]
    rev x2 -> x0, local copies, waits for them, and re-layouts: 1.97 us -> none  [per_device(): w[::-1, ::-1].transpose(3, 0, 1, 2).reshape(width, 9 * width)]
    pad x2 -> x0, local copies, waits for them, and re-layouts: 1.89 us -> none  [the longest x1 1.29 us: per_device(): jnp.pad(w_out, ((0, 16 - chans), (0, 0)))]
    all_to_all x2 -> x0, local copies, waits for them, and re-layouts: 1.83 us -> none  [per_device(): lax.all_to_all(wanted.reshape(n_band, MOST), 'band', split_axis=0, concat...]
  transfers between devices with their start and end apart: 7 -> 7, of which waited for: 2 -> 5; matrix products, arithmetic and copies ran while one was open for 13% -> 2% of each run, Pallas kernels for 0% -> 2%
where the time goes in v3:
time: 135 us
  blocking collectives  40.2 us (30%)
  Pallas kernels  35.8 us (27%)
  waiting for transfers between devices  27.3 us (20%)
  starting transfers between devices  25 us (19%)
  local copies, waits for them, and re-layouts  4.78 us (4%)
    all_to_all x1, blocking collectives, per_device(): lax.all_to_all(merge(asked, pack, n_tile), 'tile', split_axis=0, concat_a...  23.8 us
    pallas_call x1, Pallas kernels, net(): pl.pallas_call(net_kernel, out_shape=(jax.ShapeDtypeStruct((chans, rows,...  19.9 us
    all_to_all x1, blocking collectives, per_device(): pack = lax.all_to_all(pack, 'band', split_axis=0, concat_axis=0, tiled=True)  16.4 us
    all_to_all x1, waiting for transfers between devices, per_device(): sums = lax.all_to_all(sums, ALL, split_axis=0, concat_axis=0, tiled=True)  16.2 us
    ppermute x4, starting transfers between devices, halo(): return (lax.ppermute(last, axis, up), lax.ppermute(first, axis, down))  11.2 us
    pallas_call x1, Pallas kernels, make_feed(): pl.pallas_call(feed_kernel, grid=(blocks,), out_shape=(jax.ShapeDtypeStru...  6.89 us
    ppermute x4, waiting for transfers between devices, halo(): return (lax.ppermute(last, axis, up), lax.ppermute(first, axis, down))  6.61 us
    all_to_all x1, starting transfers between devices, per_device(): lax.all_to_all(wanted, 'band', split_axis=0, concat_axis=0, tiled=True)  5.87 us
  transfers between devices with their start and end apart: 7, of which 5 were waited for; matrix products, arithmetic and copies ran while one was open for 2% of the time, Pallas kernels for 2%

profile of v3, /device:TPU:1, one launch (start us, length us, event | category | flops | bytes accessed | tf_op | source)
XLA Modules:
  0.0 134.5 jit_solution(16443379498546357107)
XLA Ops:
  0.6 1.3 shard_map.154
  2.0 5.9 %all-to-all-start = ((s32[4,8,128]{2,1,0:T(8,128)}), s32[4,8,128]{2,1,0:T(8,128)S(1)}, u32[]{:S(2)}, u32[]{:S(2)}) async-start(s32[4,8,128]{2,1,0:T(8,128)} %get-tuple-element.43), calls=%async_computation | async-start | bytes 32768 | tf_op jit(solution)/shard_map/all_to_all | solution.py:598
  7.8 1.5 %copy.20 = bf16[1,64,38,128]{3,2,1,0:T(8,128)(2,1)S(1)} copy(bf16[1,64,38,128]{3,1,2,0:T(8,128)(2,1)} %param.13) | data formatting | bytes 1245184 | tf_op args[2]
  9.3 2.5 %shard_map.155 = (bf16[32,4096]{1,0:T(8,128)(2,1)}, bf16[256,80]{1,0:T(8,128)(2,1)}, bf16[128,1152]{1,0:T(8,128)(2,1)}, bf16[128,1152]{1,0:T(8,128)(2,1)}, bf16[...) custom-call(bf16[12,32,128]{2,1,0:T(8,128)(2,1)} %noisy_ref.1, ...), custom_call_target="tpu_custom_call" | custom-call | tf_op jit(solution)/shard_map/pallas_call | solution.py:123
  11.9 0.2 all-to-all-done.asked_ref
  12.0 1.5 %shard_map.156 = bf16[16,38,128]{2,1,0:T(8,128)(2,1)} custom-call(s32[4,8,128]{2,1,0:T(8,128)S(1)} %all-to-all-done.asked_ref, bf16[64,38,128]{2,1,0:T(8,128)(2,1)S(1)} %bitcast.11), custom_call_target="tpu_custom_call" | custom-call | tf_op jit(solution)/shard_map/pallas_call | solution.py:153
  13.5 4.1 %all-to-all-start.1 = ((bf16[16,38,128]{2,1,0:T(8,128)(2,1)}), bf16[16,38,128]{2,1,0:T(8,128)(2,1)S(1)}, u32[]{:S(2)}, u32[]{:S(2)}) async-start(bf16[16,38,128]{2,1,0:T(8,128)(2,1)} %shard_map.156), calls=%async_computation.1 | async-start | bytes 327680 | tf_op jit(solution)/shard_map/all_to_all | solution.py:603
  17.6 0.7 add_convert_fusion.flag_ref
  18.3 4.3 %all-to-all-done.1.arrived_ref = bf16[16,38,128]{2,1,0:T(8,128)(2,1)S(1)} async-done(((bf16[16,38,128]{2,1,0:T(8,128)(2,1)}), bf16[16,38,128]{2,1,0:T(8,128)(2,1)S(1)}, u32[]{:S(2)}, u32[]{:S(2)}) %all-to-all-start.1) | async-done | bytes 155680 | tf_op jit(solution)/shard_map/all_to_all | solution.py:603
  22.6 0.0 copy-start.4
  22.6 0.7 copy-done.4
  23.3 6.9 %shard_map.157 = (bf16[80,4096]{1,0:T(8,128)(2,1)}, bf16[80,256]{1,0:T(8,128)(2,1)}, bf16[80,256]{1,0:T(8,128)(2,1)}, bf16[80,256]{1,0:T(8,128)(2,1)}) custom-call(s32[8]{0:T(128)} %get-tuple-element.42.place_ref, bf16[16,38,128]{2,1,0:T(8,128)(2,1)} %copy-done.4, bf16[8,128,4096]{2,1,0:T(8,128)(2,1)} %bitcast.12, ...), custom_call_target="tpu_custom_call" | custom-call | tf_op jit(solution)/shard_map/pallas_call | solution.py:208
  30.2 5.7 %collective-permute-start = (bf16[80,256]{1,0:T(8,128)(2,1)}, bf16[80,256]{1,0:T(8,128)(2,1)S(1)}, u32[]{:S(2)}, u32[]{:S(2)}) collective-permute-start(bf16[80,256]{1,0:T(8,128)(2,1)} %get-tuple-element.57), channel_id=1, source_target_pairs={{0,4},{4,8},{8,12},{12,16},{16,20},{20,24},{24,28},{28,32},{32,36}... | collective-permute-start | bytes 122888 | tf_op jit(solution)/shard_map/ppermute | solution.py:582
  35.8 1.9 %collective-permute-start.1 = (bf16[80,256]{1,0:T(8,128)(2,1)}, bf16[80,256]{1,0:T(8,128)(2,1)S(1)}, u32[]{:S(2)}, u32[]{:S(2)}) collective-permute-start(bf16[80,256]{1,0:T(8,128)(2,1)} %get-tuple-element.58), channel_id=1, source_target_pairs={{4,0},{8,4},{12,8},{16,12},{20,16},{24,20},{28,24},{32,28},{36,32}... | collective-permute-start | bytes 122888 | tf_op jit(solution)/shard_map/ppermute | solution.py:582
  37.8 0.0 collective-permute-done.top_ref
  37.8 0.0 copy-start
  37.8 3.6 %collective-permute-done.1.bot_ref = bf16[80,256]{1,0:T(8,128)(2,1)S(1)} collective-permute-done((bf16[80,256]{1,0:T(8,128)(2,1)}, bf16[80,256]{1,0:T(8,128)(2,1)S(1)}, u32[]{:S(2)}, u32[]{:S(2)}) %collective-permute-start.1) | collective-permute-done | bytes 40992 | tf_op jit(solution)/shard_map/ppermute | solution.py:582
  41.4 0.0 copy-start.1
  41.4 0.0 copy-start.2
  41.4 0.8 copy-done.2
  42.2 0.2 shard_map.158
  42.4 0.0 copy-start.3
  42.4 0.6 copy-done.3
  43.0 2.2 %collective-permute-start.2 = (bf16[80,128]{1,0:T(8,128)(2,1)S(1)}, bf16[80,128]{1,0:T(8,128)(2,1)S(1)}, u32[]{:S(2)}, u32[]{:S(2)}) collective-permute-start(bf16[80,128]{1,0:T(8,128)(2,1)S(1)} %get-tuple-element.60), channel_id=1, source_target_pairs={{0,1},{1,2},{2,3},{4,5},{5,6},{6,7},{8,9},{9,10},{10,11},{12,13},{... | collective-permute-start | bytes 61448 | tf_op jit(solution)/shard_map/ppermute | solution.py:582
  45.1 1.5 %collective-permute-start.3 = (bf16[80,128]{1,0:T(8,128)(2,1)S(1)}, bf16[80,128]{1,0:T(8,128)(2,1)S(1)}, u32[]{:S(2)}, u32[]{:S(2)}) collective-permute-start(bf16[80,128]{1,0:T(8,128)(2,1)S(1)} %get-tuple-element.61), channel_id=1, source_target_pairs={{1,0},{2,1},{3,2},{5,4},{6,5},{7,6},{9,8},{10,9},{11,10},{13,12},{... | collective-permute-start | bytes 61448 | tf_op jit(solution)/shard_map/ppermute | solution.py:582
  46.6 0.0 collective-permute-done.2.left_ref
  46.6 0.0 copy-start.5
  46.6 3.0 %collective-permute-done.3.right_ref = bf16[80,128]{1,0:T(8,128)(2,1)S(1)} collective-permute-done((bf16[80,128]{1,0:T(8,128)(2,1)S(1)}, bf16[80,128]{1,0:T(8,128)(2,1)S(1)}, u32[]{:S(2)}, u32[]{:S(2)}) %collective-permute-start.3) | collective-permute-done | bytes 20512 | tf_op jit(solution)/shard_map/ppermute | solution.py:582
  49.7 0.0 copy-start.6
  49.7 0.0 copy-done
  49.7 0.0 copy-done.1
  49.7 0.0 copy-done.5
  49.7 0.6 copy-done.6
  50.3 19.9 %shard_map.159 = (f32[12,32,128]{2,1,0:T(8,128)}, bf16[4,832,128]{2,1,0:T(8,128)(2,1)}) custom-call(s32[8]{0:T(128)} %get-tuple-element.42.place_ref, f32[4]{0:T(128)} %add_convert_fusion.flag_ref, bf16[80,4096]{1,0:T(8,128)(2,1)} %get-tuple-element.56.feed_ref, bf16[80,256]{1,0:T(8,128)(2,1)} %copy-done, bf16[80,256]{1,0:T(8,128)(2,1)} %copy-done.1, ...), custom_call_target="tpu_custom_call" | custom-call | tf_op jit(solution)/shard_map/pallas_call | solution.py:446
  70.2 16.4 %all_to_all.25.parts_ref = bf16[4,832,128]{2,1,0:T(8,128)(2,1)S(1)} all-to-all(bf16[4,832,128]{2,1,0:T(8,128)(2,1)} %get-tuple-element.71), channel_id=1, replica_groups=mesh['tile'=32,'band'=4] {'band'}, dimensions={0} | all-to-all | bytes 1703936 | tf_op jit(solution)/shard_map/all_to_all | solution.py:620
  86.6 1.3 shard_map.160
  87.9 23.8 %all_to_all.26.parts_ref = bf16[32,112,128]{2,1,0:T(8,128)(2,1)S(1)} all-to-all(bf16[32,112,128]{2,1,0:T(8,128)(2,1)S(1)} %shard_map.160), channel_id=1, replica_groups=mesh['tile'=32,'band'=4] {'tile'}, dimensions={0} | all-to-all | bytes 1835008 | tf_op jit(solution)/shard_map/all_to_all | solution.py:621
  111.7 1.0 shard_map.161
  112.8 3.8 %all-to-all-start.4 = ((bf16[128,24,128]{2,1,0:T(8,128)(2,1)}), bf16[128,24,128]{2,1,0:T(8,128)(2,1)S(1)}, u32[]{:S(2)}, u32[]{:S(2)}) async-start(bf16[128,24,128]{2,1,0:T(8,128)(2,1)} %get-tuple-element.73), calls=%async_computation.4 | async-start | bytes 1572864 | tf_op jit(solution)/shard_map/all_to_all | solution.py:627
  116.6 0.6 copy.18
  117.2 16.2 %all-to-all-done.4.parts_ref = bf16[128,24,128]{2,1,0:T(8,128)(2,1)S(1)} async-done(((bf16[128,24,128]{2,1,0:T(8,128)(2,1)}), bf16[128,24,128]{2,1,0:T(8,128)(2,1)S(1)}, u32[]{:S(2)}, u32[]{:S(2)}) %all-to-all-start.4) | async-done | bytes 786464 | tf_op jit(solution)/shard_map/all_to_all | solution.py:627
  133.4 1.1 shard_map.162
Async XLA Ops:
  2.0 10.1 %all-to-all-start = ((s32[4,8,128]{2,1,0:T(8,128)}), s32[4,8,128]{2,1,0:T(8,128)S(1)}, u32[]{:S(2)}, u32[]{:S(2)}) async-start(s32[4,8,128]{2,1,0:T(8,128)} %get-tuple-element.43), calls=%async_computation | async-start | bytes 32768 | tf_op jit(solution)/shard_map/all_to_all | solution.py:598
  13.5 9.1 %all-to-all-start.1 = ((bf16[16,38,128]{2,1,0:T(8,128)(2,1)}), bf16[16,38,128]{2,1,0:T(8,128)(2,1)S(1)}, u32[]{:S(2)}, u32[]{:S(2)}) async-start(bf16[16,38,128]{2,1,0:T(8,128)(2,1)} %shard_map.156), calls=%async_computation.1 | async-start | bytes 327680 | tf_op jit(solution)/shard_map/all_to_all | solution.py:603
  22.6 0.7 copy-start.4
  30.2 7.6 %collective-permute-start = (bf16[80,256]{1,0:T(8,128)(2,1)}, bf16[80,256]{1,0:T(8,128)(2,1)S(1)}, u32[]{:S(2)}, u32[]{:S(2)}) collective-permute-start(bf16[80,256]{1,0:T(8,128)(2,1)} %get-tuple-element.57), channel_id=1, source_target_pairs={{0,4},{4,8},{8,12},{12,16},{16,20},{20,24},{24,28},{28,32},{32,36}... | collective-permute-start | bytes 122888 | tf_op jit(solution)/shard_map/ppermute | solution.py:582
  35.8 5.5 %collective-permute-start.1 = (bf16[80,256]{1,0:T(8,128)(2,1)}, bf16[80,256]{1,0:T(8,128)(2,1)S(1)}, u32[]{:S(2)}, u32[]{:S(2)}) collective-permute-start(bf16[80,256]{1,0:T(8,128)(2,1)} %get-tuple-element.58), channel_id=1, source_target_pairs={{4,0},{8,4},{12,8},{16,12},{20,16},{24,20},{28,24},{32,28},{36,32}... | collective-permute-start | bytes 122888 | tf_op jit(solution)/shard_map/ppermute | solution.py:582
  37.8 11.9 %copy-start = (bf16[80,256]{1,0:T(8,128)(2,1)}, bf16[80,256]{1,0:T(8,128)(2,1)S(1)}, u32[]{:S(2)}) copy-start(bf16[80,256]{1,0:T(8,128)(2,1)S(1)} %collective-permute-done.top_ref) | copy-start | bytes 122884
  41.4 8.3 %copy-start.1 = (bf16[80,256]{1,0:T(8,128)(2,1)}, bf16[80,256]{1,0:T(8,128)(2,1)S(1)}, u32[]{:S(2)}) copy-start(bf16[80,256]{1,0:T(8,128)(2,1)S(1)} %collective-permute-done.1.bot_ref) | copy-start | bytes 122884
  41.4 0.8 copy-start.2
  42.4 0.6 copy-start.3
  43.0 3.7 %collective-permute-start.2 = (bf16[80,128]{1,0:T(8,128)(2,1)S(1)}, bf16[80,128]{1,0:T(8,128)(2,1)S(1)}, u32[]{:S(2)}, u32[]{:S(2)}) collective-permute-start(bf16[80,128]{1,0:T(8,128)(2,1)S(1)} %get-tuple-element.60), channel_id=1, source_target_pairs={{0,1},{1,2},{2,3},{4,5},{5,6},{6,7},{8,9},{9,10},{10,11},{12,13},{... | collective-permute-start | bytes 61448 | tf_op jit(solution)/shard_map/ppermute | solution.py:582
  45.1 4.5 %collective-permute-start.3 = (bf16[80,128]{1,0:T(8,128)(2,1)S(1)}, bf16[80,128]{1,0:T(8,128)(2,1)S(1)}, u32[]{:S(2)}, u32[]{:S(2)}) collective-permute-start(bf16[80,128]{1,0:T(8,128)(2,1)S(1)} %get-tuple-element.61), channel_id=1, source_target_pairs={{1,0},{2,1},{3,2},{5,4},{6,5},{7,6},{9,8},{10,9},{11,10},{13,12},{... | collective-permute-start | bytes 61448 | tf_op jit(solution)/shard_map/ppermute | solution.py:582
  46.6 3.0 %copy-start.5 = (bf16[80,128]{1,0:T(8,128)(2,1)}, bf16[80,128]{1,0:T(8,128)(2,1)S(1)}, u32[]{:S(2)}) copy-start(bf16[80,128]{1,0:T(8,128)(2,1)S(1)} %collective-permute-done.2.left_ref) | copy-start | bytes 61444
  49.7 0.6 copy-start.6
  112.8 20.6 %all-to-all-start.4 = ((bf16[128,24,128]{2,1,0:T(8,128)(2,1)}), bf16[128,24,128]{2,1,0:T(8,128)(2,1)S(1)}, u32[]{:S(2)}, u32[]{:S(2)}) async-start(bf16[128,24,128]{2,1,0:T(8,128)(2,1)} %get-tuple-element.73), calls=%async_computation.4 | async-start | bytes 1572864 | tf_op jit(solution)/shard_map/all_to_all | solution.py:627

commit v4 on v3

--- a/solution.py
+++ b/solution.py
@@ -16,9 +16,9 @@
 NOISY_AT = 48
 GRAD_AT = 60
 WIDE = 48
-SUMS = 2560
+SUMS = 2432
 OUT_AT = 80
-LOW, HIGH = 40, 112
+HIGH = 96
 CHUNK = 24
 NT = (((1,), (1,)), ((), ()))
 
@@ -39,32 +39,35 @@
     return pl.BlockSpec(memory_space=pltpu.SMEM)
 
 
-def plan_kernel(band_ref, slot_ref, place_ref, wanted_ref):
+def plan_kernel(me_ref, band_ref, slot_ref, place_ref, near_ref, *wanted_refs):
     count = slot_ref.shape[0]
-    at_band = lax.broadcasted_iota(jnp.int32, wanted_ref.shape, 0)
-    at_rank = lax.broadcasted_iota(jnp.int32, wanted_ref.shape, 2)
-    wanted = jnp.full(wanted_ref.shape, -1, jnp.int32)
+    n_band = len(wanted_refs)
+    lane = lax.broadcasted_iota(jnp.int32, wanted_refs[0].shape, 1)
+    wanted = [jnp.full(ref.shape, -1, jnp.int32) for ref in wanted_refs]
     for j in range(count):
         band = band_ref[j]
         rank = jnp.int32(0)
         for i in range(j):
             rank = rank + jnp.where(band_ref[i] == band, 1, 0)
+        ahead = band - me_ref[0]
+        ahead = jnp.where(ahead < 0, ahead + n_band, ahead)
         place_ref[j] = band * MOST + rank
-        hit = jnp.logical_and(at_band == band, at_rank == rank)
-        wanted = jnp.where(hit, slot_ref[j], wanted)
-    wanted_ref[...] = wanted
-
-
-def plan(bands, slots, n_band):
+        near_ref[j] = ahead * MOST + rank
+        for k in range(n_band):
+            spot = jnp.where(ahead == k, rank, -1)
+            wanted[k] = jnp.where(lane == spot, slot_ref[j], wanted[k])
+    for k in range(n_band):
+        wanted_refs[k][...] = wanted[k]
+
+
+def plan(me, bands, slots, n_band):
     return pl.pallas_call(
         plan_kernel,
-        out_shape=(
-            jax.ShapeDtypeStruct(slots.shape, jnp.int32),
-            jax.ShapeDtypeStruct((n_band, 8, 128), jnp.int32),
-        ),
-        in_specs=[scalars(), scalars()],
-        out_specs=(scalars(), whole()),
-    )(bands, slots)
+        out_shape=(jax.ShapeDtypeStruct(slots.shape, jnp.int32),) * 2
+        + (jax.ShapeDtypeStruct((8, 128), jnp.int32),) * n_band,
+        in_specs=[scalars()] * 3,
+        out_specs=(scalars(),) * 2 + (whole(),) * n_band,
+    )(me, bands, slots)
 
 
 def prep_kernel(
@@ -143,53 +146,63 @@
     )(noisy, grad_pred, w_in.T, w_out, w_one, w_two)
 
 
-def serve_kernel(asked_ref, coarse_ref, out_ref):
-    for i in range(out_ref.shape[0]):
-        out_ref[i] = coarse_ref[jnp.maximum(asked_ref[i // MOST, 0, i % MOST], 0)]
+def serve_kernel(n_band, *refs):
+    asked_refs, coarse_ref, out_refs = refs[:n_band], refs[n_band], refs[n_band + 1 :]
+    for asked_ref, out_ref in zip(asked_refs, out_refs):
+        for i in range(MOST):
+            out_ref[i] = coarse_ref[jnp.maximum(asked_ref[0, i], 0)]
 
 
 def serve(asked, coarse):
-    slots = asked.shape[0] * MOST
-    return pl.pallas_call(
-        serve_kernel,
-        out_shape=jax.ShapeDtypeStruct((slots,) + coarse.shape[1:], coarse.dtype),
-        in_specs=[scalars(), whole()],
+    n_band = len(asked)
+    shape = jax.ShapeDtypeStruct((MOST,) + coarse.shape[1:], coarse.dtype)
+    return pl.pallas_call(
+        functools.partial(serve_kernel, n_band),
+        out_shape=(shape,) * n_band,
+        in_specs=[scalars()] * n_band + [whole()],
+        out_specs=(whole(),) * n_band,
+        compiler_params=vmem(4),
+    )(*asked, coarse)
+
+
+def feed_kernel(n_band, near_ref, *refs):
+    arrived_refs = refs[:n_band]
+    interp_ref, given_ref, hit_ref = refs[n_band : n_band + 3]
+    feed_ref, first_ref, last_ref, edge_ref, arrived, picked = refs[n_band + 3 :]
+    ch = arrived.shape[1]
+    count, cells, n = interp_ref.shape
+    lanes = hit_ref.shape[0]
+    bf = jnp.bfloat16
+    for k in range(n_band):
+        arrived[k * MOST : (k + 1) * MOST] = arrived_refs[k][...]
+    for j in range(count):
+        picked[:, j * cells : (j + 1) * cells] = arrived[near_ref[j]]
+    feed_ref[...] = jnp.zeros_like(feed_ref)
+    feed_ref[NOISY_AT:, :] = given_ref[...]
+    edge = jnp.zeros(edge_ref.shape, jnp.float32)
+    for step in range(n // lanes):
+        block = slice(step * lanes, (step + 1) * lanes)
+        matrix = interp_ref[:, :, block].reshape(count * cells, lanes)
+        feed_ref[0:ch, block] = f32dot(picked[...], matrix).astype(bf)
+        piece = f32dot(feed_ref[:, block], hit_ref[...])
+        edge = edge + pltpu.roll(piece, 2 + step * (lanes // 128), 1)
+    edge_ref[...] = edge.astype(bf)
+    first_ref[...] = feed_ref[:, 0:256]
+    last_ref[...] = feed_ref[:, n - 256 :]
+
+
+def stash_kernel(source_ref, out_ref):
+    pltpu.sync_copy(source_ref, out_ref)
+
+
+def stash(array):
+    return pl.pallas_call(
+        stash_kernel,
+        out_shape=pltpu.VMEM(array.shape, array.dtype),
+        in_specs=[pl.BlockSpec(memory_space=pltpu.HBM)],
         out_specs=whole(),
         compiler_params=vmem(4),
-    )(asked, coarse)
-
-
-def feed_kernel(
-    place_ref, arrived_ref, interp_ref, given_ref, hit_ref, feed_ref, first_ref, last_ref, edge_ref, picked
-):
-    step = pl.program_id(0)
-    ch = arrived_ref.shape[1]
-    count = interp_ref.shape[0]
-    cells = interp_ref.shape[1]
-    lanes = interp_ref.shape[2]
-
-    @pl.when(step == 0)
-    def _():
-        edge_ref[...] = jnp.zeros_like(edge_ref)
-        for j in range(count):
-            picked[:, j * cells : (j + 1) * cells] = arrived_ref[place_ref[j]]
-
-    matrix = interp_ref[...].reshape(count * cells, lanes)
-    cond = f32dot(picked[...], matrix).astype(jnp.bfloat16)
-    feed_ref[...] = jnp.zeros_like(feed_ref)
-    feed_ref[0:ch, :] = cond
-    feed_ref[NOISY_AT:, :] = given_ref[...]
-
-    @pl.when(step == 0)
-    def _():
-        first_ref[...] = feed_ref[:, 0:256]
-
-    @pl.when(step == pl.num_programs(0) - 1)
-    def _():
-        last_ref[...] = feed_ref[:, lanes - 256 :]
-
-    piece = pltpu.roll(f32dot(feed_ref[...], hit_ref[...]), 2 + step * (lanes // 128), 1)
-    edge_ref[...] += piece.astype(jnp.bfloat16)
+    )(pltpu.with_memory_space_constraint(array, pltpu.HBM))
 
 
 def column_picks(lanes):
@@ -200,36 +213,23 @@
     return jnp.asarray(hit, jnp.bfloat16)
 
 
-def make_feed(place, arrived, interp, given, blocks=4):
+def make_feed(near, arrived, interp, given, blocks=4):
     count, cells, n = interp.shape
-    ch = arrived.shape[1]
-    lanes = n // blocks
+    n_band = len(arrived)
+    ch = arrived[0].shape[1]
     bf = jnp.bfloat16
-    return pl.pallas_call(
-        feed_kernel,
-        grid=(blocks,),
-        out_shape=(
-            jax.ShapeDtypeStruct((FEED, n), bf),
-            jax.ShapeDtypeStruct((FEED, 256), bf),
-            jax.ShapeDtypeStruct((FEED, 256), bf),
-            jax.ShapeDtypeStruct((FEED, 256), bf),
-        ),
-        in_specs=[
-            scalars(),
-            whole(),
-            pl.BlockSpec((count, cells, lanes), lambda i: (0, 0, i)),
-            pl.BlockSpec((FEED - NOISY_AT, lanes), lambda i: (0, i)),
-            whole(),
+    side = jax.ShapeDtypeStruct((FEED, 256), bf)
+    return pl.pallas_call(
+        functools.partial(feed_kernel, n_band),
+        out_shape=(jax.ShapeDtypeStruct((FEED, n), bf), side, side, side),
+        in_specs=[scalars()] + [whole()] * (n_band + 3),
+        out_specs=(whole(),) * 4,
+        scratch_shapes=[
+            pltpu.VMEM((n_band * MOST, ch, cells), bf),
+            pltpu.VMEM((ch, count * cells), bf),
         ],
-        out_specs=(
-            pl.BlockSpec((FEED, lanes), lambda i: (0, i)),
-            pl.BlockSpec((FEED, 256), lambda i: (0, 0)),
-            pl.BlockSpec((FEED, 256), lambda i: (0, 0)),
-            pl.BlockSpec((FEED, 256), lambda i: (0, 0)),
-        ),
-        scratch_shapes=[pltpu.VMEM((ch, count * cells), bf)],
-        compiler_params=vmem(56),
-    )(place, arrived, interp, given, column_picks(lanes))
+        compiler_params=vmem(16),
+    )(near, *arrived, interp, given, column_picks(n // blocks))
 
 
 def strip_kernel(top_ref, bot_ref, edge_ref, left_ref, right_ref, own_ref):
@@ -291,15 +291,11 @@
     sum_one_ref,
     sum_two_ref,
     dcond_ref,
-    matrix_ref,
-    sem,
 ):
     rows = pred_ref.shape[1]
     tall = rows + 4
     ch = 128
     bf, f32 = jnp.bfloat16, jnp.float32
-    fetch = pltpu.make_async_copy(interp_ref, matrix_ref, sem)
-    fetch.start()
     lane = lax.broadcasted_iota(jnp.int32, (ch, 128), 1)
     at_left = lane == 0
     at_right = lane == 127
@@ -360,47 +356,35 @@
             put(a_zero_ref, row + k, act[:, lanes], edge_a, row + k)
             put(d_two_ref, row + k, both[ch:, lanes], edge_d, row + k)
 
-    half = (rows + 2) // 2
-    for row in (0, half):
-        act, slope = silu_parts(f32dot(w_one_ref[...], around(a_zero_ref, row, half)))
-        back = f32dot(w_two_back_ref[...], around(d_two_ref, row, half)) * slope
-        for k in range(half):
-            lanes = slice(k * 128, (k + 1) * 128)
-            act_row, back_row = act[:, lanes], back[:, lanes]
-            if row + k == 0:
-                act_row, back_row = act_row * flag_ref[0], back_row * flag_ref[0]
-            if row + k == rows + 1:
-                act_row, back_row = act_row * flag_ref[1], back_row * flag_ref[1]
-            put(a_one_ref, row + k, act_row, edge_a_one, row + k + 1)
-            put(d_one_ref, row + k, back_row, edge_d_one, row + k + 1)
-
-    half = rows // 2
-    sum_in = jnp.zeros((ch, FEED), f32)
-    sum_out = jnp.zeros((ch, FEED - NOISY_AT), f32)
-    for row in (0, half):
-        mine = slice((row + 2) * 128, (row + 2 + half) * 128)
-        inner = slice((row + 1) * 128, (row + 1 + half) * 128)
-        x = x_ref[:, mine]
-        d_two = d_two_ref[ch : 2 * ch, mine]
-        cols_one = around(a_one_ref, row, half)
-        z_two = f32dot(w_two_ref[...], cols_one)
-        a_two = (a_zero_ref[ch : 2 * ch, mine].astype(f32) + z_two).astype(bf)
-        pred = f32dot(w_out_ref[...], a_two)
-        for k in range(half):
-            pred_ref[:, row + k, :] = pred[0 : pred_ref.shape[0], k * 128 : (k + 1) * 128]
-        sum_out = sum_out + nt_dot(a_two, x[NOISY_AT:, :])
-        part_two = nt_dot(d_two, cols_one)
-        back = f32dot(w_one_back_ref[...], around(d_one_ref, row, half))
-        d_zero = ((back + d_two.astype(f32)) * slope_ref[:, mine]).astype(bf)
-        sum_in = sum_in + nt_dot(d_zero, x)
-        dcond_ref[:, row * 128 : (row + half) * 128] = f32dot(w_cond_ref[...], d_zero).astype(bf)
-        part_one = nt_dot(d_one_ref[ch : 2 * ch, inner], around(a_zero_ref, row + 1, half))
+    act, slope = silu_parts(f32dot(w_one_ref[...], around(a_zero_ref, 0, rows + 2)))
+    back = f32dot(w_two_back_ref[...], around(d_two_ref, 0, rows + 2)) * slope
+    for row in range(rows + 2):
+        lanes = slice(row * 128, (row + 1) * 128)
+        act_row, back_row = act[:, lanes], back[:, lanes]
         if row == 0:
-            sum_two_ref[...] = part_two
-            sum_one_ref[...] = part_one
-        else:
-            sum_two_ref[...] += part_two
-            sum_one_ref[...] += part_one
+            act_row, back_row = act_row * flag_ref[0], back_row * flag_ref[0]
+        if row == rows + 1:
+            act_row, back_row = act_row * flag_ref[1], back_row * flag_ref[1]
+        put(a_one_ref, row, act_row, edge_a_one, row + 1)
+        put(d_one_ref, row, back_row, edge_d_one, row + 1)
+
+    mine = slice(256, (rows + 2) * 128)
+    x = x_ref[:, mine]
+    d_two = d_two_ref[ch : 2 * ch, mine]
+    cols_one = around(a_one_ref, 0, rows)
+    z_two = f32dot(w_two_ref[...], cols_one)
+    a_two = (a_zero_ref[ch : 2 * ch, mine].astype(f32) + z_two).astype(bf)
+    pred = f32dot(w_out_ref[...], a_two)
+    for k in range(rows):
+        pred_ref[:, k, :] = pred[0 : pred_ref.shape[0], k * 128 : (k + 1) * 128]
+    sum_out = nt_dot(a_two, x[NOISY_AT:, :])
+    sum_two_ref[...] = nt_dot(d_two, cols_one)
+    back = f32dot(w_one_back_ref[...], around(d_one_ref, 0, rows))
+    d_zero = ((back + d_two.astype(f32)) * slope_ref[:, mine]).astype(bf)
+    sum_in = nt_dot(d_zero, x)
+    dcond_ref[...] = f32dot(w_cond_ref[...], d_zero).astype(bf)
+    d_one = d_one_ref[ch : 2 * ch, 128 : (rows + 1) * 128]
+    sum_one_ref[...] = nt_dot(d_one, around(a_zero_ref, 1, rows))
 
     bands = pack_ref.shape[0]
     share_rows = SUMS // bands
@@ -419,12 +403,10 @@
         store((9 + tap) * ch, sum_one_ref[:, lanes].astype(bf))
     pad = jnp.zeros((ch, 128 - OUT_AT - (FEED - NOISY_AT)), f32)
     store(18 * ch, jnp.concatenate([sum_in, sum_out, pad], axis=1).astype(bf))
-    store(19 * ch, jnp.zeros((ch, 128), bf))
     for band in range(bands):
         pack_ref[band, share_rows:, :] = jnp.zeros((MOST * WIDE, 128), bf)
-    fetch.wait()
-    count, cells, n = matrix_ref.shape
-    blocks = nt_dot(dcond_ref[...], matrix_ref[...].reshape(count * cells, n)).astype(bf)
+    count, cells, n = interp_ref.shape
+    blocks = nt_dot(dcond_ref[...], interp_ref[...].reshape(count * cells, n)).astype(bf)
     for j in range(count):
         place = place_ref[j]
         spot = share_rows + jnp.bitwise_and(place, MOST - 1) * WIDE
@@ -442,7 +424,6 @@
     bf, f32 = jnp.bfloat16, jnp.float32
     tall = (rows + 4) * cols
     inner = (rows + 2) * cols
-    interp = args[-1]
     return pl.pallas_call(
         net_kernel,
         out_shape=(
@@ -450,8 +431,7 @@
             jax.ShapeDtypeStruct((n_band, SUMS // n_band + MOST * WIDE, 128), bf),
         ),
         in_specs=[scalars(), scalars()]
-        + [whole()] * (len(args) - 3)
-        + [pl.BlockSpec(memory_space=pl.ANY)],
+        + [whole()] * (len(args) - 2),
         out_specs=(whole(),) * 2,
         scratch_shapes=[
             pltpu.VMEM((FEED, tall), bf),
@@ -463,15 +443,15 @@
             pltpu.VMEM((ch, 9 * ch), f32),
             pltpu.VMEM((ch, 9 * ch), f32),
             pltpu.VMEM((WIDE, rows * cols), bf),
-            pltpu.VMEM(interp.shape, bf),
-            pltpu.SemaphoreType.DMA(()),
         ],
-        compiler_params=vmem(56),
+        compiler_params=vmem(36),
     )(*args)
 
 
-def merge_kernel(asked_ref, parts_ref, out_ref, total, weights):
-    bands = parts_ref.shape[0]
+def merge_kernel(ch, n_band, me_ref, *refs):
+    asked_refs = refs[:n_band]
+    parts_ref, out_ref, total, weights = refs[n_band:]
+    bands = n_band
     dests = out_ref.shape[0]
     share_rows = weights.shape[0]
     f32 = jnp.float32
@@ -482,32 +462,39 @@
     weights[...] = whole_sum
     each = share_rows // dests
     for dest in range(dests):
-        total[dest, 2 * LOW : 2 * LOW + each, :] = weights[dest * each : (dest + 1) * each, :]
+        total[dest, 2 * ch : 2 * ch + each, :] = weights[dest * each : (dest + 1) * each, :]
     for i in range(bands * MOST):
-        slot = asked_ref[i // MOST, 0, i % MOST]
+        band = me_ref[0] - i // MOST
+        band = jnp.where(band < 0, band + bands, band)
+        slot = asked_refs[i // MOST][0, i % MOST]
         start = share_rows + (i % MOST) * WIDE
-        block = parts_ref[i // MOST, start : start + WIDE, :].astype(f32)[0:LOW]
-
-        @pl.when(slot >= 0)
+        block = parts_ref[band, start : start + WIDE, :].astype(f32)[0:ch]
+        odd = jnp.bitwise_and(slot, 1)
+
+        @pl.when(jnp.logical_and(slot >= 0, odd == 0))
         def _(slot=slot, block=block):
-            spot = pl.ds(pl.multiple_of(jnp.bitwise_and(slot, 1) * LOW, 8), LOW)
-            total[jnp.right_shift(slot, 1), spot, :] += block
+            total[jnp.right_shift(slot, 1), 0:ch, :] += block
+
+        @pl.when(jnp.logical_and(slot >= 0, odd == 1))
+        def _(slot=slot, block=block):
+            total[jnp.right_shift(slot, 1), ch : 2 * ch, :] += block
 
     out_ref[...] = total[...].astype(jnp.bfloat16)
 
 
-def merge(asked, parts, dests):
-    return pl.pallas_call(
-        merge_kernel,
+def merge(me, asked, parts, dests, ch):
+    n_band = len(asked)
+    return pl.pallas_call(
+        functools.partial(merge_kernel, ch, n_band),
         out_shape=jax.ShapeDtypeStruct((dests, HIGH, 128), jnp.bfloat16),
-        in_specs=[scalars(), whole()],
+        in_specs=[scalars()] * (n_band + 1) + [whole()],
         out_specs=whole(),
         scratch_shapes=[
             pltpu.VMEM((dests, HIGH, 128), jnp.float32),
             pltpu.VMEM((SUMS // parts.shape[0], 128), jnp.float32),
         ],
         compiler_params=vmem(12),
-    )(asked, parts)
+    )(me, *asked, parts)
 
 
 def share_kernel(parts_ref, block_ref, out_ref, total):
@@ -517,8 +504,10 @@
     total[...] = value
     ch = block_ref.shape[2]
     for k in range(block_ref.shape[1]):
-        block_ref[0, k] = total[k * LOW : k * LOW + ch, :]
-    chunk = total[2 * LOW : 2 * LOW + CHUNK, :].astype(jnp.bfloat16)
+        block_ref[0, k] = total[k * ch : (k + 1) * ch, :]
+    rest = block_ref.shape[1] * ch
+    chunk = value[rest:].astype(jnp.bfloat16)
+    chunk = jnp.concatenate([chunk, jnp.zeros((CHUNK - chunk.shape[0], 128), jnp.bfloat16)], axis=0)
     out_ref[...] = jnp.broadcast_to(chunk[None], out_ref.shape)
 
 
@@ -582,6 +571,15 @@
     return lax.ppermute(last, axis, up), lax.ppermute(first, axis, down)
 
 
+def ahead(parts, axis, way):
+    count = lax.axis_size(axis)
+    moved = [parts[0]]
+    for k in range(1, count):
+        pairs = [(i, (i + k * way) % count) for i in range(count)]
+        moved.append(lax.ppermute(parts[k], axis, pairs))
+    return moved
+
+
 def per_device(
     noisy, grad_pred, coarse, margin_band, margin_slot, interp, w_in, w_conv1, w_conv2, w_out
 ):
@@ -594,19 +592,20 @@
     n_tile = lax.axis_size("tile")
     local_interp = interp[0, 0]
 
-    place, wanted = plan(margin_band.reshape(-1), margin_slot, n_band)
-    asked = lax.all_to_all(wanted, "band", split_axis=0, concat_axis=0, tiled=True)
-    prepared = prep(noisy, grad_pred, w_in, w_out, w_conv1, w_conv2)
-    asked, prepared = lax.optimization_barrier((asked, prepared))
-    given, weights = prepared[0], tuple(prepared[1:])
-    served = serve(asked, coarse[0])
-    arrived = lax.all_to_all(served, "band", split_axis=0, concat_axis=0, tiled=True)
     tile, band = lax.axis_index("tile"), lax.axis_index("band")
     flags = jnp.stack([tile > 0, tile < n_tile - 1, band > 0, band < n_band - 1])
     flags = flags.astype(jnp.float32)
-    arrived, flags = lax.optimization_barrier((arrived, flags))
-
-    feed, first, last, edge = make_feed(place, arrived, local_interp, given)
+    me = band.reshape(1)
+    place, near, *wanted = plan(me, margin_band.reshape(-1), margin_slot, n_band)
+    asked = ahead(wanted, "band", 1)
+    prepared = prep(noisy, grad_pred, w_in, w_out, w_conv1, w_conv2)
+    asked, prepared, flags, late = lax.optimization_barrier(
+        (asked, prepared, flags, local_interp)
+    )
+    stashed = pltpu.with_memory_space_constraint(stash(late), pltpu.VMEM)
+    given, weights = prepared[0], tuple(prepared[1:])
+    arrived = ahead(serve(asked, coarse[0]), "band", -1)
+    feed, first, last, edge = make_feed(near, arrived, stashed, given)
     top, bot = halo(first, last, "tile")
     left_out, right_out, own = strips(top, bot, edge)
     left, right = halo(left_out, right_out, "band")
@@ -615,11 +614,11 @@
         rows,
         cols,
         n_band,
-        (place, flags, feed, top, bot, left, right, own) + weights + (local_interp,),
+        (place, flags, feed, top, bot, left, right, own) + weights + (stashed,),
     )
     pack = lax.all_to_all(pack, "band", split_axis=0, concat_axis=0, tiled=True)
     parts = lax.all_to_all(
-        merge(asked, pack, n_tile), "tile", split_axis=0, concat_axis=0, tiled=True
+        merge(me, asked, pack, n_tile, coarse_ch), "tile", split_axis=0, concat_axis=0, tiled=True
     )
     coarse_grad, sums = share(
         parts, (1, per_band // n_tile) + coarse.shape[2:], n_tile * n_band

time: 135 us -> 123 us (0.911)
  waiting for transfers between devices: 27.3 us -> 23.1 us
  Pallas kernels: 35.8 us -> 32.8 us
  local copies, waits for them, and re-layouts: 4.78 us -> 2.86 us
    all_to_all x2 -> x0, starting transfers between devices: 9.93 us -> none  [the longest x1 5.87 us: per_device(): lax.all_to_all(wanted, 'band', split_axis=0, concat_axis=0, tiled=True)]
    ppermute x0 -> x6, starting transfers between devices: none -> 9.15 us  [ahead(): moved.append(lax.ppermute(parts[k], axis, pairs))]
    all_to_all x2 -> x0, waiting for transfers between devices: 4.53 us -> none  [the longest x1 4.35 us: per_device(): lax.all_to_all(served, 'band', split_axis=0, concat_axis=0, tiled=True)]
    all_to_all x1, blocking collectives: 23.8 us -> 21.8 us  [per_device(): lax.all_to_all(merge(me, asked, pack, n_tile, coarse_ch), 'tile', split_a...]
    unnamed x16 -> x28, local copies, waits for them, and re-layouts: 4.78 us -> 2.86 us
    pallas_call x1, Pallas kernels: 19.9 us -> 18.3 us  [net(): pl.pallas_call(net_kernel, out_shape=(jax.ShapeDtypeStruct((chans, rows,...]
    pallas_call x3 -> x4, Pallas kernels: 9.64 us -> 8.14 us  [the longest x1 3.45 us: stash(): pl.pallas_call(stash_kernel, out_shape=pltpu.VMEM(array.shape, array.dtyp...]
  transfers between devices with their start and end apart: 7 -> 11, of which waited for: 5 -> 4; matrix products, arithmetic and copies ran while one was open for 2% -> 2% of each run, Pallas kernels for 2% -> 5%
where the time goes in v4:
time: 123 us
  blocking collectives  39 us (32%)
  Pallas kernels  32.8 us (27%)
  starting transfers between devices  24.1 us (20%)
  waiting for transfers between devices  23.1 us (19%)
  local copies, waits for them, and re-layouts  2.86 us (2%)
    all_to_all x1, blocking collectives, per_device(): lax.all_to_all(merge(me, asked, pack, n_tile, coarse_ch), 'tile', split_a...  21.8 us
    pallas_call x1, Pallas kernels, net(): pl.pallas_call(net_kernel, out_shape=(jax.ShapeDtypeStruct((chans, rows,...  18.3 us
    all_to_all x1, blocking collectives, per_device(): pack = lax.all_to_all(pack, 'band', split_axis=0, concat_axis=0, tiled=True)  17.2 us
    all_to_all x1, waiting for transfers between devices, per_device(): sums = lax.all_to_all(sums, ALL, split_axis=0, concat_axis=0, tiled=True)  16.2 us
    ppermute x4, starting transfers between devices, halo(): return (lax.ppermute(last, axis, up), lax.ppermute(first, axis, down))  10.9 us
    ppermute x6, starting transfers between devices, ahead(): moved.append(lax.ppermute(parts[k], axis, pairs))  9.15 us
    ppermute x4, waiting for transfers between devices, halo(): return (lax.ppermute(last, axis, up), lax.ppermute(first, axis, down))  6.42 us
    all_to_all x1, starting transfers between devices, per_device(): sums = lax.all_to_all(sums, ALL, split_axis=0, concat_axis=0, tiled=True)  3.98 us
  transfers between devices with their start and end apart: 11, of which 4 were waited for; matrix products, arithmetic and copies ran while one was open for 2% of the time, Pallas kernels for 5%

profile of v4, /device:TPU:1, one launch (start us, length us, event | category | flops | bytes accessed | tf_op | source)
XLA Modules:
  0.0 122.8 jit_solution(4906515746310000198)
XLA Ops:
  0.6 1.4 %shard_map.154 = (s32[8]{0:T(128)}, s32[8]{0:T(128)}, s32[8,128]{1,0:T(8,128)}, s32[8,128]{1,0:T(8,128)}, s32[8,128]{1,0:T(8,128)}, /*index=5*/s32[8,128]{1,0:T(8,128)}) custom-call(s32[1]{0:T(128)} %bitcast.me_ref, s32[8]{0:T(128)} %bitcast.16, s32[8]{0:T(128)} %slot_ref.1), custom_call_target="tpu_custom_call" | custom-call | tf_op jit(solution)/shard_map/pallas_call | solution.py:64
  2.0 2.5 %collective-permute-start = (s32[8,128]{1,0:T(8,128)}, s32[8,128]{1,0:T(8,128)S(1)}, u32[]{:S(2)}, u32[]{:S(2)}) collective-permute-start(s32[8,128]{1,0:T(8,128)} %get-tuple-element.55), channel_id=1, source_target_pairs={{0,1},{1,2},{2,3},{3,0},{4,5},{5,6},{6,7},{7,4},{8,9},{9,10},{10,1... | collective-permute-start | bytes 12296 | tf_op jit(solution)/shard_map/ppermute | solution.py:579
  4.6 3.3 %collective-permute-start.1 = (s32[8,128]{1,0:T(8,128)}, s32[8,128]{1,0:T(8,128)S(1)}, u32[]{:S(2)}, u32[]{:S(2)}) collective-permute-start(s32[8,128]{1,0:T(8,128)} %get-tuple-element.56), channel_id=1, source_target_pairs={{0,2},{1,3},{2,0},{3,1},{4,6},{5,7},{6,4},{7,5},{8,10},{9,11},{10,... | collective-permute-start | bytes 12296 | tf_op jit(solution)/shard_map/ppermute | solution.py:579
  7.9 0.7 collective-permute-start.2
  8.6 0.1 add_convert_fusion.flag_ref
  8.7 1.5 %copy.20 = bf16[1,64,38,128]{3,2,1,0:T(8,128)(2,1)S(1)} copy(bf16[1,64,38,128]{3,1,2,0:T(8,128)(2,1)} %param.13) | data formatting | bytes 1245184 | tf_op args[2]
  10.2 2.6 %shard_map.155 = (bf16[32,4096]{1,0:T(8,128)(2,1)}, bf16[256,80]{1,0:T(8,128)(2,1)}, bf16[128,1152]{1,0:T(8,128)(2,1)}, bf16[128,1152]{1,0:T(8,128)(2,1)}, bf16[...) custom-call(bf16[12,32,128]{2,1,0:T(8,128)(2,1)} %noisy_ref.1, ...), custom_call_target="tpu_custom_call" | custom-call | tf_op jit(solution)/shard_map/pallas_call | solution.py:126
  12.7 0.0 collective-permute-done.refs_1_
  12.7 0.0 collective-permute-done.1.refs_2_
  12.7 0.0 collective-permute-done.2.refs_3_
  12.7 0.0 copy-start.7
  12.7 0.7 copy-done.7
  13.4 0.8 shard_map.156
  14.3 0.1 collective-permute-start.3
  14.3 2.5 %collective-permute-start.4 = (bf16[4,38,128]{2,1,0:T(8,128)(2,1)S(1)}, bf16[4,38,128]{2,1,0:T(8,128)(2,1)S(1)}, u32[]{:S(2)}, u32[]{:S(2)}) collective-permute-start(bf16[4,38,128]{2,1,0:T(8,128)(2,1)S(1)} %get-tuple-element.74), channel_id=1, source_target_pairs={{0,2},{1,3},{2,0},{3,1},{4,6},{5,7},{6,4},{7,5},{8,10},{9,11},{10,... | collective-permute-start | bytes 116744 | tf_op jit(solution)/shard_map/ppermute | solution.py:579
  16.9 0.0 collective-permute-start.5
  16.9 3.5 %shard_map.157.refs_4_.interp_ref = bf16[8,128,4096]{2,1,0:T(8,128)(2,1)S(1)} custom-call(bf16[8,128,4096]{2,1,0:T(8,128)(2,1)} %bitcast.13), custom_call_target="tpu_custom_call" | custom-call | tf_op jit(solution)/shard_map/pallas_call | solution.py:199
  20.3 0.0 copy-start.9
  20.3 0.0 copy-start.10
  20.4 0.0 copy-start.11
  20.4 0.0 collective-permute-done.3.refs_1_
  20.4 0.0 collective-permute-done.4.refs_2_
  20.4 0.5 collective-permute-done.5.refs_3_
  20.9 0.0 copy-done
  20.9 0.0 copy-done.5
  20.9 0.0 copy-done.12
  20.9 2.5 %shard_map.158 = (bf16[80,4096]{1,0:T(8,128)(2,1)S(1)}, bf16[80,256]{1,0:T(8,128)(2,1)S(1)}, bf16[80,256]{1,0:T(8,128)(2,1)S(1)}, bf16[80,256]{1,0:T(8,128)(2,1)S(1)}) custom-call(s32[8]{0:T(128)S(1)} %copy-done.12, bf16[4,38,128]{2,1,0:T(8,128)(2,1)S(1)} %get-tuple-element.72.refs_0_, bf16[4,38,128]{2,1,0:T(8,128)(2,1)S(1)} %collective-permute-done.3.refs_1_, ...), custom_call_target="tpu_custom_call" | custom-call | tf_op jit(solution)/shard_map/pallas_call | solution.py:222
  23.4 0.0 copy-start.8
  23.5 6.2 %collective-permute-start.6 = (bf16[80,256]{1,0:T(8,128)(2,1)S(1)}, bf16[80,256]{1,0:T(8,128)(2,1)S(1)}, u32[]{:S(2)}, u32[]{:S(2)}) collective-permute-start(bf16[80,256]{1,0:T(8,128)(2,1)S(1)} %get-tuple-element.79), channel_id=1, source_target_pairs={{0,4},{4,8},{8,12},{12,16},{16,20},{20,24},{24,28},{28,32},{32,36}... | collective-permute-start | bytes 122888 | tf_op jit(solution)/shard_map/ppermute | solution.py:571
  29.7 1.9 %collective-permute-start.7 = (bf16[80,256]{1,0:T(8,128)(2,1)S(1)}, bf16[80,256]{1,0:T(8,128)(2,1)S(1)}, u32[]{:S(2)}, u32[]{:S(2)}) collective-permute-start(bf16[80,256]{1,0:T(8,128)(2,1)S(1)} %get-tuple-element.80), channel_id=1, source_target_pairs={{4,0},{8,4},{12,8},{16,12},{20,16},{24,20},{28,24},{32,28},{36,32}... | collective-permute-start | bytes 122888 | tf_op jit(solution)/shard_map/ppermute | solution.py:571
  31.6 0.0 collective-permute-done.6.top_ref
  31.6 3.4 %collective-permute-done.7.bot_ref = bf16[80,256]{1,0:T(8,128)(2,1)S(1)} collective-permute-done((bf16[80,256]{1,0:T(8,128)(2,1)S(1)}, bf16[80,256]{1,0:T(8,128)(2,1)S(1)}, u32[]{:S(2)}, u32[]{:S(2)}) %collective-permute-start.7) | collective-permute-done | bytes 40992 | tf_op jit(solution)/shard_map/ppermute | solution.py:571
  35.0 0.2 shard_map.159
  35.2 1.3 %collective-permute-start.8 = (bf16[80,128]{1,0:T(8,128)(2,1)S(1)}, bf16[80,128]{1,0:T(8,128)(2,1)S(1)}, u32[]{:S(2)}, u32[]{:S(2)}) collective-permute-start(bf16[80,128]{1,0:T(8,128)(2,1)S(1)} %get-tuple-element.82), channel_id=1, source_target_pairs={{0,1},{1,2},{2,3},{4,5},{5,6},{6,7},{8,9},{9,10},{10,11},{12,13},{... | collective-permute-start | bytes 61448 | tf_op jit(solution)/shard_map/ppermute | solution.py:571
  36.5 1.5 %collective-permute-start.9 = (bf16[80,128]{1,0:T(8,128)(2,1)S(1)}, bf16[80,128]{1,0:T(8,128)(2,1)S(1)}, u32[]{:S(2)}, u32[]{:S(2)}) collective-permute-start(bf16[80,128]{1,0:T(8,128)(2,1)S(1)} %get-tuple-element.83), channel_id=1, source_target_pairs={{1,0},{2,1},{3,2},{5,4},{6,5},{7,6},{9,8},{10,9},{11,10},{13,12},{... | collective-permute-start | bytes 61448 | tf_op jit(solution)/shard_map/ppermute | solution.py:571
  38.0 0.0 collective-permute-done.8.left_ref
  38.0 3.0 %collective-permute-done.9.right_ref = bf16[80,128]{1,0:T(8,128)(2,1)S(1)} collective-permute-done((bf16[80,128]{1,0:T(8,128)(2,1)S(1)}, bf16[80,128]{1,0:T(8,128)(2,1)S(1)}, u32[]{:S(2)}, u32[]{:S(2)}) %collective-permute-start.9) | collective-permute-done | bytes 20512 | tf_op jit(solution)/shard_map/ppermute | solution.py:571
  41.0 0.0 copy-done.1
  41.0 0.0 copy-done.2
  41.1 18.3 %shard_map.160 = (f32[12,32,128]{2,1,0:T(8,128)}, bf16[4,800,128]{2,1,0:T(8,128)(2,1)S(1)}) custom-call(s32[8]{0:T(128)S(1)} %copy-done.11, f32[4]{0:T(128)S(1)} %add_convert_fusion.flag_ref, bf16[80,4096]{1,0:T(8,128)(2,1)S(1)} %get-tuple-element.78.feed_ref, bf16[80,256]{1,0:T(8,128)(2,1)S(1)} %collective-permute-done.6.top_ref, ...), custom_call_target="tpu_custom_call" | custom-call | tf_op jit(solution)/shard_map/pallas_call | solution.py:427
  59.4 17.2 %all_to_all.15.refs_4_ = bf16[4,800,128]{2,1,0:T(8,128)(2,1)S(1)} all-to-all(bf16[4,800,128]{2,1,0:T(8,128)(2,1)S(1)} %get-tuple-element.93), channel_id=1, replica_groups=mesh['tile'=32,'band'=4] {'band'}, dimensions={0} | all-to-all | bytes 1638400 | tf_op jit(solution)/shard_map/all_to_all | solution.py:619
  76.6 1.4 %shard_map.161 = bf16[32,96,128]{2,1,0:T(8,128)(2,1)S(1)} custom-call(s32[1]{0:T(128)} %bitcast.me_ref, s32[8,128]{1,0:T(8,128)S(1)} %copy-done.8, s32[8,128]{1,0:T(8,128)S(1)} %collective-permute-done.refs_1_, s32[8,128]{1,0:T(8,128)S(1)} %collective-permute-done.1.refs_2_, s32[8,128]{1,0:T(8,128)S(1)} %collective-permute-done.2.refs_3_, ...), custom_call_target="tpu_custom_call" | custom-call | tf_op jit(solution)/shard_map/pallas_call | solution.py:487
  78.0 21.8 %all_to_all.16.parts_ref = bf16[32,96,128]{2,1,0:T(8,128)(2,1)S(1)} all-to-all(bf16[32,96,128]{2,1,0:T(8,128)(2,1)S(1)} %shard_map.161), channel_id=1, replica_groups=mesh['tile'=32,'band'=4] {'tile'}, dimensions={0} | all-to-all | bytes 1572864 | tf_op jit(solution)/shard_map/all_to_all | solution.py:620
  99.7 1.1 shard_map.162
  100.8 4.0 %all-to-all-start.2 = ((bf16[128,24,128]{2,1,0:T(8,128)(2,1)}), bf16[128,24,128]{2,1,0:T(8,128)(2,1)S(1)}, u32[]{:S(2)}, u32[]{:S(2)}) async-start(bf16[128,24,128]{2,1,0:T(8,128)(2,1)} %get-tuple-element.95), calls=%async_computation.2 | async-start | bytes 1572864 | tf_op jit(solution)/shard_map/all_to_all | solution.py:626
  104.8 0.6 copy.18
  105.5 16.2 %all-to-all-done.2.parts_ref = bf16[128,24,128]{2,1,0:T(8,128)(2,1)S(1)} async-done(((bf16[128,24,128]{2,1,0:T(8,128)(2,1)}), bf16[128,24,128]{2,1,0:T(8,128)(2,1)S(1)}, u32[]{:S(2)}, u32[]{:S(2)}) %all-to-all-start.2) | async-done | bytes 786464 | tf_op jit(solution)/shard_map/all_to_all | solution.py:626
  121.6 1.1 shard_map.163
  (15 shorter events, 0.0 us)
Async XLA Ops:
  2.0 10.7 %collective-permute-start = (s32[8,128]{1,0:T(8,128)}, s32[8,128]{1,0:T(8,128)S(1)}, u32[]{:S(2)}, u32[]{:S(2)}) collective-permute-start(s32[8,128]{1,0:T(8,128)} %get-tuple-element.55), channel_id=1, source_target_pairs={{0,1},{1,2},{2,3},{3,0},{4,5},{5,6},{6,7},{7,4},{8,9},{9,10},{10,1... | collective-permute-start | bytes 12296 | tf_op jit(solution)/shard_map/ppermute | solution.py:579
  4.6 8.2 %collective-permute-start.1 = (s32[8,128]{1,0:T(8,128)}, s32[8,128]{1,0:T(8,128)S(1)}, u32[]{:S(2)}, u32[]{:S(2)}) collective-permute-start(s32[8,128]{1,0:T(8,128)} %get-tuple-element.56), channel_id=1, source_target_pairs={{0,2},{1,3},{2,0},{3,1},{4,6},{5,7},{6,4},{7,5},{8,10},{9,11},{10,... | collective-permute-start | bytes 12296 | tf_op jit(solution)/shard_map/ppermute | solution.py:579
  7.9 4.9 %collective-permute-start.2 = (s32[8,128]{1,0:T(8,128)}, s32[8,128]{1,0:T(8,128)S(1)}, u32[]{:S(2)}, u32[]{:S(2)}) collective-permute-start(s32[8,128]{1,0:T(8,128)} %get-tuple-element.57), channel_id=1, source_target_pairs={{0,3},{1,0},{2,1},{3,2},{4,7},{5,4},{6,5},{7,6},{8,11},{9,8},{10,9... | collective-permute-start | bytes 12296 | tf_op jit(solution)/shard_map/ppermute | solution.py:579
  12.7 0.7 copy-start.7
  14.3 6.1 %collective-permute-start.3 = (bf16[4,38,128]{2,1,0:T(8,128)(2,1)S(1)}, bf16[4,38,128]{2,1,0:T(8,128)(2,1)S(1)}, u32[]{:S(2)}, u32[]{:S(2)}) collective-permute-start(bf16[4,38,128]{2,1,0:T(8,128)(2,1)S(1)} %get-tuple-element.73), channel_id=1, source_target_pairs={{0,3},{1,0},{2,1},{3,2},{4,7},{5,4},{6,5},{7,6},{8,11},{9,8},{10,9... | collective-permute-start | bytes 116744 | tf_op jit(solution)/shard_map/ppermute | solution.py:579
  14.3 6.0 %collective-permute-start.4 = (bf16[4,38,128]{2,1,0:T(8,128)(2,1)S(1)}, bf16[4,38,128]{2,1,0:T(8,128)(2,1)S(1)}, u32[]{:S(2)}, u32[]{:S(2)}) collective-permute-start(bf16[4,38,128]{2,1,0:T(8,128)(2,1)S(1)} %get-tuple-element.74), channel_id=1, source_target_pairs={{0,2},{1,3},{2,0},{3,1},{4,6},{5,7},{6,4},{7,5},{8,10},{9,11},{10,... | collective-permute-start | bytes 116744 | tf_op jit(solution)/shard_map/ppermute | solution.py:579
  16.8 4.1 %copy-start = (bf16[1024,256]{1,0:T(8,128)(2,1)S(1)}, bf16[1024,256]{1,0:T(8,128)(2,1)}, u32[]{:S(2)}) copy-start(bf16[1024,256]{1,0:T(8,128)(2,1)} %constant.17.clone.refs_6_) | copy-start | bytes 1572868
  16.8 4.1 %copy-start.5 = (bf16[32,4096]{1,0:T(8,128)(2,1)S(1)}, bf16[32,4096]{1,0:T(8,128)(2,1)}, u32[]{:S(2)}) copy-start(bf16[32,4096]{1,0:T(8,128)(2,1)} %get-tuple-element.77.refs_5_) | copy-start | bytes 786436
  16.9 4.1 %copy-start.12 = (s32[8]{0:T(128)S(1)}, s32[8]{0:T(128)}, u32[]{:S(2)}) copy-start(s32[8]{0:T(128)} %get-tuple-element.67.near_ref) | copy-start | bytes 100
  16.9 4.1 %collective-permute-start.5 = (bf16[4,38,128]{2,1,0:T(8,128)(2,1)S(1)}, bf16[4,38,128]{2,1,0:T(8,128)(2,1)S(1)}, u32[]{:S(2)}, u32[]{:S(2)}) collective-permute-start(bf16[4,38,128]{2,1,0:T(8,128)(2,1)S(1)} %get-tuple-element.75), channel_id=1, source_target_pairs={{0,1},{1,2},{2,3},{3,0},{4,5},{5,6},{6,7},{7,4},{8,9},{9,10},{10,1... | collective-permute-start | bytes 116744 | tf_op jit(solution)/shard_map/ppermute | solution.py:579
  20.3 20.7 %copy-start.1 = (bf16[128,1152]{1,0:T(8,128)(2,1)S(1)}, bf16[128,1152]{1,0:T(8,128)(2,1)}, u32[]{:S(2)}) copy-start(bf16[128,1152]{1,0:T(8,128)(2,1)} %get-tuple-element.86.w_one_ref) | copy-start | bytes 884740
  20.3 20.7 %copy-start.2 = (bf16[128,1152]{1,0:T(8,128)(2,1)S(1)}, bf16[128,1152]{1,0:T(8,128)(2,1)}, u32[]{:S(2)}) copy-start(bf16[128,1152]{1,0:T(8,128)(2,1)} %get-tuple-element.87.w_one_back_ref) | copy-start | bytes 884740
  20.3 20.7 %copy-start.3 = (bf16[128,1152]{1,0:T(8,128)(2,1)S(1)}, bf16[128,1152]{1,0:T(8,128)(2,1)}, u32[]{:S(2)}) copy-start(bf16[128,1152]{1,0:T(8,128)(2,1)} %get-tuple-element.88.w_two_ref) | copy-start | bytes 884740
  20.3 20.7 %copy-start.4 = (bf16[128,1152]{1,0:T(8,128)(2,1)S(1)}, bf16[128,1152]{1,0:T(8,128)(2,1)}, u32[]{:S(2)}) copy-start(bf16[128,1152]{1,0:T(8,128)(2,1)} %get-tuple-element.89.w_two_back_ref) | copy-start | bytes 884740
  20.3 20.7 %copy-start.6 = (bf16[256,80]{1,0:T(8,128)(2,1)S(1)}, bf16[256,80]{1,0:T(8,128)(2,1)}, u32[]{:S(2)}) copy-start(bf16[256,80]{1,0:T(8,128)(2,1)} %get-tuple-element.85.w_first_ref) | copy-start | bytes 122884
  20.3 20.7 %copy-start.9 = (bf16[48,128]{1,0:T(8,128)(2,1)S(1)}, bf16[48,128]{1,0:T(8,128)(2,1)}, u32[]{:S(2)}) copy-start(bf16[48,128]{1,0:T(8,128)(2,1)} %get-tuple-element.91.w_cond_ref) | copy-start | bytes 36868
  20.3 20.7 %copy-start.10 = (bf16[16,128]{1,0:T(8,128)(2,1)S(1)}, bf16[16,128]{1,0:T(8,128)(2,1)}, u32[]{:S(2)}) copy-start(bf16[16,128]{1,0:T(8,128)(2,1)} %get-tuple-element.90.w_out_ref) | copy-start | bytes 12292
  20.4 20.7 %copy-start.11 = (s32[8]{0:T(128)S(1)}, s32[8]{0:T(128)}, u32[]{:S(2)}) copy-start(s32[8]{0:T(128)} %get-tuple-element.53.place_ref) | copy-start | bytes 100
  23.4 53.1 %copy-start.8 = (s32[8,128]{1,0:T(8,128)S(1)}, s32[8,128]{1,0:T(8,128)}, u32[]{:S(2)}) copy-start(s32[8,128]{1,0:T(8,128)} %get-tuple-element.68.refs_0_) | copy-start | bytes 12292
  23.5 8.2 %collective-permute-start.6 = (bf16[80,256]{1,0:T(8,128)(2,1)S(1)}, bf16[80,256]{1,0:T(8,128)(2,1)S(1)}, u32[]{:S(2)}, u32[]{:S(2)}) collective-permute-start(bf16[80,256]{1,0:T(8,128)(2,1)S(1)} %get-tuple-element.79), channel_id=1, source_target_pairs={{0,4},{4,8},{8,12},{12,16},{16,20},{20,24},{24,28},{28,32},{32,36}... | collective-permute-start | bytes 122888 | tf_op jit(solution)/shard_map/ppermute | solution.py:571
  29.7 5.3 %collective-permute-start.7 = (bf16[80,256]{1,0:T(8,128)(2,1)S(1)}, bf16[80,256]{1,0:T(8,128)(2,1)S(1)}, u32[]{:S(2)}, u32[]{:S(2)}) collective-permute-start(bf16[80,256]{1,0:T(8,128)(2,1)S(1)} %get-tuple-element.80), channel_id=1, source_target_pairs={{4,0},{8,4},{12,8},{16,12},{20,16},{24,20},{28,24},{32,28},{36,32}... | collective-permute-start | bytes 122888 | tf_op jit(solution)/shard_map/ppermute | solution.py:571
  35.2 2.8 %collective-permute-start.8 = (bf16[80,128]{1,0:T(8,128)(2,1)S(1)}, bf16[80,128]{1,0:T(8,128)(2,1)S(1)}, u32[]{:S(2)}, u32[]{:S(2)}) collective-permute-start(bf16[80,128]{1,0:T(8,128)(2,1)S(1)} %get-tuple-element.82), channel_id=1, source_target_pairs={{0,1},{1,2},{2,3},{4,5},{5,6},{6,7},{8,9},{9,10},{10,11},{12,13},{... | collective-permute-start | bytes 61448 | tf_op jit(solution)/shard_map/ppermute | solution.py:571
  36.5 4.5 %collective-permute-start.9 = (bf16[80,128]{1,0:T(8,128)(2,1)S(1)}, bf16[80,128]{1,0:T(8,128)(2,1)S(1)}, u32[]{:S(2)}, u32[]{:S(2)}) collective-permute-start(bf16[80,128]{1,0:T(8,128)(2,1)S(1)} %get-tuple-element.83), channel_id=1, source_target_pairs={{1,0},{2,1},{3,2},{5,4},{6,5},{7,6},{9,8},{10,9},{11,10},{13,12},{... | collective-permute-start | bytes 61448 | tf_op jit(solution)/shard_map/ppermute | solution.py:571
  100.8 20.8 %all-to-all-start.2 = ((bf16[128,24,128]{2,1,0:T(8,128)(2,1)}), bf16[128,24,128]{2,1,0:T(8,128)(2,1)S(1)}, u32[]{:S(2)}, u32[]{:S(2)}) async-start(bf16[128,24,128]{2,1,0:T(8,128)(2,1)} %get-tuple-element.95), calls=%async_computation.2 | async-start | bytes 1572864 | tf_op jit(solution)/shard_map/all_to_all | solution.py:626

commit v5 on v4

--- a/solution.py
+++ b/solution.py
@@ -70,14 +70,37 @@
     )(me, bands, slots)
 
 
+def given_kernel(noisy_ref, grad_ref, given_ref, noisy_wide, grad_wide):
+    bf, f32 = jnp.bfloat16, jnp.float32
+    chans, rows, _ = noisy_ref.shape
+    noisy_wide[...] = noisy_ref[...].astype(f32)
+    grad_wide[...] = grad_ref[...].astype(f32)
+    pad = jnp.zeros((FEED - NOISY_AT - 2 * chans, 128), f32)
+    for r in range(rows):
+        pieces = [noisy_wide[:, r, :], grad_wide[:, r, :], pad]
+        given_ref[:, r * 128 : (r + 1) * 128] = jnp.concatenate(pieces, axis=0).astype(bf)
+
+
+def make_given(noisy, grad_pred):
+    _, rows, cols = noisy.shape
+    return pl.pallas_call(
+        given_kernel,
+        out_shape=jax.ShapeDtypeStruct((FEED - NOISY_AT, rows * cols), jnp.bfloat16),
+        in_specs=[whole()] * 2,
+        out_specs=whole(),
+        scratch_shapes=[
+            pltpu.VMEM(noisy.shape, jnp.float32),
+            pltpu.VMEM(noisy.shape, jnp.float32),
+        ],
+        compiler_params=vmem(56),
+    )(noisy, grad_pred)
+
+
 def prep_kernel(
-    noisy_ref,
-    grad_ref,
     w_in_ref,
     w_out_ref,
     w_one_ref,
     w_two_ref,
-    given_ref,
     first_ref,
     one_ref,
     one_back_ref,
@@ -86,13 +109,10 @@
     out_ref,
     cond_ref,
     small,
-    noisy_wide,
-    grad_wide,
 ):
     bf, f32 = jnp.bfloat16, jnp.float32
-    chans, rows, _ = noisy_ref.shape
+    chans, ch = w_out_ref.shape
     coarse_ch = w_in_ref.shape[0] - chans
-    ch = w_in_ref.shape[1]
     small[...] = jnp.zeros_like(small)
     w_in = w_in_ref[...].astype(f32)
     w_out = w_out_ref[...].astype(f32)
@@ -110,23 +130,15 @@
             lanes = slice(tap * ch, (tap + 1) * ch)
             straight[:, lanes] = source[tap // 3, tap % 3]
             back[:, lanes] = source[2 - tap // 3, 2 - tap % 3].T
-    noisy_wide[...] = noisy_ref[...].astype(f32)
-    grad_wide[...] = grad_ref[...].astype(f32)
-    pad = jnp.zeros((FEED - NOISY_AT - 2 * chans, 128), f32)
-    for r in range(rows):
-        pieces = [noisy_wide[:, r, :], grad_wide[:, r, :], pad]
-        given_ref[:, r * 128 : (r + 1) * 128] = jnp.concatenate(pieces, axis=0).astype(bf)
-
-
-def prep(noisy, grad_pred, w_in, w_out, w_one, w_two):
+
+
+def prep(w_in, w_out, w_one, w_two):
     bf = jnp.bfloat16
-    chans, rows, cols = noisy.shape
     ch = w_in.shape[0]
     square = jax.ShapeDtypeStruct((ch, 9 * ch), bf)
     return pl.pallas_call(
         prep_kernel,
         out_shape=(
-            jax.ShapeDtypeStruct((FEED - NOISY_AT, rows * cols), bf),
             jax.ShapeDtypeStruct((2 * ch, FEED), bf),
             square,
             square,
@@ -135,15 +147,11 @@
             jax.ShapeDtypeStruct((16, ch), bf),
             jax.ShapeDtypeStruct((WIDE, ch), bf),
         ),
-        in_specs=[whole()] * 6,
-        out_specs=(whole(),) * 8,
-        scratch_shapes=[
-            pltpu.VMEM((128, 2 * ch), jnp.float32),
-            pltpu.VMEM(noisy.shape, jnp.float32),
-            pltpu.VMEM(noisy.shape, jnp.float32),
-        ],
-        compiler_params=vmem(56),
-    )(noisy, grad_pred, w_in.T, w_out, w_one, w_two)
+        in_specs=[whole()] * 4,
+        out_specs=(whole(),) * 7,
+        scratch_shapes=[pltpu.VMEM((128, 2 * ch), jnp.float32)],
+        compiler_params=vmem(8),
+    )(w_in.T, w_out, w_one, w_two)
 
 
 def serve_kernel(n_band, *refs):
@@ -598,16 +606,15 @@
     me = band.reshape(1)
     place, near, *wanted = plan(me, margin_band.reshape(-1), margin_slot, n_band)
     asked = ahead(wanted, "band", 1)
-    prepared = prep(noisy, grad_pred, w_in, w_out, w_conv1, w_conv2)
-    asked, prepared, flags, late = lax.optimization_barrier(
-        (asked, prepared, flags, local_interp)
-    )
+    given = make_given(noisy, grad_pred)
+    asked, given, flags, late = lax.optimization_barrier((asked, given, flags, local_interp))
     stashed = pltpu.with_memory_space_constraint(stash(late), pltpu.VMEM)
-    given, weights = prepared[0], tuple(prepared[1:])
     arrived = ahead(serve(asked, coarse[0]), "band", -1)
     feed, first, last, edge = make_feed(near, arrived, stashed, given)
     top, bot = halo(first, last, "tile")
     left_out, right_out, own = strips(top, bot, edge)
+    left_out, *late = lax.optimization_barrier((left_out, w_in, w_out, w_conv1, w_conv2))
+    weights = tuple(prep(*late))
     left, right = halo(left_out, right_out, "band")
     pred, pack = net(
         chans,

time: 123 us -> 122 us (level)
  starting transfers between devices: 24.1 us -> 26.8 us
  waiting for transfers between devices: 23.1 us -> 20.5 us
    ppermute x4, starting transfers between devices: 10.9 us -> 13.6 us  [halo(): return (lax.ppermute(last, axis, up), lax.ppermute(first, axis, down))]
    ppermute x4, waiting for transfers between devices: 6.42 us -> 3.75 us  [halo(): return (lax.ppermute(last, axis, up), lax.ppermute(first, axis, down))]
    pallas_call x1 -> x2, Pallas kernels: 2.55 us -> 2.2 us  [the longest x1 1.91 us: make_given(): pl.pallas_call(given_kernel, out_shape=jax.ShapeDtypeStruct((FEED - NOISY...]
    unnamed x28 -> x22, local copies, waits for them, and re-layouts: 2.86 us -> 2.84 us
where the time goes in v5:
time: 122 us; the launch traced here: 121 us
  blocking collectives  37.9 us (31%)
  Pallas kernels  32.3 us (26%)
  starting transfers between devices  26.8 us (22%)
  waiting for transfers between devices  20.5 us (17%)
  local copies, waits for them, and re-layouts  2.84 us (2%)
    all_to_all x1, blocking collectives, per_device(): lax.all_to_all(merge(me, asked, pack, n_tile, coarse_ch), 'tile', split_a...  21.9 us
    pallas_call x1, Pallas kernels, net(): pl.pallas_call(net_kernel, out_shape=(jax.ShapeDtypeStruct((chans, rows,...  18.1 us
    all_to_all x1, waiting for transfers between devices, per_device(): sums = lax.all_to_all(sums, ALL, split_axis=0, concat_axis=0, tiled=True)  16.2 us
    all_to_all x1, blocking collectives, per_device(): pack = lax.all_to_all(pack, 'band', split_axis=0, concat_axis=0, tiled=True)  16 us
    ppermute x4, starting transfers between devices, halo(): return (lax.ppermute(last, axis, up), lax.ppermute(first, axis, down))  13.6 us
    ppermute x6, starting transfers between devices, ahead(): moved.append(lax.ppermute(parts[k], axis, pairs))  9.16 us
    all_to_all x1, starting transfers between devices, per_device(): sums = lax.all_to_all(sums, ALL, split_axis=0, concat_axis=0, tiled=True)  3.98 us
    ppermute x4, waiting for transfers between devices, halo(): return (lax.ppermute(last, axis, up), lax.ppermute(first, axis, down))  3.75 us
  transfers between devices with their start and end apart: 11, of which 4 were waited for; matrix products, arithmetic and copies ran while one was open for 2% of the time, Pallas kernels for 5%

profile of v5, /device:TPU:1, one launch (start us, length us, event | category | flops | bytes accessed | tf_op | source)
XLA Modules:
  0.0 121.2 jit_solution(13761649581522063706)
XLA Ops:
  0.6 1.4 %shard_map.154 = (s32[8]{0:T(128)}, s32[8]{0:T(128)}, s32[8,128]{1,0:T(8,128)}, s32[8,128]{1,0:T(8,128)}, s32[8,128]{1,0:T(8,128)}, /*index=5*/s32[8,128]{1,0:T(8,128)}) custom-call(s32[1]{0:T(128)} %bitcast.me_ref, s32[8]{0:T(128)} %bitcast.16, s32[8]{0:T(128)} %slot_ref.1), custom_call_target="tpu_custom_call" | custom-call | tf_op jit(solution)/shard_map/pallas_call | solution.py:64
  2.0 2.5 %collective-permute-start = (s32[8,128]{1,0:T(8,128)}, s32[8,128]{1,0:T(8,128)S(1)}, u32[]{:S(2)}, u32[]{:S(2)}) collective-permute-start(s32[8,128]{1,0:T(8,128)} %get-tuple-element.52), channel_id=1, source_target_pairs={{0,1},{1,2},{2,3},{3,0},{4,5},{5,6},{6,7},{7,4},{8,9},{9,10},{10,1... | collective-permute-start | bytes 12296 | tf_op jit(solution)/shard_map/ppermute | solution.py:587
  4.6 3.3 %collective-permute-start.1 = (s32[8,128]{1,0:T(8,128)}, s32[8,128]{1,0:T(8,128)S(1)}, u32[]{:S(2)}, u32[]{:S(2)}) collective-permute-start(s32[8,128]{1,0:T(8,128)} %get-tuple-element.53), channel_id=1, source_target_pairs={{0,2},{1,3},{2,0},{3,1},{4,6},{5,7},{6,4},{7,5},{8,10},{9,11},{10,... | collective-permute-start | bytes 12296 | tf_op jit(solution)/shard_map/ppermute | solution.py:587
  7.9 0.7 collective-permute-start.2
  8.6 0.1 add_convert_fusion.flag_ref
  8.7 1.5 %copy.20 = bf16[1,64,38,128]{3,2,1,0:T(8,128)(2,1)S(1)} copy(bf16[1,64,38,128]{3,1,2,0:T(8,128)(2,1)} %param.13) | data formatting | bytes 1245184 | tf_op args[2]
  10.2 1.9 %shard_map.155.refs_5_ = bf16[32,4096]{1,0:T(8,128)(2,1)} custom-call(bf16[12,32,128]{2,1,0:T(8,128)(2,1)} %noisy_ref.1, bf16[12,32,128]{2,1,0:T(8,128)(2,1)} %grad_ref.1), custom_call_target="tpu_custom_call" | custom-call | tf_op jit(solution)/shard_map/pallas_call | solution.py:86
  12.1 0.0 collective-permute-done.refs_1_
  12.1 0.0 collective-permute-done.1.refs_2_
  12.1 0.0 collective-permute-done.2.refs_3_
  12.1 0.0 copy-start.4
  12.1 0.7 copy-done.4
  12.8 0.8 shard_map.156
  13.6 0.5 collective-permute-start.3
  14.1 2.1 %collective-permute-start.4 = (bf16[4,38,128]{2,1,0:T(8,128)(2,1)S(1)}, bf16[4,38,128]{2,1,0:T(8,128)(2,1)S(1)}, u32[]{:S(2)}, u32[]{:S(2)}) collective-permute-start(bf16[4,38,128]{2,1,0:T(8,128)(2,1)S(1)} %get-tuple-element.63), channel_id=1, source_target_pairs={{0,2},{1,3},{2,0},{3,1},{4,6},{5,7},{6,4},{7,5},{8,10},{9,11},{10,... | collective-permute-start | bytes 116744 | tf_op jit(solution)/shard_map/ppermute | solution.py:587
  16.2 0.0 collective-permute-start.5
  16.2 3.5 %shard_map.157.refs_4_.interp_ref = bf16[8,128,4096]{2,1,0:T(8,128)(2,1)S(1)} custom-call(bf16[8,128,4096]{2,1,0:T(8,128)(2,1)} %bitcast.14), custom_call_target="tpu_custom_call" | custom-call | tf_op jit(solution)/shard_map/pallas_call | solution.py:207
  19.7 0.0 collective-permute-done.3.refs_1_
  19.7 0.0 collective-permute-done.4.refs_2_
  19.7 0.6 collective-permute-done.5.refs_3_
  20.3 0.0 copy-done
  20.3 0.0 copy-done.1
  20.3 0.0 copy-done.9
  20.3 2.5 %shard_map.158 = (bf16[80,4096]{1,0:T(8,128)(2,1)S(1)}, bf16[80,256]{1,0:T(8,128)(2,1)S(1)}, bf16[80,256]{1,0:T(8,128)(2,1)S(1)}, bf16[80,256]{1,0:T(8,128)(2,1)S(1)}) custom-call(s32[8]{0:T(128)S(1)} %copy-done.9, bf16[4,38,128]{2,1,0:T(8,128)(2,1)S(1)} %get-tuple-element.61.refs_0_, bf16[4,38,128]{2,1,0:T(8,128)(2,1)S(1)} %collective-permute-done.3.refs_1_, ...), custom_call_target="tpu_custom_call" | custom-call | tf_op jit(solution)/shard_map/pallas_call | solution.py:230
  22.8 0.0 copy-start.5
  22.8 6.2 %collective-permute-start.6 = (bf16[80,256]{1,0:T(8,128)(2,1)S(1)}, bf16[80,256]{1,0:T(8,128)(2,1)S(1)}, u32[]{:S(2)}, u32[]{:S(2)}) collective-permute-start(bf16[80,256]{1,0:T(8,128)(2,1)S(1)} %get-tuple-element.68), channel_id=1, source_target_pairs={{0,4},{4,8},{8,12},{12,16},{16,20},{20,24},{24,28},{28,32},{32,36}... | collective-permute-start | bytes 122888 | tf_op jit(solution)/shard_map/ppermute | solution.py:579
  29.0 1.9 %collective-permute-start.7 = (bf16[80,256]{1,0:T(8,128)(2,1)S(1)}, bf16[80,256]{1,0:T(8,128)(2,1)S(1)}, u32[]{:S(2)}, u32[]{:S(2)}) collective-permute-start(bf16[80,256]{1,0:T(8,128)(2,1)S(1)} %get-tuple-element.69), channel_id=1, source_target_pairs={{4,0},{8,4},{12,8},{16,12},{20,16},{24,20},{28,24},{32,28},{36,32}... | collective-permute-start | bytes 122888 | tf_op jit(solution)/shard_map/ppermute | solution.py:579
  31.0 0.0 collective-permute-done.6.top_ref
  31.0 3.4 %collective-permute-done.7.bot_ref = bf16[80,256]{1,0:T(8,128)(2,1)S(1)} collective-permute-done((bf16[80,256]{1,0:T(8,128)(2,1)S(1)}, bf16[80,256]{1,0:T(8,128)(2,1)S(1)}, u32[]{:S(2)}, u32[]{:S(2)}) %collective-permute-start.7) | collective-permute-done | bytes 40992 | tf_op jit(solution)/shard_map/ppermute | solution.py:579
  34.3 0.2 shard_map.159
  34.5 1.3 %collective-permute-start.9 = (bf16[80,128]{1,0:T(8,128)(2,1)S(1)}, bf16[80,128]{1,0:T(8,128)(2,1)S(1)}, u32[]{:S(2)}, u32[]{:S(2)}) collective-permute-start(bf16[80,128]{1,0:T(8,128)(2,1)S(1)} %get-tuple-element.73), channel_id=1, source_target_pairs={{1,0},{2,1},{3,2},{5,4},{6,5},{7,6},{9,8},{10,9},{11,10},{13,12},{... | collective-permute-start | bytes 61448 | tf_op jit(solution)/shard_map/ppermute | solution.py:579
  35.8 4.2 %collective-permute-start.8 = (bf16[80,128]{1,0:T(8,128)(2,1)S(1)}, bf16[80,128]{1,0:T(8,128)(2,1)S(1)}, u32[]{:S(2)}, u32[]{:S(2)}) collective-permute-start(bf16[80,128]{1,0:T(8,128)(2,1)S(1)} %get-tuple-element.71), channel_id=1, source_target_pairs={{0,1},{1,2},{2,3},{4,5},{5,6},{6,7},{8,9},{9,10},{10,11},{12,13},{... | collective-permute-start | bytes 61448 | tf_op jit(solution)/shard_map/ppermute | solution.py:579
  40.0 0.0 copy-done.2
  40.0 0.0 copy-done.3
  40.0 0.0 copy-done.6
  40.1 0.3 shard_map.160
  40.4 0.0 collective-permute-done.9.right_ref
  40.4 0.4 collective-permute-done.8.left_ref
  40.7 0.0 copy-done.8
  40.7 18.1 %shard_map.161 = (f32[12,32,128]{2,1,0:T(8,128)}, bf16[4,800,128]{2,1,0:T(8,128)(2,1)S(1)}) custom-call(s32[8]{0:T(128)S(1)} %copy-done.8, f32[4]{0:T(128)S(1)} %add_convert_fusion.flag_ref, bf16[80,4096]{1,0:T(8,128)(2,1)S(1)} %get-tuple-element.67.feed_ref, bf16[80,256]{1,0:T(8,128)(2,1)S(1)} %collective-permute-done.6.top_ref, ...), custom_call_target="tpu_custom_call" | custom-call | tf_op jit(solution)/shard_map/pallas_call | solution.py:435
  58.9 16.0 %all_to_all.15.refs_4_ = bf16[4,800,128]{2,1,0:T(8,128)(2,1)S(1)} all-to-all(bf16[4,800,128]{2,1,0:T(8,128)(2,1)S(1)} %get-tuple-element.87), channel_id=1, replica_groups=mesh['tile'=32,'band'=4] {'band'}, dimensions={0} | all-to-all | bytes 1638400 | tf_op jit(solution)/shard_map/all_to_all | solution.py:626
  74.9 1.4 %shard_map.162 = bf16[32,96,128]{2,1,0:T(8,128)(2,1)S(1)} custom-call(s32[1]{0:T(128)} %bitcast.me_ref, s32[8,128]{1,0:T(8,128)S(1)} %copy-done.5, s32[8,128]{1,0:T(8,128)S(1)} %collective-permute-done.refs_1_, s32[8,128]{1,0:T(8,128)S(1)} %collective-permute-done.1.refs_2_, s32[8,128]{1,0:T(8,128)S(1)} %collective-permute-done.2.refs_3_, ...), custom_call_target="tpu_custom_call" | custom-call | tf_op jit(solution)/shard_map/pallas_call | solution.py:495
  76.3 21.9 %all_to_all.16.parts_ref = bf16[32,96,128]{2,1,0:T(8,128)(2,1)S(1)} all-to-all(bf16[32,96,128]{2,1,0:T(8,128)(2,1)S(1)} %shard_map.162), channel_id=1, replica_groups=mesh['tile'=32,'band'=4] {'tile'}, dimensions={0} | all-to-all | bytes 1572864 | tf_op jit(solution)/shard_map/all_to_all | solution.py:627
  98.2 1.1 shard_map.163
  99.3 4.0 %all-to-all-start.2 = ((bf16[128,24,128]{2,1,0:T(8,128)(2,1)}), bf16[128,24,128]{2,1,0:T(8,128)(2,1)S(1)}, u32[]{:S(2)}, u32[]{:S(2)}) async-start(bf16[128,24,128]{2,1,0:T(8,128)(2,1)} %get-tuple-element.89), calls=%async_computation.2 | async-start | bytes 1572864 | tf_op jit(solution)/shard_map/all_to_all | solution.py:633
  103.3 0.6 copy.18
  103.9 16.2 %all-to-all-done.2.parts_ref = bf16[128,24,128]{2,1,0:T(8,128)(2,1)S(1)} async-done(((bf16[128,24,128]{2,1,0:T(8,128)(2,1)}), bf16[128,24,128]{2,1,0:T(8,128)(2,1)S(1)}, u32[]{:S(2)}, u32[]{:S(2)}) %all-to-all-start.2) | async-done | bytes 786464 | tf_op jit(solution)/shard_map/all_to_all | solution.py:633
  120.1 1.1 shard_map.164
  (10 shorter events, 0.0 us)
Async XLA Ops:
  2.0 10.0 %collective-permute-start = (s32[8,128]{1,0:T(8,128)}, s32[8,128]{1,0:T(8,128)S(1)}, u32[]{:S(2)}, u32[]{:S(2)}) collective-permute-start(s32[8,128]{1,0:T(8,128)} %get-tuple-element.52), channel_id=1, source_target_pairs={{0,1},{1,2},{2,3},{3,0},{4,5},{5,6},{6,7},{7,4},{8,9},{9,10},{10,1... | collective-permute-start | bytes 12296 | tf_op jit(solution)/shard_map/ppermute | solution.py:587
  4.6 7.5 %collective-permute-start.1 = (s32[8,128]{1,0:T(8,128)}, s32[8,128]{1,0:T(8,128)S(1)}, u32[]{:S(2)}, u32[]{:S(2)}) collective-permute-start(s32[8,128]{1,0:T(8,128)} %get-tuple-element.53), channel_id=1, source_target_pairs={{0,2},{1,3},{2,0},{3,1},{4,6},{5,7},{6,4},{7,5},{8,10},{9,11},{10,... | collective-permute-start | bytes 12296 | tf_op jit(solution)/shard_map/ppermute | solution.py:587
  7.9 4.2 %collective-permute-start.2 = (s32[8,128]{1,0:T(8,128)}, s32[8,128]{1,0:T(8,128)S(1)}, u32[]{:S(2)}, u32[]{:S(2)}) collective-permute-start(s32[8,128]{1,0:T(8,128)} %get-tuple-element.54), channel_id=1, source_target_pairs={{0,3},{1,0},{2,1},{3,2},{4,7},{5,4},{6,5},{7,6},{8,11},{9,8},{10,9... | collective-permute-start | bytes 12296 | tf_op jit(solution)/shard_map/ppermute | solution.py:587
  12.1 0.7 copy-start.4
  13.6 6.1 %collective-permute-start.3 = (bf16[4,38,128]{2,1,0:T(8,128)(2,1)S(1)}, bf16[4,38,128]{2,1,0:T(8,128)(2,1)S(1)}, u32[]{:S(2)}, u32[]{:S(2)}) collective-permute-start(bf16[4,38,128]{2,1,0:T(8,128)(2,1)S(1)} %get-tuple-element.62), channel_id=1, source_target_pairs={{0,3},{1,0},{2,1},{3,2},{4,7},{5,4},{6,5},{7,6},{8,11},{9,8},{10,9... | collective-permute-start | bytes 116744 | tf_op jit(solution)/shard_map/ppermute | solution.py:587
  14.1 5.6 %collective-permute-start.4 = (bf16[4,38,128]{2,1,0:T(8,128)(2,1)S(1)}, bf16[4,38,128]{2,1,0:T(8,128)(2,1)S(1)}, u32[]{:S(2)}, u32[]{:S(2)}) collective-permute-start(bf16[4,38,128]{2,1,0:T(8,128)(2,1)S(1)} %get-tuple-element.63), channel_id=1, source_target_pairs={{0,2},{1,3},{2,0},{3,1},{4,6},{5,7},{6,4},{7,5},{8,10},{9,11},{10,... | collective-permute-start | bytes 116744 | tf_op jit(solution)/shard_map/ppermute | solution.py:587
  16.2 4.1 %copy-start = (bf16[32,4096]{1,0:T(8,128)(2,1)S(1)}, bf16[32,4096]{1,0:T(8,128)(2,1)}, u32[]{:S(2)}) copy-start(bf16[32,4096]{1,0:T(8,128)(2,1)} %shard_map.155.refs_5_) | copy-start | bytes 786436
  16.2 4.1 %copy-start.1 = (bf16[1024,256]{1,0:T(8,128)(2,1)S(1)}, bf16[1024,256]{1,0:T(8,128)(2,1)}, u32[]{:S(2)}) copy-start(bf16[1024,256]{1,0:T(8,128)(2,1)} %constant.17.clone.refs_6_) | copy-start | bytes 1572868
  16.2 4.1 %copy-start.9 = (s32[8]{0:T(128)S(1)}, s32[8]{0:T(128)}, u32[]{:S(2)}) copy-start(s32[8]{0:T(128)} %get-tuple-element.56.near_ref) | copy-start | bytes 100
  16.2 4.1 %collective-permute-start.5 = (bf16[4,38,128]{2,1,0:T(8,128)(2,1)S(1)}, bf16[4,38,128]{2,1,0:T(8,128)(2,1)S(1)}, u32[]{:S(2)}, u32[]{:S(2)}) collective-permute-start(bf16[4,38,128]{2,1,0:T(8,128)(2,1)S(1)} %get-tuple-element.64), channel_id=1, source_target_pairs={{0,1},{1,2},{2,3},{3,0},{4,5},{5,6},{6,7},{7,4},{8,9},{9,10},{10,1... | collective-permute-start | bytes 116744 | tf_op jit(solution)/shard_map/ppermute | solution.py:587
  19.7 20.4 %copy-start.2 = (bf16[3,3,128,128]{3,2,1,0:T(8,128)(2,1)S(1)}, bf16[3,3,128,128]{3,2,1,0:T(8,128)(2,1)}, u32[]{:S(2)}) copy-start(bf16[3,3,128,128]{3,2,1,0:T(8,128)(2,1)} %w_one_ref) | copy-start | bytes 884740
  19.7 20.4 %copy-start.3 = (bf16[3,3,128,128]{3,2,1,0:T(8,128)(2,1)S(1)}, bf16[3,3,128,128]{3,2,1,0:T(8,128)(2,1)}, u32[]{:S(2)}) copy-start(bf16[3,3,128,128]{3,2,1,0:T(8,128)(2,1)} %w_two_ref) | copy-start | bytes 884740
  19.7 20.4 %copy-start.6 = (bf16[128,50]{0,1:T(8,128)(2,1)S(1)}, bf16[128,50]{0,1:T(8,128)(2,1)}, u32[]{:S(2)}) copy-start(bf16[128,50]{0,1:T(8,128)(2,1)} %param.17) | copy-start | bytes 38404
  19.7 20.4 %copy-start.7 = (bf16[12,128]{1,0:T(8,128)(2,1)S(1)}, bf16[12,128]{1,0:T(8,128)(2,1)}, u32[]{:S(2)}) copy-start(bf16[12,128]{1,0:T(8,128)(2,1)} %w_out_ref) | copy-start | bytes 9220
  19.7 21.1 %copy-start.8 = (s32[8]{0:T(128)S(1)}, s32[8]{0:T(128)}, u32[]{:S(2)}) copy-start(s32[8]{0:T(128)} %get-tuple-element.50.place_ref) | copy-start | bytes 100
  22.8 52.1 %copy-start.5 = (s32[8,128]{1,0:T(8,128)S(1)}, s32[8,128]{1,0:T(8,128)}, u32[]{:S(2)}) copy-start(s32[8,128]{1,0:T(8,128)} %get-tuple-element.57.refs_0_) | copy-start | bytes 12292
  22.8 8.2 %collective-permute-start.6 = (bf16[80,256]{1,0:T(8,128)(2,1)S(1)}, bf16[80,256]{1,0:T(8,128)(2,1)S(1)}, u32[]{:S(2)}, u32[]{:S(2)}) collective-permute-start(bf16[80,256]{1,0:T(8,128)(2,1)S(1)} %get-tuple-element.68), channel_id=1, source_target_pairs={{0,4},{4,8},{8,12},{12,16},{16,20},{20,24},{24,28},{28,32},{32,36}... | collective-permute-start | bytes 122888 | tf_op jit(solution)/shard_map/ppermute | solution.py:579
  29.0 5.3 %collective-permute-start.7 = (bf16[80,256]{1,0:T(8,128)(2,1)S(1)}, bf16[80,256]{1,0:T(8,128)(2,1)S(1)}, u32[]{:S(2)}, u32[]{:S(2)}) collective-permute-start(bf16[80,256]{1,0:T(8,128)(2,1)S(1)} %get-tuple-element.69), channel_id=1, source_target_pairs={{4,0},{8,4},{12,8},{16,12},{20,16},{24,20},{28,24},{32,28},{36,32}... | collective-permute-start | bytes 122888 | tf_op jit(solution)/shard_map/ppermute | solution.py:579
  34.5 5.8 %collective-permute-start.9 = (bf16[80,128]{1,0:T(8,128)(2,1)S(1)}, bf16[80,128]{1,0:T(8,128)(2,1)S(1)}, u32[]{:S(2)}, u32[]{:S(2)}) collective-permute-start(bf16[80,128]{1,0:T(8,128)(2,1)S(1)} %get-tuple-element.73), channel_id=1, source_target_pairs={{1,0},{2,1},{3,2},{5,4},{6,5},{7,6},{9,8},{10,9},{11,10},{13,12},{... | collective-permute-start | bytes 61448 | tf_op jit(solution)/shard_map/ppermute | solution.py:579
  35.8 4.9 %collective-permute-start.8 = (bf16[80,128]{1,0:T(8,128)(2,1)S(1)}, bf16[80,128]{1,0:T(8,128)(2,1)S(1)}, u32[]{:S(2)}, u32[]{:S(2)}) collective-permute-start(bf16[80,128]{1,0:T(8,128)(2,1)S(1)} %get-tuple-element.71), channel_id=1, source_target_pairs={{0,1},{1,2},{2,3},{4,5},{5,6},{6,7},{8,9},{9,10},{10,11},{12,13},{... | collective-permute-start | bytes 61448 | tf_op jit(solution)/shard_map/ppermute | solution.py:579
  99.3 20.8 %all-to-all-start.2 = ((bf16[128,24,128]{2,1,0:T(8,128)(2,1)}), bf16[128,24,128]{2,1,0:T(8,128)(2,1)S(1)}, u32[]{:S(2)}, u32[]{:S(2)}) async-start(bf16[128,24,128]{2,1,0:T(8,128)(2,1)} %get-tuple-element.89), calls=%async_computation.2 | async-start | bytes 1572864 | tf_op jit(solution)/shard_map/all_to_all | solution.py:633
